TPU v7x, 512 devices: a whole 4x4x16 slice. The times are simulated.
512 devices in a mesh: dp: 16 (over y, z_hi, core), feat: 32 (over z_lo, x).
Axes of the slice: x: 4, y: 4, z: 16 (z_hi: 2, z_lo: 8; z = z_hi * 8 + z_lo), core: 2. Of those that a mesh axis runs over, the one named last changes fastest.
Arguments:
- inputs: bfloat16 [4096, 16384], P('dp', 'feat'), may hold values from -6 to 6
- cotangent: bfloat16 [4096, 16384], P('dp', 'feat'), may hold values from -6 to 6
- butterfly: bfloat16 [6, 16384, 512], P(None, ('feat', 'dp')), may hold values from -0.109375 to 0.109375
- low_in: bfloat16 [16384, 256], P(('feat', 'dp')), may hold values from -0.046875 to 0.046875
- low_out: bfloat16 [256, 16384], P(None, ('feat', 'dp')), may hold values from -0.375 to 0.375
Outputs:
- output: bfloat16 [4096, 16384], P('dp', 'feat')
- grad_inputs: bfloat16 [4096, 16384], P('dp', 'feat')
- grad_butterfly: float32 [6, 16384, 512], P(None, ('feat', 'dp'))
- grad_low_in: float32 [16384, 256], P(('feat', 'dp'))
- grad_low_out: float32 [256, 16384], P(None, ('feat', 'dp'))
All inputs are finite; a program needn't handle non-finite values.
Results may differ from a plain program's by a relative error of at most 0.015.
Values may be sent and summed in bfloat16 or wider, within the bound.
No kernel may reach another device: no remote copies, remote signals or barrier semaphores. Data moves between devices by JAX's collectives and lax.ppermute only.
A program may use at most 64 MiB of HBM per device.

v0:
```python
import math

import jax
import jax.numpy as jnp
from jax import lax
from jax.sharding import PartitionSpec as P

BS = 512
LEVELS = 5


def from_partner(value, axis, stride):
    mask = 2**stride
    pairs = [(source, source ^ mask) for source in range(lax.axis_size(axis))]
    return lax.ppermute(value, axis, pairs)


def forward_mul(left, weights):
    return jnp.einsum("tnr,nrc->tnc", left, weights, preferred_element_type=jnp.float32)


def backward_mul(left, weights):
    return jnp.einsum("tnc,nrc->tnr", left, weights, preferred_element_type=jnp.float32)


def body(inputs, cotangent, butterfly, low_in, low_out):
    tok_count, width = inputs.shape
    factor = 1.0 / math.sqrt(tok_count * lax.axis_size("dp"))
    blocks = width // BS
    local_bits = blocks.bit_length() - 1
    in_blocks = inputs.reshape(tok_count, blocks, BS)
    cot_blocks = cotangent.reshape(tok_count, blocks, BS)
    weight_full, low_in_full, low_out_full = (
        lax.all_gather(butterfly, "dp", axis=1, tiled=True),
        lax.all_gather(low_in, "dp", axis=0, tiled=True),
        lax.all_gather(low_out, "dp", axis=1, tiled=True),
    )
    weight_blocks = weight_full.reshape(LEVELS + 1, blocks, BS, BS)
    part_s = jnp.dot(inputs, low_in_full, preferred_element_type=jnp.float32)
    part_t = lax.dot_general(
        cotangent, low_out_full, (((1,), (1,)), ((), ())), preferred_element_type=jnp.float32
    )
    sum_s, sum_t = lax.psum((part_s, part_t), "feat")
    low_s = sum_s.astype(jnp.bfloat16)
    low_t = sum_t.astype(jnp.bfloat16)
    result = forward_mul(in_blocks, weight_blocks[0])
    partners = [in_blocks]
    for level in range(LEVELS):
        near = from_partner(inputs, "feat", level - local_bits).reshape(tok_count, blocks, BS)
        partners.append(near)
        result = result + forward_mul(near, weight_blocks[level + 1])
    result = result.reshape(tok_count, width) + jnp.dot(
        low_s, low_out_full, preferred_element_type=jnp.float32
    )
    output = result.astype(jnp.bfloat16)
    back = backward_mul(cot_blocks, weight_blocks[0])
    for level in range(LEVELS):
        term = backward_mul(cot_blocks, weight_blocks[level + 1]).astype(jnp.bfloat16)
        term = from_partner(term, "feat", level - local_bits)
        back = back + term.astype(jnp.float32)
    back = back.reshape(tok_count, width) + lax.dot_general(
        low_t, low_in_full, (((1,), (1,)), ((), ())), preferred_element_type=jnp.float32
    )
    grad_inputs = back.astype(jnp.bfloat16)
    grad_list = [
        jnp.einsum("tnr,tnc->nrc", near, cot_blocks, preferred_element_type=jnp.float32).reshape(
            width, BS
        )
        for near in partners
    ]
    grad_weights = jnp.stack(grad_list) * factor
    grad_down = (
        lax.dot_general(inputs, low_t, (((0,), (0,)), ((), ())), preferred_element_type=jnp.float32)
        * factor
    )
    grad_up = (
        lax.dot_general(
            low_s, cotangent, (((0,), (0,)), ((), ())), preferred_element_type=jnp.float32
        )
        * factor
    )
    grad_butterfly, grad_low_in, grad_low_out = (
        lax.psum_scatter(
            grad_weights.astype(jnp.bfloat16), "dp", scatter_dimension=1, tiled=True
        ).astype(jnp.float32),
        lax.psum_scatter(
            grad_down.astype(jnp.bfloat16), "dp", scatter_dimension=0, tiled=True
        ).astype(jnp.float32),
        lax.psum_scatter(
            grad_up.astype(jnp.bfloat16), "dp", scatter_dimension=1, tiled=True
        ).astype(jnp.float32),
    )
    return (output, grad_inputs, grad_butterfly, grad_low_in, grad_low_out)


def solution(mesh):
    return jax.shard_map(
        body,
        mesh=mesh,
        in_specs=(
            P("dp", "feat"),
            P("dp", "feat"),
            P(None, ("feat", "dp"), None),
            P(("feat", "dp"), None),
            P(None, ("feat", "dp")),
        ),
        out_specs=(
            P("dp", "feat"),
            P("dp", "feat"),
            P(None, ("feat", "dp"), None),
            P(("feat", "dp"), None),
            P(None, ("feat", "dp")),
        ),
        check_vma=False,
    )
```

profile of v0, /device:TPU:32, one launch (start us, length us, event | category | flops | bytes accessed | tf_op | source)
XLA Modules:
  0.0 815.0 jit_solution(13628782252003648812)
XLA Ops:
  7.2 50.5 %all_gather.10 = bf16[512,256]{1,0:T(8,128)(2,1)S(1)} all-gather(bf16[32,256]{1,0:T(8,128)(2,1)} %param.8), channel_id=1, replica_groups=mesh['dp'=16,'feat'=32] {'dp'}, dimensions={0}, use_global_device_ids=true | all-gather | bytes 278528 | tf_op jit(solution)/shard_map/all_gather | solution.py:35
  57.8 37.5 %all_gather.11 = bf16[256,512]{0,1:T(8,128)(2,1)S(1)} all-gather(bf16[256,32]{0,1:T(8,128)(2,1)} %param.9), channel_id=1, replica_groups=mesh['dp'=16,'feat'=32] {'dp'}, dimensions={1}, use_global_device_ids=true | all-gather | bytes 278528 | tf_op jit(solution)/shard_map/all_gather | solution.py:36
  96.7 217.4 %all-reduce.2 = (bf16[256,256]{1,0:T(8,128)(2,1)S(1)}, bf16[256,256]{1,0:T(8,128)(2,1)S(1)}) all-reduce(f32[256,256]{1,0:T(8,128)S(1)} %fusion.31, f32[256,256]{1,0:T(8,128)S(1)} %fusion.32), channel_id=1, replica_groups=mesh['dp'=16,'feat'=32] {'feat'}, use_global_device_ids=true, to_apply=%region_0.0 | all-reduce | flops 131072 | bytes 786432 | tf_op jit(solution)/shard_map/psum | solution.py:43
  315.3 1.9 collective-permute-start.4
  317.3 9.6 %collective-permute-start.3 = (bf16[256,512]{1,0:T(8,128)(2,1)S(1)}, bf16[256,512]{1,0:T(8,128)(2,1)S(1)}, u32[]{:S(2)}, u32[]{:S(2)}) collective-permute-start(bf16[256,512]{1,0:T(8,128)(2,1)S(1)} %copy-done.2), channel_id=1, source_target_pairs={{0,8},{1,9},{2,10},{3,11},{4,12},{5,13},{6,14},{7,15},{8,0},{9,1},... | collective-permute-start | bytes 786440 | tf_op jit(solution)/shard_map/ppermute | solution.py:15
  326.9 11.7 %collective-permute-start.2 = (bf16[256,512]{1,0:T(8,128)(2,1)S(1)}, bf16[256,512]{1,0:T(8,128)(2,1)S(1)}, u32[]{:S(2)}, u32[]{:S(2)}) collective-permute-start(bf16[256,512]{1,0:T(8,128)(2,1)S(1)} %copy-done.2), channel_id=1, source_target_pairs={{0,4},{1,5},{2,6},{3,7},{4,0},{5,1},{6,2},{7,3},{8,12},{9,13},{10,... | collective-permute-start | bytes 786440 | tf_op jit(solution)/shard_map/ppermute | solution.py:15
  338.6 3.0 collective-permute-start.1
  345.0 4.8 collective-permute-done
  351.6 2.6 multiply_convert_fusion
  356.9 66.1 %reduce-scatter.12.cloned.1.call-done = bf16[32,256]{1,0:T(8,128)(2,1)} async-done(((bf16[512,256]{1,0:T(8,128)(2,1)}), bf16[32,256]{1,0:T(8,128)(2,1)}) %reduce-scatter.12.cloned.1.call-update) | async-done | bytes 16400
  424.6 92.9 %reduce-scatter.10.cloned.1.call-done = bf16[32,256]{1,0:T(8,128)(2,1)} async-done(((bf16[512,256]{1,0:T(8,128)(2,1)}), bf16[32,256]{1,0:T(8,128)(2,1)}) %reduce-scatter.10.cloned.1.call-update) | async-done | bytes 16400
  519.0 127.0 %reduce-scatter.8.cloned.1.call-done = bf16[6,32,512]{2,1,0:T(8,128)(2,1)} async-done(((bf16[6,512,512]{2,1,0:T(8,128)(2,1)}), bf16[6,32,512]{2,1,0:T(8,128)(2,1)}) %reduce-scatter.8.cloned.1.call-update) | async-done | bytes 196624 | tf_op jit(solution)/shard_map/reduce_scatter | solution.py:83
  647.7 97.7 %all-gather.2.cloned.1.call-done = bf16[6,512,512]{2,1,0:T(8,128)(2,1)} async-done(((bf16[6,32,512]{2,1,0:T(8,128)(2,1)}), bf16[6,512,512]{2,1,0:T(8,128)(2,1)}) %all-gather.2.cloned.1.call-update) | async-done | bytes 3145744 | tf_op jit(solution)/shard_map/all_gather | solution.py:34
  745.4 2.2 fusion.15
  747.6 3.4 collective-permute-start.5
  751.0 2.1 fusion.16
  753.1 4.8 collective-permute-start.6
  757.9 2.1 fusion.17
  760.0 10.3 %collective-permute-start.7 = (bf16[256,1,512]{0,2,1:T(8,128)(2,1)}, bf16[256,1,512]{0,2,1:T(8,128)(2,1)}, u32[]{:S(2)}, u32[]{:S(2)}) collective-permute-start(bf16[256,1,512]{0,2,1:T(8,128)(2,1)} %fusion.17), channel_id=1, source_target_pairs={{0,4},{1,5},{2,6},{3,7},{4,0},{5,1},{6,2},{7,3},{8,12},{9,13},{10,... | collective-permute-start | bytes 786440 | tf_op jit(solution)/shard_map/ppermute | solution.py:15
  771.3 2.0 collective-permute-start.8
  774.4 3.2 collective-permute-start.9
  783.3 8.4 %collective-permute-done.8 = bf16[256,1,512]{0,2,1:T(8,128)(2,1)} collective-permute-done((bf16[256,1,512]{0,2,1:T(8,128)(2,1)}, bf16[256,1,512]{0,2,1:T(8,128)(2,1)}, u32[]{:S(2)}, u32[]{:S(2)}) %collective-permute-start.8) | collective-permute-done | bytes 262176 | tf_op jit(solution)/shard_map/ppermute | solution.py:15
  791.7 12.5 %collective-permute-done.9 = bf16[256,1,512]{0,2,1:T(8,128)(2,1)} collective-permute-done((bf16[256,1,512]{0,2,1:T(8,128)(2,1)}, bf16[256,1,512]{0,2,1:T(8,128)(2,1)}, u32[]{:S(2)}, u32[]{:S(2)}) %collective-permute-start.9) | collective-permute-done | bytes 262176 | tf_op jit(solution)/shard_map/ppermute | solution.py:15
  804.2 2.5 fusion.20
  (73 shorter events, 24.6 us)
Async XLA Ops:
  7.2 88.1 %copy-start = (bf16[256,512]{1,0:T(8,128)(2,1)S(1)}, bf16[256,512]{1,0:T(8,128)(2,1)}, u32[]{:S(2)}) copy-start(bf16[256,512]{1,0:T(8,128)(2,1)} %param.6) | copy-start | bytes 786436
  7.2 308.1 %copy-start.2 = (bf16[256,512]{1,0:T(8,128)(2,1)S(1)}, bf16[256,512]{1,0:T(8,128)(2,1)}, u32[]{:S(2)}) copy-start(bf16[256,512]{1,0:T(8,128)(2,1)} %param.5) | copy-start | bytes 786436
  7.2 415.9 %reduce-scatter.12.cloned.1.call-start = ((), (), s32[]{:S(2)}) async-start(), calls=%async_computation.6 | async-start | bytes 278528
  315.3 202.2 %reduce-scatter.10.cloned.1.call-start = ((), (), s32[]{:S(2)}) async-start(), calls=%async_computation.5 | async-start | bytes 278528
  315.3 35.9 %collective-permute-start.4 = (bf16[256,512]{1,0:T(8,128)(2,1)S(1)}, bf16[256,512]{1,0:T(8,128)(2,1)S(1)}, u32[]{:S(2)}, u32[]{:S(2)}) collective-permute-start(bf16[256,512]{1,0:T(8,128)(2,1)S(1)} %copy-done.2), channel_id=1, source_target_pairs={{0,16},{1,17},{2,18},{3,19},{4,20},{5,21},{6,22},{7,23},{8,24},{9,... | collective-permute-start | bytes 786440 | tf_op jit(solution)/shard_map/ppermute | solution.py:15
  317.3 33.6 %collective-permute-start.3 = (bf16[256,512]{1,0:T(8,128)(2,1)S(1)}, bf16[256,512]{1,0:T(8,128)(2,1)S(1)}, u32[]{:S(2)}, u32[]{:S(2)}) collective-permute-start(bf16[256,512]{1,0:T(8,128)(2,1)S(1)} %copy-done.2), channel_id=1, source_target_pairs={{0,8},{1,9},{2,10},{3,11},{4,12},{5,13},{6,14},{7,15},{8,0},{9,1},... | collective-permute-start | bytes 786440 | tf_op jit(solution)/shard_map/ppermute | solution.py:15
  326.9 23.6 %collective-permute-start.2 = (bf16[256,512]{1,0:T(8,128)(2,1)S(1)}, bf16[256,512]{1,0:T(8,128)(2,1)S(1)}, u32[]{:S(2)}, u32[]{:S(2)}) collective-permute-start(bf16[256,512]{1,0:T(8,128)(2,1)S(1)} %copy-done.2), channel_id=1, source_target_pairs={{0,4},{1,5},{2,6},{3,7},{4,0},{5,1},{6,2},{7,3},{8,12},{9,13},{10,... | collective-permute-start | bytes 786440 | tf_op jit(solution)/shard_map/ppermute | solution.py:15
  338.6 11.6 %collective-permute-start.1 = (bf16[256,512]{1,0:T(8,128)(2,1)S(1)}, bf16[256,512]{1,0:T(8,128)(2,1)S(1)}, u32[]{:S(2)}, u32[]{:S(2)}) collective-permute-start(bf16[256,512]{1,0:T(8,128)(2,1)S(1)} %copy-done.2), channel_id=1, source_target_pairs={{0,2},{1,3},{2,0},{3,1},{4,6},{5,7},{6,4},{7,5},{8,10},{9,11},{10,... | collective-permute-start | bytes 786440 | tf_op jit(solution)/shard_map/ppermute | solution.py:15
  341.6 8.3 %collective-permute-start = (bf16[256,512]{1,0:T(8,128)(2,1)S(1)}, bf16[256,512]{1,0:T(8,128)(2,1)S(1)}, u32[]{:S(2)}, u32[]{:S(2)}) collective-permute-start(bf16[256,512]{1,0:T(8,128)(2,1)S(1)} %copy-done.2), channel_id=1, source_target_pairs={{0,1},{1,0},{2,3},{3,2},{4,5},{5,4},{6,7},{7,6},{8,9},{9,8},{10,11... | collective-permute-start | bytes 786440 | tf_op jit(solution)/shard_map/ppermute | solution.py:15
  344.6 301.3 %reduce-scatter.8.cloned.1.call-start = ((), (), s32[]{:S(2)}) async-start(), calls=%async_computation.4 | async-start | bytes 3342336 | tf_op jit(solution)/shard_map/reduce_scatter | solution.py:83
  350.5 6.4 copy-start.11
  350.9 3.3 copy-start.9
  351.2 3.0 copy-start.7
  354.2 391.1 %all-gather.2.cloned.1.call-start = ((), (), s32[]{:S(2)}) async-start(), calls=%async_computation.3 | async-start | bytes 3342336 | tf_op jit(solution)/shard_map/all_gather | solution.py:34
  745.4 24.9 %copy-start.1 = (bf16[6,512,512]{2,1,0:T(8,128)(2,1)S(1)}, bf16[6,512,512]{2,1,0:T(8,128)(2,1)}, u32[]{:S(2)}) copy-start(bf16[6,512,512]{2,1,0:T(8,128)(2,1)} %all-gather.2.cloned.1.call-done) | copy-start | bytes 9437188
  747.6 31.3 %copy-start.10 = (bf16[256,512]{1,0:T(8,128)(2,1)S(1)}, bf16[256,512]{1,0:T(8,128)(2,1)}, u32[]{:S(2)}) copy-start(bf16[256,512]{1,0:T(8,128)(2,1)} %copy-done.9) | copy-start | bytes 786436
  747.6 35.7 %collective-permute-start.5 = (bf16[256,1,512]{0,2,1:T(8,128)(2,1)}, bf16[256,1,512]{0,2,1:T(8,128)(2,1)}, u32[]{:S(2)}, u32[]{:S(2)}) collective-permute-start(bf16[256,1,512]{0,2,1:T(8,128)(2,1)} %fusion.15), channel_id=1, source_target_pairs={{0,1},{1,0},{2,3},{3,2},{4,5},{5,4},{6,7},{7,6},{8,9},{9,8},{10,11... | collective-permute-start | bytes 786440 | tf_op jit(solution)/shard_map/ppermute | solution.py:15
  753.1 26.2 %copy-start.8 = (bf16[256,512]{1,0:T(8,128)(2,1)S(1)}, bf16[256,512]{1,0:T(8,128)(2,1)}, u32[]{:S(2)}) copy-start(bf16[256,512]{1,0:T(8,128)(2,1)} %copy-done.7) | copy-start | bytes 786436
  753.1 30.2 %collective-permute-start.6 = (bf16[256,1,512]{0,2,1:T(8,128)(2,1)}, bf16[256,1,512]{0,2,1:T(8,128)(2,1)}, u32[]{:S(2)}, u32[]{:S(2)}) collective-permute-start(bf16[256,1,512]{0,2,1:T(8,128)(2,1)} %fusion.16), channel_id=1, source_target_pairs={{0,2},{1,3},{2,0},{3,1},{4,6},{5,7},{6,4},{7,5},{8,10},{9,11},{10,... | collective-permute-start | bytes 786440 | tf_op jit(solution)/shard_map/ppermute | solution.py:15
  760.0 19.7 %copy-start.3 = (bf16[256,512]{1,0:T(8,128)(2,1)S(1)}, bf16[256,512]{1,0:T(8,128)(2,1)}, u32[]{:S(2)}) copy-start(bf16[256,512]{1,0:T(8,128)(2,1)} %param.5) | copy-start | bytes 786436
  760.0 23.3 %collective-permute-start.7 = (bf16[256,1,512]{0,2,1:T(8,128)(2,1)}, bf16[256,1,512]{0,2,1:T(8,128)(2,1)}, u32[]{:S(2)}, u32[]{:S(2)}) collective-permute-start(bf16[256,1,512]{0,2,1:T(8,128)(2,1)} %fusion.17), channel_id=1, source_target_pairs={{0,4},{1,5},{2,6},{3,7},{4,0},{5,1},{6,2},{7,3},{8,12},{9,13},{10,... | collective-permute-start | bytes 786440 | tf_op jit(solution)/shard_map/ppermute | solution.py:15
  771.3 8.7 %copy-start.13 = (bf16[256,512]{1,0:T(8,128)(2,1)S(1)}, bf16[256,512]{1,0:T(8,128)(2,1)}, u32[]{:S(2)}) copy-start(bf16[256,512]{1,0:T(8,128)(2,1)} %copy-done.12) | copy-start | bytes 786436
  771.3 20.3 %collective-permute-start.8 = (bf16[256,1,512]{0,2,1:T(8,128)(2,1)}, bf16[256,1,512]{0,2,1:T(8,128)(2,1)}, u32[]{:S(2)}, u32[]{:S(2)}) collective-permute-start(bf16[256,1,512]{0,2,1:T(8,128)(2,1)} %fusion.18), channel_id=1, source_target_pairs={{0,8},{1,9},{2,10},{3,11},{4,12},{5,13},{6,14},{7,15},{8,0},{9,1},... | collective-permute-start | bytes 786440 | tf_op jit(solution)/shard_map/ppermute | solution.py:15
  774.4 29.7 %collective-permute-start.9 = (bf16[256,1,512]{0,2,1:T(8,128)(2,1)}, bf16[256,1,512]{0,2,1:T(8,128)(2,1)}, u32[]{:S(2)}, u32[]{:S(2)}) collective-permute-start(bf16[256,1,512]{0,2,1:T(8,128)(2,1)} %fusion.19), channel_id=1, source_target_pairs={{0,16},{1,17},{2,18},{3,19},{4,20},{5,21},{6,22},{7,23},{8,24},{9,... | collective-permute-start | bytes 786440 | tf_op jit(solution)/shard_map/ppermute | solution.py:15
  (4 other events, 5.7 us)
Sparse Core Ops, SparseCore 0:
  315.4 107.6 reduce-scatter.11
  428.9 88.4 reduce-scatter.9
  522.4 123.5 reduce-scatter.7
  649.2 96.1 all-gather.1
where the time goes:
time: 816 us; the launch traced here: 815 us
  waiting for transfers between devices  410 us (50%)
  blocking collectives  305 us (37%)
  starting transfers between devices  52.1 us (6%)
  matrix products  20.7 us (3%)
  between operations  14.1 us (2%)
  local copies, waits for them, and re-layouts  8.45 us (1%)
    psum x1, blocking collectives, body(): sum_s, sum_t = lax.psum((part_s, part_t), 'feat')  217 us
    unnamed x6, waiting for transfers between devices  160 us
    reduce_scatter x1, waiting for transfers between devices, body(): lax.psum_scatter(grad_weights.astype(jnp.bfloat16), 'dp', scatter_dimensi...  127 us
    all_gather x1, waiting for transfers between devices, body(): lax.all_gather(butterfly, 'dp', axis=1, tiled=True)  97.7 us
    ppermute x10, starting transfers between devices, from_partner(): return lax.ppermute(value, axis, pairs)  51.9 us
    all_gather x1, blocking collectives, body(): lax.all_gather(low_in, 'dp', axis=0, tiled=True)  50.5 us
    all_gather x1, blocking collectives, body(): lax.all_gather(low_out, 'dp', axis=1, tiled=True)  37.5 us
    ppermute x10, waiting for transfers between devices, from_partner(): return lax.ppermute(value, axis, pairs)  25.7 us
  transfers between devices with their start and end apart: 14, of which 7 were waited for; matrix products, arithmetic and copies ran while one was open for 3% of the time, Pallas kernels for 0%

commit v1 on v0

v1 whole, which is shorter than its diff:
```python
import functools

import jax
import jax.numpy as jnp
from jax import lax
from jax.experimental import pallas as pl
from jax.experimental.pallas import tpu as pltpu
from jax.sharding import PartitionSpec as P

BS = 512
LEVELS = 5
R = 256
SCALE = 1.0 / 64.0
F32 = jnp.float32
BF16 = jnp.bfloat16


def dp_pairs(step):
    pairs = []
    for i in range(16):
        y, h, c = step(i // 4, (i // 2) % 2, i % 2)
        pairs.append((i, (y * 2 + h) * 2 + c))
    return pairs


CORE = dp_pairs(lambda y, h, c: (y, h, 1 - c))
Z_HI = dp_pairs(lambda y, h, c: (y, 1 - h, c))
Y_STEP = [dp_pairs(lambda y, h, c, k=k: ((y + k) % 4, h, c)) for k in range(4)]
X_STEP = [[(i, (i // 4) * 4 + (i % 4 + k) % 4) for i in range(32)] for k in range(4)]
PARTNER = [[(i, i ^ (1 << level)) for i in range(32)] for level in range(LEVELS)]
CORE_GROUPS = [[2 * i, 2 * i + 1] for i in range(8)]


def over_dp(value, pairs):
    return lax.ppermute(value, "dp", pairs)


def over_feat(value, pairs):
    return lax.ppermute(value, "feat", pairs)


def dot_nn(a, b):
    return lax.dot_general(a, b, (((1,), (0,)), ((), ())), preferred_element_type=F32)


def dot_nt(a, b):
    return lax.dot_general(a, b, (((1,), (1,)), ((), ())), preferred_element_type=F32)


def dot_tn(a, b):
    return lax.dot_general(a, b, (((0,), (0,)), ((), ())), preferred_element_type=F32)


def call(kernel, out, place, *args, scratch=(), name, limit=24):
    shapes = [jax.ShapeDtypeStruct(s, d) for s, d in out]
    return pl.pallas_call(
        kernel,
        out_shape=shapes,
        in_specs=[pl.BlockSpec(memory_space=pltpu.SMEM)]
        + [pl.BlockSpec(memory_space=pltpu.VMEM)] * len(args),
        out_specs=[pl.BlockSpec(memory_space=pltpu.VMEM)] * len(out),
        scratch_shapes=list(scratch),
        compiler_params=pltpu.CompilerParams(vmem_limit_bytes=limit << 20),
        name=name,
    )(place, *args)


def chunk_of(place, y, h, c):
    return c * 4 + lax.rem(place[0] - y + 4, 4), lax.rem(place[1] + h, 2)


def rows_of(place, k, g, c):
    y = lax.rem(place[0] + k, 4)
    h = lax.rem(place[1] + g, 2)
    return pl.multiple_of(((y * 2 + h) * 2 + c) * 32, 32)


def project_kernel(place, gathered, inputs, cot, low, p0, p1, p2, p3, part):
    for d in range(16):
        i, j = chunk_of(place, d // 4, (d // 2) % 2, d % 2)
        low[d * 32 : (d + 1) * 32, :] = gathered[i, j]
    part[:, :R] = dot_nn(inputs[...], low[:, :R])
    part[:, R:] = dot_nn(cot[...], low[:, R:])
    for k, out in enumerate((p0, p1, p2, p3)):
        row = pl.multiple_of(lax.rem(place[3] + k, 4) * 64, 64)
        out[...] = part[pl.ds(row, 64), :].astype(out.dtype)


def weights_kernel(place, gathered, inputs, near0, near1, cot, z, back, front, far, w):
    for d in range(16):
        i, j = chunk_of(place, d // 4, (d // 2) % 2, d % 2)
        w[:, d * 32 : (d + 1) * 32, :] = gathered[i, j]
    for level in range(LEVELS):
        z[level] = dot_nt(cot[...], w[level + 1]).astype(BF16)
    back[...] = dot_nt(cot[...], w[0])
    front[...] = dot_nn(inputs[...], w[0]) + dot_nn(near0[...], w[1]) + dot_nn(near1[...], w[2])
    far[...] = w[3:]


def split_rows(place, grad, n, keep, send):
    for k in range(4):
        for g in range(2):
            keep[k, g, n] = grad[pl.ds(rows_of(place, k, g, place[2]), 32), :].astype(BF16)
            send[k, g, n] = grad[pl.ds(rows_of(place, k, g, 1 - place[2]), 32), :].astype(BF16)


def near_grads_kernel(place, inputs, near0, near1, cot, keep, send, grad):
    for n, left in enumerate((inputs, near0, near1)):
        grad[...] = dot_tn(left[...], cot[...])
        split_rows(place, grad, n, keep, send)


def far_grads_kernel(
    place, far0, far1, far2, inputs, cot, st0, st1, st2, st3, keep, send, st, grad
):
    for k, part in enumerate((st0, st1, st2, st3)):
        row = pl.multiple_of(lax.rem(place[3] + 4 - k, 4) * 64, 64)
        st[pl.ds(row, 64), :] = part[...]
    for n, left in enumerate((far0, far1, far2)):
        grad[...] = dot_tn(left[...], cot[...])
        split_rows(place, grad, n, keep, send)
    grad[:, :R] = dot_tn(inputs[...], st[:, R:])
    grad[:, R:] = dot_tn(cot[...], st[:, :R])
    split_rows(place, grad, 3, keep, send)


def core_sum_kernel(place, keep, got, q0, q1, q2, q3):
    for k, out in enumerate((q0, q1, q2, q3)):
        out[...] = (keep[k].astype(F32) + got[k].astype(F32)).astype(out.dtype)


def y_sum_kernel(place, q0, q1, q2, q3, mine, send):
    total = q0[...] + q1[...].astype(F32) + q2[...].astype(F32) + q3[...].astype(F32)
    mine[...] = total[0]
    send[...] = total[1].astype(BF16)


def output_kernel(place, front, far0, far1, far2, w, st, low, out):
    total = front[...] + dot_nt(st[:, :R], low[:, R:])
    for n, left in enumerate((far0, far1, far2)):
        total = total + dot_nn(left[...], w[n])
    out[...] = total.astype(BF16)


def grad_inputs_kernel(place, back, z0, z1, z2, z3, z4, st, low, out):
    total = back[...] + dot_nt(st[:, R:], low[:, :R])
    for z in (z0, z1, z2, z3, z4):
        total = total + z[...].astype(F32)
    out[...] = total.astype(BF16)


def reduce_rows(place, kernel, args, n, scratch, name):
    half = (4, 2, n, 32, BS)
    quarter = (2, n, 32, BS)
    extra = call(
        kernel, [(half, BF16)] * 2 + scratch, place, *args,
        scratch=[pltpu.VMEM((BS, BS), F32)], name=name,
    )
    keep, send = extra[:2]
    got = over_dp(send, CORE)
    q = call(core_sum_kernel, [(quarter, F32)] + [(quarter, BF16)] * 3, place, keep, got,
             name=name + "_core")
    r = [over_dp(q[k], Y_STEP[k]) for k in (1, 2, 3)]
    mine, far = call(y_sum_kernel, [(quarter[1:], F32), (quarter[1:], BF16)], place, q[0], *r,
                     name=name + "_y")
    got = over_dp(far, Z_HI)
    return (mine + got.astype(F32)) * SCALE, extra[2:]


def gather_rows(shard):
    pair = jnp.stack([shard, over_dp(shard, Z_HI)])
    steps = [pair] + [over_dp(pair, Y_STEP[k]) for k in (1, 2, 3)]
    return lax.all_gather(
        jnp.stack(steps), "dp", axis=0, tiled=True, axis_index_groups=CORE_GROUPS
    )


def body(inputs, cotangent, butterfly, low_in, low_out):
    dp = lax.axis_index("dp")
    place = jnp.stack([dp // 4, (dp // 2) % 2, dp % 2, lax.axis_index("feat") % 4]).astype(jnp.int32)
    low_all = gather_rows(jnp.concatenate([low_in, low_out.T], axis=1))
    w_all = gather_rows(butterfly)
    near = [over_feat(inputs, PARTNER[level]) for level in range(LEVELS)]

    piece = (64, 2 * R)
    low, *parts = call(
        project_kernel, [((BS, 2 * R), BF16), (piece, F32)] + [(piece, BF16)] * 3,
        place, low_all, inputs, cotangent,
        scratch=[pltpu.VMEM((256, 2 * R), F32)], name="project",
    )
    total = parts[0]
    for k in (1, 2, 3):
        total = total + over_feat(parts[k], X_STEP[k]).astype(F32)
    total = total.astype(BF16)
    for level in (2, 3, 4):
        total = (total.astype(F32) + over_feat(total, PARTNER[level]).astype(F32)).astype(BF16)
    st_parts = [total] + [over_feat(total, X_STEP[k]) for k in (1, 2, 3)]

    block = (256, BS)
    z, back, front, w_far = call(
        weights_kernel,
        [((LEVELS,) + block, BF16), (block, F32), (block, F32), ((3, BS, BS), BF16)],
        place, w_all, inputs, near[0], near[1], cotangent,
        scratch=[pltpu.VMEM((LEVELS + 1, BS, BS), BF16)], name="weights",
    )
    z_near = [over_feat(z[level], PARTNER[level]) for level in range(LEVELS)]

    grads_a, _ = reduce_rows(
        place, near_grads_kernel, (inputs, near[0], near[1], cotangent), 3, [], "near_grads"
    )
    grads_b, (st,) = reduce_rows(
        place, far_grads_kernel, (near[2], near[3], near[4], inputs, cotangent, *st_parts), 4,
        [((256, 2 * R), BF16)], "far_grads",
    )
    (output,) = call(
        output_kernel, [(block, BF16)], place, front, near[2], near[3], near[4], w_far, st, low,
        name="output",
    )
    (grad_inputs,) = call(
        grad_inputs_kernel, [(block, BF16)], place, back, *z_near, st, low, name="grad_inputs"
    )
    grad_butterfly = jnp.concatenate([grads_a, grads_b[:3]], axis=0)
    return output, grad_inputs, grad_butterfly, grads_b[3, :, :R], grads_b[3, :, R:].T


def solution(mesh):
    specs = (
        P("dp", "feat"),
        P("dp", "feat"),
        P(None, ("feat", "dp"), None),
        P(("feat", "dp"), None),
        P(None, ("feat", "dp")),
    )
    return jax.shard_map(body, mesh=mesh, in_specs=specs, out_specs=specs, check_vma=False)
```

time: 816 us -> 275 us (0.34)
  the two profiles are of different devices: /device:TPU:32 before, /device:TPU:8 now
where the time goes in v1:
time: 275 us; the launch traced here: 274 us
  starting transfers between devices  155 us (56%)
  waiting for transfers between devices  83.3 us (30%)
  between operations  14.7 us (5%)
  Pallas kernels  11.9 us (4%)
  other arithmetic  4.13 us (2%)
    ppermute x18, starting transfers between devices, over_dp(): return lax.ppermute(value, 'dp', pairs)  79.8 us
    ppermute x19, starting transfers between devices, over_feat(): return lax.ppermute(value, 'feat', pairs)  74.7 us
    ppermute x19, waiting for transfers between devices, over_feat(): return lax.ppermute(value, 'feat', pairs)  52.1 us
    ppermute x18, waiting for transfers between devices, over_dp(): return lax.ppermute(value, 'dp', pairs)  31.1 us
    pallas_call x10, Pallas kernels, call(): pl.pallas_call(kernel, out_shape=shapes, in_specs=[pl.BlockSpec(memory_sp...  11.9 us
  transfers between devices with their start and end apart: 38, of which 17 were waited for; matrix products, arithmetic and copies ran while one was open for 1% of the time, Pallas kernels for 3%

profile of v1, /device:TPU:8, one launch (start us, length us, event | category | flops | bytes accessed | tf_op | source)
XLA Modules:
  0.0 273.5 jit_solution(12656922263955200269)
XLA Ops:
  7.2 15.7 %collective-permute-start = (bf16[6,32,512]{2,1,0:T(8,128)(2,1)}, bf16[6,32,512]{2,1,0:T(8,128)(2,1)S(1)}, u32[]{:S(2)}, u32[]{:S(2)}) collective-permute-start(bf16[6,32,512]{2,1,0:T(8,128)(2,1)} %param.7), channel_id=1, source_target_pairs={{0,64},{32,96},{64,0},{96,32},{128,192},{160,224},{192,128},{224,1... | collective-permute-start | bytes 589832 | tf_op jit(solution)/shard_map/ppermute | solution.py:35
  25.6 10.4 %collective-permute-done = bf16[6,32,512]{2,1,0:T(8,128)(2,1)S(1)} collective-permute-done((bf16[6,32,512]{2,1,0:T(8,128)(2,1)}, bf16[6,32,512]{2,1,0:T(8,128)(2,1)S(1)}, u32[]{:S(2)}, u32[]{:S(2)}) %collective-permute-start) | collective-permute-done | bytes 196640 | tf_op jit(solution)/shard_map/ppermute | solution.py:35
  40.3 3.5 %collective-permute-start.2 = (bf16[2,6,32,512]{3,2,1,0:T(8,128)(2,1)S(1)}, bf16[2,6,32,512]{3,2,1,0:T(8,128)(2,1)S(1)}, u32[]{:S(2)}, u32[]{:S(2)}) collective-permute-start(bf16[2,6,32,512]{3,2,1,0:T(8,128)(2,1)S(1)} %get-tuple-element.63), channel_id=1, source_target_pairs={{0,256},{32,288},{64,320},{96,352},{128,384},{160,416},{192,448},{... | collective-permute-start | bytes 1179656 | tf_op jit(solution)/shard_map/ppermute | solution.py:35
  43.9 3.8 %collective-permute-start.1 = (bf16[2,6,32,512]{3,2,1,0:T(8,128)(2,1)S(1)}, bf16[2,6,32,512]{3,2,1,0:T(8,128)(2,1)S(1)}, u32[]{:S(2)}, u32[]{:S(2)}) collective-permute-start(bf16[2,6,32,512]{3,2,1,0:T(8,128)(2,1)S(1)} %get-tuple-element.63), channel_id=1, source_target_pairs={{0,128},{32,160},{64,192},{96,224},{128,256},{160,288},{192,320},{... | collective-permute-start | bytes 1179656 | tf_op jit(solution)/shard_map/ppermute | solution.py:35
  49.8 3.8 %collective-permute-start.11 = (bf16[2,32,512]{2,1,0:T(8,128)(2,1)S(1)}, bf16[2,32,512]{2,1,0:T(8,128)(2,1)S(1)}, u32[]{:S(2)}, u32[]{:S(2)}) collective-permute-start(bf16[2,32,512]{2,1,0:T(8,128)(2,1)S(1)} %get-tuple-element.67), channel_id=1, source_target_pairs={{0,256},{32,288},{64,320},{96,352},{128,384},{160,416},{192,448},{... | collective-permute-start | bytes 196616 | tf_op jit(solution)/shard_map/ppermute | solution.py:35
  53.9 3.5 %collective-permute-start.10 = (bf16[2,32,512]{2,1,0:T(8,128)(2,1)S(1)}, bf16[2,32,512]{2,1,0:T(8,128)(2,1)S(1)}, u32[]{:S(2)}, u32[]{:S(2)}) collective-permute-start(bf16[2,32,512]{2,1,0:T(8,128)(2,1)S(1)} %get-tuple-element.67), channel_id=1, source_target_pairs={{0,128},{32,160},{64,192},{96,224},{128,256},{160,288},{192,320},{... | collective-permute-start | bytes 196616 | tf_op jit(solution)/shard_map/ppermute | solution.py:35
  64.7 4.7 %collective-permute-start.15 = (bf16[64,512]{1,0:T(8,128)(2,1)S(1)}, bf16[64,512]{1,0:T(8,128)(2,1)S(1)}, u32[]{:S(2)}, u32[]{:S(2)}) collective-permute-start(bf16[64,512]{1,0:T(8,128)(2,1)S(1)} %get-tuple-element.36), channel_id=1, source_target_pairs={{0,3},{1,0},{2,1},{3,2},{4,7},{5,4},{6,5},{7,6},{8,11},{9,8},{10,9... | collective-permute-start | bytes 196616 | tf_op jit(solution)/shard_map/ppermute | solution.py:39
  79.5 12.1 %collective-permute-start.16 = (bf16[64,512]{1,0:T(8,128)(2,1)S(1)}, bf16[64,512]{1,0:T(8,128)(2,1)S(1)}, u32[]{:S(2)}, u32[]{:S(2)}) collective-permute-start(bf16[64,512]{1,0:T(8,128)(2,1)S(1)} %add_convert_fusion.3), channel_id=1, source_target_pairs={{0,4},{1,5},{2,6},{3,7},{4,0},{5,1},{6,2},{7,3},{8,12},{9,13},{10,... | collective-permute-start | bytes 196616 | tf_op jit(solution)/shard_map/ppermute | solution.py:39
  95.8 5.1 %collective-permute-done.17 = bf16[64,512]{1,0:T(8,128)(2,1)S(1)} collective-permute-done((bf16[64,512]{1,0:T(8,128)(2,1)S(1)}, bf16[64,512]{1,0:T(8,128)(2,1)S(1)}, u32[]{:S(2)}, u32[]{:S(2)}) %collective-permute-start.17) | collective-permute-done | bytes 65568 | tf_op jit(solution)/shard_map/ppermute | solution.py:39
  100.9 11.2 %collective-permute-start.18 = (bf16[64,512]{1,0:T(8,128)(2,1)S(1)}, bf16[64,512]{1,0:T(8,128)(2,1)S(1)}, u32[]{:S(2)}, u32[]{:S(2)}) collective-permute-start(bf16[64,512]{1,0:T(8,128)(2,1)S(1)} %add_convert_fusion.1), channel_id=1, source_target_pairs={{0,16},{1,17},{2,18},{3,19},{4,20},{5,21},{6,22},{7,23},{8,24},{9,... | collective-permute-start | bytes 196616 | tf_op jit(solution)/shard_map/ppermute | solution.py:39
  114.1 4.6 %collective-permute-start.7 = (bf16[256,512]{1,0:T(8,128)(2,1)S(1)}, bf16[256,512]{1,0:T(8,128)(2,1)S(1)}, u32[]{:S(2)}, u32[]{:S(2)}) collective-permute-start(bf16[256,512]{1,0:T(8,128)(2,1)S(1)} %copy-done), channel_id=1, source_target_pairs={{0,8},{1,9},{2,10},{3,11},{4,12},{5,13},{6,14},{7,15},{8,0},{9,1},... | collective-permute-start | bytes 786440 | tf_op jit(solution)/shard_map/ppermute | solution.py:39
  131.0 3.5 %collective-permute-start.20 = (bf16[64,512]{1,0:T(8,128)(2,1)S(1)}, bf16[64,512]{1,0:T(8,128)(2,1)S(1)}, u32[]{:S(2)}, u32[]{:S(2)}) collective-permute-start(bf16[64,512]{1,0:T(8,128)(2,1)S(1)} %add_convert_fusion.st0), channel_id=1, source_target_pairs={{0,2},{1,3},{2,0},{3,1},{4,6},{5,7},{6,4},{7,5},{8,10},{9,11},{10,... | collective-permute-start | bytes 196616 | tf_op jit(solution)/shard_map/ppermute | solution.py:39
  134.5 10.6 %collective-permute-done.8.far2 = bf16[256,512]{1,0:T(8,128)(2,1)S(1)} collective-permute-done((bf16[256,512]{1,0:T(8,128)(2,1)S(1)}, bf16[256,512]{1,0:T(8,128)(2,1)S(1)}, u32[]{:S(2)}, u32[]{:S(2)}) %collective-permute-start.8) | collective-permute-done | bytes 262176 | tf_op jit(solution)/shard_map/ppermute | solution.py:39
  147.4 3.9 %collective-permute-done.21.st3 = bf16[64,512]{1,0:T(8,128)(2,1)S(1)} collective-permute-done((bf16[64,512]{1,0:T(8,128)(2,1)S(1)}, bf16[64,512]{1,0:T(8,128)(2,1)S(1)}, u32[]{:S(2)}, u32[]{:S(2)}) %collective-permute-start.21) | collective-permute-done | bytes 65568 | tf_op jit(solution)/shard_map/ppermute | solution.py:39
  160.9 3.7 %collective-permute-start.28 = (bf16[2,3,32,512]{3,2,1,0:T(8,128)(2,1)S(1)}, bf16[2,3,32,512]{3,2,1,0:T(8,128)(2,1)S(1)}, u32[]{:S(2)}, u32[]{:S(2)}) collective-permute-start(bf16[2,3,32,512]{3,2,1,0:T(8,128)(2,1)S(1)} %get-tuple-element.44), channel_id=1, source_target_pairs={{0,128},{32,160},{64,192},{96,224},{128,256},{160,288},{192,320},{... | collective-permute-start | bytes 589832 | tf_op jit(solution)/shard_map/ppermute | solution.py:35
  164.7 4.9 %collective-permute-start.29 = (bf16[2,3,32,512]{3,2,1,0:T(8,128)(2,1)S(1)}, bf16[2,3,32,512]{3,2,1,0:T(8,128)(2,1)S(1)}, u32[]{:S(2)}, u32[]{:S(2)}) collective-permute-start(bf16[2,3,32,512]{3,2,1,0:T(8,128)(2,1)S(1)} %get-tuple-element.45), channel_id=1, source_target_pairs={{0,256},{32,288},{64,320},{96,352},{128,384},{160,416},{192,448},{... | collective-permute-start | bytes 589832 | tf_op jit(solution)/shard_map/ppermute | solution.py:35
  176.2 3.6 %collective-permute-start.34 = (bf16[2,4,32,512]{3,2,1,0:T(8,128)(2,1)S(1)}, bf16[2,4,32,512]{3,2,1,0:T(8,128)(2,1)S(1)}, u32[]{:S(2)}, u32[]{:S(2)}) collective-permute-start(bf16[2,4,32,512]{3,2,1,0:T(8,128)(2,1)S(1)} %get-tuple-element.53), channel_id=1, source_target_pairs={{0,256},{32,288},{64,320},{96,352},{128,384},{160,416},{192,448},{... | collective-permute-start | bytes 786440 | tf_op jit(solution)/shard_map/ppermute | solution.py:35
  182.8 8.7 %collective-permute-start.31 = (bf16[3,32,512]{2,1,0:T(8,128)(2,1)S(1)}, bf16[3,32,512]{2,1,0:T(8,128)(2,1)S(1)}, u32[]{:S(2)}, u32[]{:S(2)}) collective-permute-start(bf16[3,32,512]{2,1,0:T(8,128)(2,1)S(1)} %get-tuple-element.48), channel_id=1, source_target_pairs={{0,64},{32,96},{64,0},{96,32},{128,192},{160,224},{192,128},{224,1... | collective-permute-start | bytes 294920 | tf_op jit(solution)/shard_map/ppermute | solution.py:35
  193.4 8.7 %collective-permute-start.36 = (bf16[4,32,512]{2,1,0:T(8,128)(2,1)S(1)}, bf16[4,32,512]{2,1,0:T(8,128)(2,1)S(1)}, u32[]{:S(2)}, u32[]{:S(2)}) collective-permute-start(bf16[4,32,512]{2,1,0:T(8,128)(2,1)S(1)} %get-tuple-element.56), channel_id=1, source_target_pairs={{0,64},{32,96},{64,0},{96,32},{128,192},{160,224},{192,128},{224,1... | collective-permute-start | bytes 393224 | tf_op jit(solution)/shard_map/ppermute | solution.py:35
  202.4 14.6 %collective-permute-done.36 = bf16[4,32,512]{2,1,0:T(8,128)(2,1)S(1)} collective-permute-done((bf16[4,32,512]{2,1,0:T(8,128)(2,1)S(1)}, bf16[4,32,512]{2,1,0:T(8,128)(2,1)S(1)}, u32[]{:S(2)}, u32[]{:S(2)}) %collective-permute-start.36) | collective-permute-done | bytes 131104 | tf_op jit(solution)/shard_map/ppermute | solution.py:35
  223.3 4.6 %collective-permute-start.23 = (bf16[256,512]{1,0:T(8,128)(2,1)S(1)}, bf16[256,512]{1,0:T(8,128)(2,1)S(1)}, u32[]{:S(2)}, u32[]{:S(2)}) collective-permute-start(bf16[256,512]{1,0:T(8,128)(2,1)S(1)} %get-tuple-element.60), channel_id=1, source_target_pairs={{0,2},{1,3},{2,0},{3,1},{4,6},{5,7},{6,4},{7,5},{8,10},{9,11},{10,... | collective-permute-start | bytes 786440 | tf_op jit(solution)/shard_map/ppermute | solution.py:39
  229.8 5.9 %collective-permute-start.25 = (bf16[256,512]{1,0:T(8,128)(2,1)S(1)}, bf16[256,512]{1,0:T(8,128)(2,1)S(1)}, u32[]{:S(2)}, u32[]{:S(2)}) collective-permute-start(bf16[256,512]{1,0:T(8,128)(2,1)S(1)} %get-tuple-element.58), channel_id=1, source_target_pairs={{0,8},{1,9},{2,10},{3,11},{4,12},{5,13},{6,14},{7,15},{8,0},{9,1},... | collective-permute-start | bytes 786440 | tf_op jit(solution)/shard_map/ppermute | solution.py:39
  242.0 5.7 %collective-permute-done.25.z3 = bf16[256,512]{1,0:T(8,128)(2,1)S(1)} collective-permute-done((bf16[256,512]{1,0:T(8,128)(2,1)S(1)}, bf16[256,512]{1,0:T(8,128)(2,1)S(1)}, u32[]{:S(2)}, u32[]{:S(2)}) %collective-permute-start.25) | collective-permute-done | bytes 262176 | tf_op jit(solution)/shard_map/ppermute | solution.py:39
  247.7 17.4 %collective-permute-done.26.z4 = bf16[256,512]{1,0:T(8,128)(2,1)S(1)} collective-permute-done((bf16[256,512]{1,0:T(8,128)(2,1)S(1)}, bf16[256,512]{1,0:T(8,128)(2,1)S(1)}, u32[]{:S(2)}, u32[]{:S(2)}) %collective-permute-start.26) | collective-permute-done | bytes 262176 | tf_op jit(solution)/shard_map/ppermute | solution.py:39
  (91 shorter events, 84.5 us)
Async XLA Ops:
  7.2 209.9 %all-gather.2.cloned.1.call-start = ((), (), s32[]{:S(2)}) async-start(), calls=%async_computation | async-start | bytes 4718592 | tf_op jit(solution)/shard_map/all_gather | solution.py:173
  7.2 28.8 %collective-permute-start = (bf16[6,32,512]{2,1,0:T(8,128)(2,1)}, bf16[6,32,512]{2,1,0:T(8,128)(2,1)S(1)}, u32[]{:S(2)}, u32[]{:S(2)}) collective-permute-start(bf16[6,32,512]{2,1,0:T(8,128)(2,1)} %param.7), channel_id=1, source_target_pairs={{0,64},{32,96},{64,0},{96,32},{128,192},{160,224},{192,128},{224,1... | collective-permute-start | bytes 589832 | tf_op jit(solution)/shard_map/ppermute | solution.py:35
  23.7 24.0 %collective-permute-start.9 = (bf16[32,512]{1,0:T(8,128)(2,1)S(1)}, bf16[32,512]{1,0:T(8,128)(2,1)S(1)}, u32[]{:S(2)}, u32[]{:S(2)}) collective-permute-start(bf16[32,512]{1,0:T(8,128)(2,1)S(1)} %get-tuple-element.69), channel_id=1, source_target_pairs={{0,64},{32,96},{64,0},{96,32},{128,192},{160,224},{192,128},{224,1... | collective-permute-start | bytes 98312 | tf_op jit(solution)/shard_map/ppermute | solution.py:35
  37.0 23.1 %collective-permute-start.3 = (bf16[2,6,32,512]{3,2,1,0:T(8,128)(2,1)S(1)}, bf16[2,6,32,512]{3,2,1,0:T(8,128)(2,1)S(1)}, u32[]{:S(2)}, u32[]{:S(2)}) collective-permute-start(bf16[2,6,32,512]{3,2,1,0:T(8,128)(2,1)S(1)} %get-tuple-element.63), channel_id=1, source_target_pairs={{0,384},{32,416},{64,448},{96,480},{128,0},{160,32},{192,64},{224,... | collective-permute-start | bytes 1179656 | tf_op jit(solution)/shard_map/ppermute | solution.py:35
  40.3 19.7 %collective-permute-start.2 = (bf16[2,6,32,512]{3,2,1,0:T(8,128)(2,1)S(1)}, bf16[2,6,32,512]{3,2,1,0:T(8,128)(2,1)S(1)}, u32[]{:S(2)}, u32[]{:S(2)}) collective-permute-start(bf16[2,6,32,512]{3,2,1,0:T(8,128)(2,1)S(1)} %get-tuple-element.63), channel_id=1, source_target_pairs={{0,256},{32,288},{64,320},{96,352},{128,384},{160,416},{192,448},{... | collective-permute-start | bytes 1179656 | tf_op jit(solution)/shard_map/ppermute | solution.py:35
  43.9 16.2 %collective-permute-start.1 = (bf16[2,6,32,512]{3,2,1,0:T(8,128)(2,1)S(1)}, bf16[2,6,32,512]{3,2,1,0:T(8,128)(2,1)S(1)}, u32[]{:S(2)}, u32[]{:S(2)}) collective-permute-start(bf16[2,6,32,512]{3,2,1,0:T(8,128)(2,1)S(1)} %get-tuple-element.63), channel_id=1, source_target_pairs={{0,128},{32,160},{64,192},{96,224},{128,256},{160,288},{192,320},{... | collective-permute-start | bytes 1179656 | tf_op jit(solution)/shard_map/ppermute | solution.py:35
  100.9 21.6 %collective-permute-start.18 = (bf16[64,512]{1,0:T(8,128)(2,1)S(1)}, bf16[64,512]{1,0:T(8,128)(2,1)S(1)}, u32[]{:S(2)}, u32[]{:S(2)}) collective-permute-start(bf16[64,512]{1,0:T(8,128)(2,1)S(1)} %add_convert_fusion.1), channel_id=1, source_target_pairs={{0,16},{1,17},{2,18},{3,19},{4,20},{5,21},{6,22},{7,23},{8,24},{9,... | collective-permute-start | bytes 196616 | tf_op jit(solution)/shard_map/ppermute | solution.py:39
  114.1 16.9 %collective-permute-start.7 = (bf16[256,512]{1,0:T(8,128)(2,1)S(1)}, bf16[256,512]{1,0:T(8,128)(2,1)S(1)}, u32[]{:S(2)}, u32[]{:S(2)}) collective-permute-start(bf16[256,512]{1,0:T(8,128)(2,1)S(1)} %copy-done), channel_id=1, source_target_pairs={{0,8},{1,9},{2,10},{3,11},{4,12},{5,13},{6,14},{7,15},{8,0},{9,1},... | collective-permute-start | bytes 786440 | tf_op jit(solution)/shard_map/ppermute | solution.py:39
  118.7 26.4 %collective-permute-start.8 = (bf16[256,512]{1,0:T(8,128)(2,1)S(1)}, bf16[256,512]{1,0:T(8,128)(2,1)S(1)}, u32[]{:S(2)}, u32[]{:S(2)}) collective-permute-start(bf16[256,512]{1,0:T(8,128)(2,1)S(1)} %copy-done), channel_id=1, source_target_pairs={{0,16},{1,17},{2,18},{3,19},{4,20},{5,21},{6,22},{7,23},{8,24},{9,... | collective-permute-start | bytes 786440 | tf_op jit(solution)/shard_map/ppermute | solution.py:39
  120.6 34.0 %collective-permute-start.4 = (bf16[256,512]{1,0:T(8,128)(2,1)S(1)}, bf16[256,512]{1,0:T(8,128)(2,1)S(1)}, u32[]{:S(2)}, u32[]{:S(2)}) collective-permute-start(bf16[256,512]{1,0:T(8,128)(2,1)S(1)} %copy-done), channel_id=1, source_target_pairs={{0,1},{1,0},{2,3},{3,2},{4,5},{5,4},{6,7},{7,6},{8,9},{9,8},{10,11... | collective-permute-start | bytes 786440 | tf_op jit(solution)/shard_map/ppermute | solution.py:39
  122.6 32.1 %collective-permute-start.5 = (bf16[256,512]{1,0:T(8,128)(2,1)S(1)}, bf16[256,512]{1,0:T(8,128)(2,1)S(1)}, u32[]{:S(2)}, u32[]{:S(2)}) collective-permute-start(bf16[256,512]{1,0:T(8,128)(2,1)S(1)} %copy-done), channel_id=1, source_target_pairs={{0,2},{1,3},{2,0},{3,1},{4,6},{5,7},{6,4},{7,5},{8,10},{9,11},{10,... | collective-permute-start | bytes 786440 | tf_op jit(solution)/shard_map/ppermute | solution.py:39
  126.1 21.3 %collective-permute-start.19 = (bf16[64,512]{1,0:T(8,128)(2,1)S(1)}, bf16[64,512]{1,0:T(8,128)(2,1)S(1)}, u32[]{:S(2)}, u32[]{:S(2)}) collective-permute-start(bf16[64,512]{1,0:T(8,128)(2,1)S(1)} %add_convert_fusion.st0), channel_id=1, source_target_pairs={{0,1},{1,2},{2,3},{3,0},{4,5},{5,6},{6,7},{7,4},{8,9},{9,10},{10,1... | collective-permute-start | bytes 196616 | tf_op jit(solution)/shard_map/ppermute | solution.py:39
  131.0 16.4 %collective-permute-start.20 = (bf16[64,512]{1,0:T(8,128)(2,1)S(1)}, bf16[64,512]{1,0:T(8,128)(2,1)S(1)}, u32[]{:S(2)}, u32[]{:S(2)}) collective-permute-start(bf16[64,512]{1,0:T(8,128)(2,1)S(1)} %add_convert_fusion.st0), channel_id=1, source_target_pairs={{0,2},{1,3},{2,0},{3,1},{4,6},{5,7},{6,4},{7,5},{8,10},{9,11},{10,... | collective-permute-start | bytes 196616 | tf_op jit(solution)/shard_map/ppermute | solution.py:39
  152.7 20.2 %collective-permute-start.32 = (bf16[4,2,4,32,512]{4,3,2,1,0:T(8,128)(2,1)S(1)}, bf16[4,2,4,32,512]{4,3,2,1,0:T(8,128)(2,1)S(1)}, u32[]{:S(2)}, u32[]{:S(2)}) collective-permute-start(bf16[4,2,4,32,512]{4,3,2,1,0:T(8,128)(2,1)S(1)} %get-tuple-element.50), channel_id=1, source_target_pairs={{0,32},{32,0},{64,96},{96,64},{128,160},{160,128},{192,224},{224,1... | collective-permute-start | bytes 3145736 | tf_op jit(solution)/shard_map/ppermute | solution.py:35
  160.9 18.9 %collective-permute-start.28 = (bf16[2,3,32,512]{3,2,1,0:T(8,128)(2,1)S(1)}, bf16[2,3,32,512]{3,2,1,0:T(8,128)(2,1)S(1)}, u32[]{:S(2)}, u32[]{:S(2)}) collective-permute-start(bf16[2,3,32,512]{3,2,1,0:T(8,128)(2,1)S(1)} %get-tuple-element.44), channel_id=1, source_target_pairs={{0,128},{32,160},{64,192},{96,224},{128,256},{160,288},{192,320},{... | collective-permute-start | bytes 589832 | tf_op jit(solution)/shard_map/ppermute | solution.py:35
  164.7 17.5 %collective-permute-start.29 = (bf16[2,3,32,512]{3,2,1,0:T(8,128)(2,1)S(1)}, bf16[2,3,32,512]{3,2,1,0:T(8,128)(2,1)S(1)}, u32[]{:S(2)}, u32[]{:S(2)}) collective-permute-start(bf16[2,3,32,512]{3,2,1,0:T(8,128)(2,1)S(1)} %get-tuple-element.45), channel_id=1, source_target_pairs={{0,256},{32,288},{64,320},{96,352},{128,384},{160,416},{192,448},{... | collective-permute-start | bytes 589832 | tf_op jit(solution)/shard_map/ppermute | solution.py:35
  173.7 17.8 %collective-permute-start.33 = (bf16[2,4,32,512]{3,2,1,0:T(8,128)(2,1)S(1)}, bf16[2,4,32,512]{3,2,1,0:T(8,128)(2,1)S(1)}, u32[]{:S(2)}, u32[]{:S(2)}) collective-permute-start(bf16[2,4,32,512]{3,2,1,0:T(8,128)(2,1)S(1)} %get-tuple-element.52), channel_id=1, source_target_pairs={{0,128},{32,160},{64,192},{96,224},{128,256},{160,288},{192,320},{... | collective-permute-start | bytes 786440 | tf_op jit(solution)/shard_map/ppermute | solution.py:35
  176.2 15.3 %collective-permute-start.34 = (bf16[2,4,32,512]{3,2,1,0:T(8,128)(2,1)S(1)}, bf16[2,4,32,512]{3,2,1,0:T(8,128)(2,1)S(1)}, u32[]{:S(2)}, u32[]{:S(2)}) collective-permute-start(bf16[2,4,32,512]{3,2,1,0:T(8,128)(2,1)S(1)} %get-tuple-element.53), channel_id=1, source_target_pairs={{0,256},{32,288},{64,320},{96,352},{128,384},{160,416},{192,448},{... | collective-permute-start | bytes 786440 | tf_op jit(solution)/shard_map/ppermute | solution.py:35
  182.8 19.5 %collective-permute-start.31 = (bf16[3,32,512]{2,1,0:T(8,128)(2,1)S(1)}, bf16[3,32,512]{2,1,0:T(8,128)(2,1)S(1)}, u32[]{:S(2)}, u32[]{:S(2)}) collective-permute-start(bf16[3,32,512]{2,1,0:T(8,128)(2,1)S(1)} %get-tuple-element.48), channel_id=1, source_target_pairs={{0,64},{32,96},{64,0},{96,32},{128,192},{160,224},{192,128},{224,1... | collective-permute-start | bytes 294920 | tf_op jit(solution)/shard_map/ppermute | solution.py:35
  193.4 23.7 %collective-permute-start.36 = (bf16[4,32,512]{2,1,0:T(8,128)(2,1)S(1)}, bf16[4,32,512]{2,1,0:T(8,128)(2,1)S(1)}, u32[]{:S(2)}, u32[]{:S(2)}) collective-permute-start(bf16[4,32,512]{2,1,0:T(8,128)(2,1)S(1)} %get-tuple-element.56), channel_id=1, source_target_pairs={{0,64},{32,96},{64,0},{96,32},{128,192},{160,224},{192,128},{224,1... | collective-permute-start | bytes 393224 | tf_op jit(solution)/shard_map/ppermute | solution.py:35
  221.2 19.8 %collective-permute-start.22 = (bf16[256,512]{1,0:T(8,128)(2,1)S(1)}, bf16[256,512]{1,0:T(8,128)(2,1)S(1)}, u32[]{:S(2)}, u32[]{:S(2)}) collective-permute-start(bf16[256,512]{1,0:T(8,128)(2,1)S(1)} %get-tuple-element.61), channel_id=1, source_target_pairs={{0,1},{1,0},{2,3},{3,2},{4,5},{5,4},{6,7},{7,6},{8,9},{9,8},{10,11... | collective-permute-start | bytes 786440 | tf_op jit(solution)/shard_map/ppermute | solution.py:39
  223.3 17.7 %collective-permute-start.23 = (bf16[256,512]{1,0:T(8,128)(2,1)S(1)}, bf16[256,512]{1,0:T(8,128)(2,1)S(1)}, u32[]{:S(2)}, u32[]{:S(2)}) collective-permute-start(bf16[256,512]{1,0:T(8,128)(2,1)S(1)} %get-tuple-element.60), channel_id=1, source_target_pairs={{0,2},{1,3},{2,0},{3,1},{4,6},{5,7},{6,4},{7,5},{8,10},{9,11},{10,... | collective-permute-start | bytes 786440 | tf_op jit(solution)/shard_map/ppermute | solution.py:39
  229.8 17.9 %collective-permute-start.25 = (bf16[256,512]{1,0:T(8,128)(2,1)S(1)}, bf16[256,512]{1,0:T(8,128)(2,1)S(1)}, u32[]{:S(2)}, u32[]{:S(2)}) collective-permute-start(bf16[256,512]{1,0:T(8,128)(2,1)S(1)} %get-tuple-element.58), channel_id=1, source_target_pairs={{0,8},{1,9},{2,10},{3,11},{4,12},{5,13},{6,14},{7,15},{8,0},{9,1},... | collective-permute-start | bytes 786440 | tf_op jit(solution)/shard_map/ppermute | solution.py:39
  235.7 29.3 %collective-permute-start.26 = (bf16[256,512]{1,0:T(8,128)(2,1)S(1)}, bf16[256,512]{1,0:T(8,128)(2,1)S(1)}, u32[]{:S(2)}, u32[]{:S(2)}) collective-permute-start(bf16[256,512]{1,0:T(8,128)(2,1)S(1)} %get-tuple-element.57), channel_id=1, source_target_pairs={{0,16},{1,17},{2,18},{3,19},{4,20},{5,21},{6,22},{7,23},{8,24},{9,... | collective-permute-start | bytes 786440 | tf_op jit(solution)/shard_map/ppermute | solution.py:39
  (20 other events, 175.0 us)
Sparse Core Ops, SparseCore 0:
  61.6 33.8 all-gather.1

commit v2 on v1

v2 whole, which is shorter than its diff:
```python
import functools

import jax
import jax.numpy as jnp
from jax import lax
from jax.experimental import pallas as pl
from jax.experimental.pallas import tpu as pltpu
from jax.sharding import PartitionSpec as P

BS = 512
LEVELS = 5
R = 256
SCALE = 1.0 / 64.0
F32 = jnp.float32
BF16 = jnp.bfloat16


def dp_pairs(step):
    pairs = []
    for i in range(16):
        y, h, c = step(i // 4, (i // 2) % 2, i % 2)
        pairs.append((i, (y * 2 + h) * 2 + c))
    return pairs


CORE = dp_pairs(lambda y, h, c: (y, h, 1 - c))
Z_HI = dp_pairs(lambda y, h, c: (y, 1 - h, c))
Y_GROUPS = [[(y * 2 + h) * 2 + c for y in range(4)] for h in range(2) for c in range(2)]
YC_GROUPS = [[(y * 2 + h) * 2 + c for y in range(4) for c in range(2)] for h in range(2)]
X_GROUPS = [[z * 4 + x for x in range(4)] for z in range(8)]
PARTNER = [[(i, i ^ (1 << level)) for i in range(32)] for level in range(LEVELS)]


def tie(value, *earlier):
    return lax.optimization_barrier((value, *earlier))[0]


def over_dp(value, pairs):
    return lax.ppermute(value, "dp", pairs)


def over_feat(value, pairs):
    return lax.ppermute(value, "feat", pairs)


def exchange(value, axis, groups):
    return lax.all_to_all(value, axis, 0, 0, tiled=True, axis_index_groups=groups)


def dot_nn(a, b):
    return lax.dot_general(a, b, (((1,), (0,)), ((), ())), preferred_element_type=F32)


def dot_nt(a, b):
    return lax.dot_general(a, b, (((1,), (1,)), ((), ())), preferred_element_type=F32)


def dot_tn(a, b):
    return lax.dot_general(a, b, (((0,), (0,)), ((), ())), preferred_element_type=F32)


def call(kernel, out, place, *args, scratch=(), name, limit=24):
    shapes = [jax.ShapeDtypeStruct(s, d) for s, d in out]
    return pl.pallas_call(
        kernel,
        out_shape=shapes,
        in_specs=[pl.BlockSpec(memory_space=pltpu.SMEM)]
        + [pl.BlockSpec(memory_space=pltpu.VMEM)] * len(args),
        out_specs=[pl.BlockSpec(memory_space=pltpu.VMEM)] * len(out),
        scratch_shapes=list(scratch),
        compiler_params=pltpu.CompilerParams(vmem_limit_bytes=limit << 20),
        name=name,
    )(place, *args)


def rows_of(place, y, g, c):
    h = lax.rem(place[1] + g, 2)
    return pl.multiple_of(((y * 2 + h) * 2 + c) * 32, 32)


def pair_kernel(place, mine, got, weights, low):
    weights[0] = mine[: LEVELS + 1]
    weights[1] = got[: LEVELS + 1]
    for k in range(8):
        low[k, 0] = mine[LEVELS + 1]
        low[k, 1] = got[LEVELS + 1]


def project_kernel(place, gathered, inputs, cot, low, out, part):
    for k in range(8):
        for g in range(2):
            low[pl.ds(rows_of(place, k // 2, g, k % 2), 32), :] = gathered[k, g]
    part[:, :R] = dot_nn(inputs[...], low[:, :R])
    part[:, R:] = dot_nn(cot[...], low[:, R:])
    for x in range(4):
        out[x] = part[x * 64 : (x + 1) * 64, :].astype(BF16)


def weights_kernel(place, gathered, cot, z0, z1, z2, z3, z4, w):
    for k in range(8):
        for g in range(2):
            w[:, pl.ds(rows_of(place, k // 2, g, k % 2), 32), :] = gathered[k, g]
    for level, z in enumerate((z0, z1, z2, z3, z4)):
        z[...] = dot_nt(cot[...], w[level + 1]).astype(BF16)


def x_sum_kernel(place, parts, out):
    total = parts[0].astype(F32)
    for x in range(1, 4):
        total = total + parts[x].astype(F32)
    out[...] = total.astype(BF16)


def near_grads_kernel(place, inputs, n0, n1, cot, out, grad):
    for n, left in enumerate((inputs, n0, n1)):
        grad[...] = dot_tn(left[...], cot[...])
        for k in range(8):
            for g in range(2):
                row = rows_of(place, k // 2, g, k % 2)
                out[k, g, n] = grad[pl.ds(row, 32), :].astype(BF16)


def far_grads_kernel(place, n2, n3, n4, st, inputs, cot, keep, send, grad):
    for n, left in enumerate((n2, n3, n4, None)):
        if left is None:
            grad[:, :R] = dot_tn(inputs[...], st[:, R:])
            grad[:, R:] = dot_tn(cot[...], st[:, :R])
        else:
            grad[...] = dot_tn(left[...], cot[...])
        for y in range(4):
            for g in range(2):
                row = rows_of(place, y, g, place[2])
                keep[y, g, n] = grad[pl.ds(row, 32), :].astype(BF16)
                row = rows_of(place, y, g, 1 - place[2])
                send[y, g, n] = grad[pl.ds(row, 32), :].astype(BF16)


def core_sum_kernel(place, keep, got, out):
    out[...] = (keep[...].astype(F32) + got[...].astype(F32)).astype(BF16)


def group_sum_kernel(place, near, far, mine, send):
    total = far[0].astype(F32)
    for y in range(1, 4):
        total = total + far[y].astype(F32)
    mine[:3] = near[0].astype(F32)
    mine[3:] = total[0]
    send[:3] = near[1]
    send[3:] = total[1].astype(BF16)


def output_kernel(place, inputs, n0, n1, n2, n3, n4, w, st, low, out):
    total = dot_nt(st[:, :R], low[:, R:])
    for n, left in enumerate((inputs, n0, n1, n2, n3, n4)):
        total = total + dot_nn(left[...], w[n])
    out[...] = total.astype(BF16)


def grad_inputs_kernel(place, cot, w, z0, z1, z2, z3, z4, st, low, out):
    total = dot_nt(cot[...], w[0]) + dot_nt(st[:, R:], low[:, :R])
    for z in (z0, z1, z2, z3, z4):
        total = total + z[...].astype(F32)
    out[...] = total.astype(BF16)


def body(inputs, cotangent, butterfly, low_in, low_out):
    dp = lax.axis_index("dp")
    place = jnp.stack([dp // 4, (dp // 2) % 2, dp % 2, lax.axis_index("feat") % 4]).astype(jnp.int32)
    block = (256, BS)
    levels = LEVELS + 1

    shard = jnp.concatenate(
        [butterfly, jnp.concatenate([low_in, low_out.T], axis=1)[None]], axis=0
    )
    got = over_dp(shard, Z_HI)
    near = [over_feat(inputs, PARTNER[l]) for l in range(2)]
    (near_parts,) = call(
        near_grads_kernel, [((8, 2, 3, 32, BS), BF16)], place, inputs, *near, cotangent,
        scratch=[pltpu.VMEM((BS, BS), F32)], name="near_grads",
    )
    got = tie(got, near_parts)
    weights, low_pair = call(
        pair_kernel, [((2, levels, 32, BS), BF16), ((8, 2, 32, 2 * R), BF16)], place, shard, got,
        name="pair",
    )
    gathered = lax.all_gather(weights, "dp", axis_index_groups=YC_GROUPS)
    low_rows = exchange(low_pair, "dp", YC_GROUPS)
    z_inputs = tie(inputs, got)
    near += [over_feat(z_inputs, PARTNER[l]) for l in range(2, LEVELS)]
    low_rows = tie(low_rows, near[2])

    low, parts = call(
        project_kernel, [((BS, 2 * R), BF16), ((4, 64, 2 * R), BF16)],
        place, low_rows, inputs, cotangent,
        scratch=[pltpu.VMEM((256, 2 * R), F32)], name="project",
    )
    parts = tie(exchange(parts, "feat", X_GROUPS), near[3])
    (total,) = call(x_sum_kernel, [((64, 2 * R), BF16)], place, parts, name="x_sum")
    for level in (2, 3, 4):
        total = (total.astype(F32) + over_feat(total, PARTNER[level]).astype(F32)).astype(BF16)
    st = exchange(jnp.broadcast_to(total, (4, 64, 2 * R)), "feat", X_GROUPS)
    st = st.reshape(256, 2 * R)

    gathered = tie(gathered, total)
    near_parts = tie(near_parts, gathered)
    near_sum = lax.psum_scatter(near_parts, "dp", axis_index_groups=YC_GROUPS)
    *z, w = call(
        weights_kernel, [(block, BF16)] * LEVELS + [((levels, BS, BS), BF16)],
        place, gathered, cotangent, name="weights",
    )
    st = tie(st, w)
    z = [over_feat(z[l], PARTNER[l]) for l in reversed(range(LEVELS))][::-1]

    half = (4, 2, 4, 32, BS)
    keep, send = call(
        far_grads_kernel, [(half, BF16)] * 2, place, *near[2:], st, inputs, cotangent,
        scratch=[pltpu.VMEM((BS, BS), F32)], name="far_grads",
    )
    got = over_dp(send, CORE)
    (parts,) = call(core_sum_kernel, [(half, BF16)], place, keep, got, name="far_grads_core")
    w = tie(w, parts)
    (output,) = call(
        output_kernel, [(block, BF16)], place, inputs, *near, w, st, low, name="output"
    )
    parts = exchange(parts, "dp", Y_GROUPS)
    piece = (levels + 1, 32, BS)
    mine, send = call(
        group_sum_kernel, [(piece, F32), (piece, BF16)], place, near_sum, parts, name="grads_sum"
    )
    grads = (mine + over_dp(send, Z_HI).astype(F32)) * SCALE
    (grad_inputs,) = call(
        grad_inputs_kernel, [(block, BF16)], place, cotangent, w, *z, tie(st, send), low,
        name="grad_inputs",
    )
    return output, grad_inputs, grads[:levels], grads[levels, :, :R], grads[levels, :, R:].T


def solution(mesh):
    specs = (
        P("dp", "feat"),
        P("dp", "feat"),
        P(None, ("feat", "dp"), None),
        P(("feat", "dp"), None),
        P(None, ("feat", "dp")),
    )
    return jax.shard_map(body, mesh=mesh, in_specs=specs, out_specs=specs, check_vma=False)
```

time: 275 us -> 222 us (0.81)
  starting transfers between devices: 155 us -> 109 us
  waiting for transfers between devices: 83.3 us -> 57.5 us
  local copies, waits for them, and re-layouts: 2.7 us -> 18.7 us
  Pallas kernels: 11.9 us -> 18.8 us
    ppermute x18 -> x3, starting transfers between devices: 79.8 us -> 27.5 us  [over_dp(): return lax.ppermute(value, 'dp', pairs)]
    ppermute x18 -> x3, waiting for transfers between devices: 31.1 us -> 3.55 us  [over_dp(): return lax.ppermute(value, 'dp', pairs)]
    all_to_all x0 -> x4, starting transfers between devices: none -> 17.7 us  [exchange(): lax.all_to_all(value, axis, 0, 0, tiled=True, axis_index_groups=groups)]
    unnamed x10 -> x44, local copies, waits for them, and re-layouts: 1.98 us -> 16.6 us
    ppermute x19 -> x13, starting transfers between devices: 74.7 us -> 64.1 us  [over_feat(): return lax.ppermute(value, 'feat', pairs)]
    pallas_call x10, Pallas kernels: 11.9 us -> 18.8 us  [call(): pl.pallas_call(kernel, out_shape=shapes, in_specs=[pl.BlockSpec(memory_sp...]
    all_to_all x0 -> x4, waiting for transfers between devices: none -> 4.1 us  [exchange(): lax.all_to_all(value, axis, 0, 0, tiled=True, axis_index_groups=groups)]
    another operation x5 -> x0, other arithmetic: 3.13 us -> none  [the longest x4 2.38 us: gather_rows(): jnp.stack(steps)]
  transfers between devices with their start and end apart: 38 -> 22, of which waited for: 17 -> 11; matrix products, arithmetic and copies ran while one was open for 1% -> 1% of each run, Pallas kernels for 3% -> 8%
where the time goes in v2:
time: 222 us; the launch traced here: 221 us
  starting transfers between devices  109 us (49%)
  waiting for transfers between devices  57.5 us (26%)
  Pallas kernels  18.8 us (8%)
  local copies, waits for them, and re-layouts  18.7 us (8%)
  between operations  14.4 us (6%)
    ppermute x13, starting transfers between devices, over_feat(): return lax.ppermute(value, 'feat', pairs)  64.1 us
    ppermute x13, waiting for transfers between devices, over_feat(): return lax.ppermute(value, 'feat', pairs)  49.8 us
    ppermute x3, starting transfers between devices, over_dp(): return lax.ppermute(value, 'dp', pairs)  27.5 us
    pallas_call x10, Pallas kernels, call(): pl.pallas_call(kernel, out_shape=shapes, in_specs=[pl.BlockSpec(memory_sp...  18.8 us
    all_to_all x4, starting transfers between devices, exchange(): lax.all_to_all(value, axis, 0, 0, tiled=True, axis_index_groups=groups)  17.7 us
    unnamed x44, local copies, waits for them, and re-layouts  16.6 us
  transfers between devices with their start and end apart: 22, of which 11 were waited for; matrix products, arithmetic and copies ran while one was open for 1% of the time, Pallas kernels for 8%

profile of v2, /device:TPU:8, one launch (start us, length us, event | category | flops | bytes accessed | tf_op | source)
XLA Modules:
  0.0 220.6 jit_solution(12566735991526743430)
XLA Ops:
  7.2 5.1 %collective-permute-start.1 = (bf16[256,512]{1,0:T(8,128)(2,1)}, bf16[256,512]{1,0:T(8,128)(2,1)S(1)}, u32[]{:S(2)}, u32[]{:S(2)}) collective-permute-start(bf16[256,512]{1,0:T(8,128)(2,1)} %inputs.7), channel_id=1, source_target_pairs={{0,2},{1,3},{2,0},{3,1},{4,6},{5,7},{6,4},{7,5},{8,10},{9,11},{10,... | collective-permute-start | bytes 786440 | tf_op jit(solution)/shard_map/ppermute | solution.py:43
  16.5 15.7 %collective-permute-start.2 = (bf16[7,32,512]{2,1,0:T(8,128)(2,1)S(1)}, bf16[7,32,512]{2,1,0:T(8,128)(2,1)S(1)}, u32[]{:S(2)}, u32[]{:S(2)}) collective-permute-start(bf16[7,32,512]{2,1,0:T(8,128)(2,1)S(1)} %pad_maximum_fusion.mine), channel_id=1, source_target_pairs={{0,64},{32,96},{64,0},{96,32},{128,192},{160,224},{192,128},{224,1... | collective-permute-start | bytes 688136 | tf_op jit(solution)/shard_map/ppermute | solution.py:39
  33.4 3.2 %near_grads.1 = bf16[8,2,3,32,512]{4,3,2,1,0:T(8,128)(2,1)} custom-call(s32[4]{0:T(128)S(1)} %pad_add_fusion.place, bf16[256,512]{1,0:T(8,128)(2,1)} %inputs.7, bf16[256,512]{1,0:T(8,128)(2,1)S(1)} %collective-permute-done.n0, bf16[256,512]{1,0:T(8,128)(2,1)S(1)} %collective-permute-done.1.n1, bf16[256,512]{1,0:T(8,128)(2,1)S(1)} %copy-done), custom_call_target="tpu_custom_call" | custom-call | tf_op jit(solution)/shard_map/near_grads/pallas_call | solution.py:64
  39.1 4.9 %all-to-all-start = ((bf16[8,2,32,512]{3,2,1,0:T(8,128)(2,1)}), bf16[8,2,32,512]{3,2,1,0:T(8,128)(2,1)S(1)}, u32[]{:S(2)}, u32[]{:S(2)}) async-start(bf16[8,2,32,512]{3,2,1,0:T(8,128)(2,1)} %get-tuple-element.31), calls=%async_computation | async-start | bytes 1048576 | tf_op jit(solution)/shard_map/all_to_all | solution.py:47
  44.0 17.6 %collective-permute-start.3 = (bf16[256,512]{1,0:T(8,128)(2,1)}, bf16[256,512]{1,0:T(8,128)(2,1)S(1)}, u32[]{:S(2)}, u32[]{:S(2)}) collective-permute-start(bf16[256,512]{1,0:T(8,128)(2,1)} %inputs.7), channel_id=1, source_target_pairs={{0,4},{1,5},{2,6},{3,7},{4,0},{5,1},{6,2},{7,3},{8,12},{9,13},{10,... | collective-permute-start | bytes 786440 | tf_op jit(solution)/shard_map/ppermute | solution.py:43
  63.6 5.0 %collective-permute-done.3.n2 = bf16[256,512]{1,0:T(8,128)(2,1)S(1)} collective-permute-done((bf16[256,512]{1,0:T(8,128)(2,1)}, bf16[256,512]{1,0:T(8,128)(2,1)S(1)}, u32[]{:S(2)}, u32[]{:S(2)}) %collective-permute-start.3) | collective-permute-done | bytes 262176 | tf_op jit(solution)/shard_map/ppermute | solution.py:43
  72.1 3.4 %all-to-all-start.1 = ((bf16[4,64,512]{2,1,0:T(8,128)(2,1)}), bf16[4,64,512]{2,1,0:T(8,128)(2,1)S(1)}, u32[]{:S(2)}, u32[]{:S(2)}) async-start(bf16[4,64,512]{2,1,0:T(8,128)(2,1)} %get-tuple-element.33), calls=%async_computation.1 | async-start | bytes 524288 | tf_op jit(solution)/shard_map/all_to_all | solution.py:47
  78.1 4.1 %all-to-all-done.1.parts = bf16[4,64,512]{2,1,0:T(8,128)(2,1)S(1)} async-done(((bf16[4,64,512]{2,1,0:T(8,128)(2,1)}), bf16[4,64,512]{2,1,0:T(8,128)(2,1)S(1)}, u32[]{:S(2)}, u32[]{:S(2)}) %all-to-all-start.1) | async-done | bytes 262176 | tf_op jit(solution)/shard_map/all_to_all | solution.py:47
  82.8 4.3 %collective-permute-start.6 = (bf16[64,512]{1,0:T(8,128)(2,1)S(1)}, bf16[64,512]{1,0:T(8,128)(2,1)S(1)}, u32[]{:S(2)}, u32[]{:S(2)}) collective-permute-start(bf16[64,512]{1,0:T(8,128)(2,1)S(1)} %x_sum.1), channel_id=1, source_target_pairs={{0,4},{1,5},{2,6},{3,7},{4,0},{5,1},{6,2},{7,3},{8,12},{9,13},{10,... | collective-permute-start | bytes 196616 | tf_op jit(solution)/shard_map/ppermute | solution.py:43
  91.2 5.1 %collective-permute-done.7 = bf16[64,512]{1,0:T(8,128)(2,1)S(1)} collective-permute-done((bf16[64,512]{1,0:T(8,128)(2,1)S(1)}, bf16[64,512]{1,0:T(8,128)(2,1)S(1)}, u32[]{:S(2)}, u32[]{:S(2)}) %collective-permute-start.7) | collective-permute-done | bytes 65568 | tf_op jit(solution)/shard_map/ppermute | solution.py:43
  96.4 6.3 %collective-permute-start.8 = (bf16[64,512]{1,0:T(8,128)(2,1)S(1)}, bf16[64,512]{1,0:T(8,128)(2,1)S(1)}, u32[]{:S(2)}, u32[]{:S(2)}) collective-permute-start(bf16[64,512]{1,0:T(8,128)(2,1)S(1)} %add_convert_fusion.1), channel_id=1, source_target_pairs={{0,16},{1,17},{2,18},{3,19},{4,20},{5,21},{6,22},{7,23},{8,24},{9,... | collective-permute-start | bytes 196616 | tf_op jit(solution)/shard_map/ppermute | solution.py:43
  102.7 3.8 %collective-permute-done.8 = bf16[64,512]{1,0:T(8,128)(2,1)S(1)} collective-permute-done((bf16[64,512]{1,0:T(8,128)(2,1)S(1)}, bf16[64,512]{1,0:T(8,128)(2,1)S(1)}, u32[]{:S(2)}, u32[]{:S(2)}) %collective-permute-start.8) | collective-permute-done | bytes 65568 | tf_op jit(solution)/shard_map/ppermute | solution.py:43
  106.6 6.3 %collective-permute-start.5 = (bf16[256,512]{1,0:T(8,128)(2,1)}, bf16[256,512]{1,0:T(8,128)(2,1)}, u32[]{:S(2)}, u32[]{:S(2)}) collective-permute-start(bf16[256,512]{1,0:T(8,128)(2,1)} %inputs.7), channel_id=1, source_target_pairs={{0,16},{1,17},{2,18},{3,19},{4,20},{5,21},{6,22},{7,23},{8,24},{9,... | collective-permute-start | bytes 786440 | tf_op jit(solution)/shard_map/ppermute | solution.py:43
  113.6 4.0 %all-to-all-start.2 = ((bf16[4,64,512]{2,1,0:T(8,128)(2,1)}), bf16[4,64,512]{2,1,0:T(8,128)(2,1)}, u32[]{:S(2)}, u32[]{:S(2)}) async-start(bf16[4,64,512]{2,1,0:T(8,128)(2,1)} %broadcast_in_dim.7), calls=%async_computation.2 | async-start | bytes 524288 | tf_op jit(solution)/shard_map/all_to_all | solution.py:47
  125.0 8.7 %collective-permute-done.5.n4 = bf16[256,512]{1,0:T(8,128)(2,1)} collective-permute-done((bf16[256,512]{1,0:T(8,128)(2,1)}, bf16[256,512]{1,0:T(8,128)(2,1)}, u32[]{:S(2)}, u32[]{:S(2)}) %collective-permute-start.5) | collective-permute-done | bytes 262176 | tf_op jit(solution)/shard_map/ppermute | solution.py:43
  139.6 2.6 %collective-permute-done.9.got = bf16[4,2,4,32,512]{4,3,2,1,0:T(8,128)(2,1)S(1)} collective-permute-done((bf16[4,2,4,32,512]{4,3,2,1,0:T(8,128)(2,1)S(1)}, bf16[4,2,4,32,512]{4,3,2,1,0:T(8,128)(2,1)S(1)}, u32[]{:S(2)}, u32[]{:S(2)}) %collective-permute-start.9) | collective-permute-done | bytes 1048608 | tf_op jit(solution)/shard_map/ppermute | solution.py:39
  144.0 5.3 %all-to-all-start.3 = ((bf16[4,2,4,32,512]{4,3,2,1,0:T(8,128)(2,1)}), bf16[4,2,4,32,512]{4,3,2,1,0:T(8,128)(2,1)}, u32[]{:S(2)}, u32[]{:S(2)}) async-start(bf16[4,2,4,32,512]{4,3,2,1,0:T(8,128)(2,1)} %copy-done.2), calls=%async_computation.4 | async-start | bytes 2097152 | tf_op jit(solution)/shard_map/all_to_all | solution.py:47
  149.3 2.7 %collective-permute-start.10 = (bf16[256,512]{1,0:T(8,128)(2,1)}, bf16[256,512]{1,0:T(8,128)(2,1)}, u32[]{:S(2)}, u32[]{:S(2)}) collective-permute-start(bf16[256,512]{1,0:T(8,128)(2,1)} %copy-done.21), channel_id=1, source_target_pairs={{0,1},{1,0},{2,3},{3,2},{4,5},{5,4},{6,7},{7,6},{8,9},{9,8},{10,11... | collective-permute-start | bytes 786440 | tf_op jit(solution)/shard_map/ppermute | solution.py:43
  152.0 3.7 %collective-permute-start.11 = (bf16[256,512]{1,0:T(8,128)(2,1)}, bf16[256,512]{1,0:T(8,128)(2,1)}, u32[]{:S(2)}, u32[]{:S(2)}) collective-permute-start(bf16[256,512]{1,0:T(8,128)(2,1)} %copy-done.20), channel_id=1, source_target_pairs={{0,2},{1,3},{2,0},{3,1},{4,6},{5,7},{6,4},{7,5},{8,10},{9,11},{10,... | collective-permute-start | bytes 786440 | tf_op jit(solution)/shard_map/ppermute | solution.py:43
  159.6 7.9 %collective-permute-start.14 = (bf16[256,512]{1,0:T(8,128)(2,1)}, bf16[256,512]{1,0:T(8,128)(2,1)}, u32[]{:S(2)}, u32[]{:S(2)}) collective-permute-start(bf16[256,512]{1,0:T(8,128)(2,1)} %copy-done.17), channel_id=1, source_target_pairs={{0,16},{1,17},{2,18},{3,19},{4,20},{5,21},{6,22},{7,23},{8,24},{9,... | collective-permute-start | bytes 786440 | tf_op jit(solution)/shard_map/ppermute | solution.py:43
  169.8 9.8 %collective-permute-start.15 = (bf16[7,32,512]{2,1,0:T(8,128)(2,1)S(1)}, bf16[7,32,512]{2,1,0:T(8,128)(2,1)S(1)}, u32[]{:S(2)}, u32[]{:S(2)}) collective-permute-start(bf16[7,32,512]{2,1,0:T(8,128)(2,1)S(1)} %get-tuple-element.48), channel_id=1, source_target_pairs={{0,64},{32,96},{64,0},{96,32},{128,192},{160,224},{192,128},{224,1... | collective-permute-start | bytes 688136 | tf_op jit(solution)/shard_map/ppermute | solution.py:39
  184.5 2.9 %output.1 = bf16[256,512]{1,0:T(8,128)(2,1)} custom-call(s32[4]{0:T(128)S(1)} %pad_add_fusion.place, bf16[256,512]{1,0:T(8,128)(2,1)} %inputs.7, bf16[256,512]{1,0:T(8,128)(2,1)S(1)} %copy-done.15, bf16[256,512]{1,0:T(8,128)(2,1)S(1)} %copy-done.13, bf16[256,512]{1,0:T(8,128)(2,1)S(1)} %copy-done.8, bf16[256,512]{1,0:T(8,128)(2,1)S(1)} %copy-done.11, ...), custom_call_target="tpu_custom_call" | custom-call | tf_op jit(solution)/shard_map/output/pallas_call | solution.py:64
  187.4 9.1 %collective-permute-done.13.z3 = bf16[256,512]{1,0:T(8,128)(2,1)} collective-permute-done((bf16[256,512]{1,0:T(8,128)(2,1)}, bf16[256,512]{1,0:T(8,128)(2,1)}, u32[]{:S(2)}, u32[]{:S(2)}) %collective-permute-start.13) | collective-permute-done | bytes 262176 | tf_op jit(solution)/shard_map/ppermute | solution.py:43
  196.4 13.3 %collective-permute-done.14.z4 = bf16[256,512]{1,0:T(8,128)(2,1)} collective-permute-done((bf16[256,512]{1,0:T(8,128)(2,1)}, bf16[256,512]{1,0:T(8,128)(2,1)}, u32[]{:S(2)}, u32[]{:S(2)}) %collective-permute-start.14) | collective-permute-done | bytes 262176 | tf_op jit(solution)/shard_map/ppermute | solution.py:43
  (86 shorter events, 51.3 us)
Async XLA Ops:
  7.2 62.2 %copy-start.1 = (bf16[256,512]{1,0:T(8,128)(2,1)S(1)}, bf16[256,512]{1,0:T(8,128)(2,1)}, u32[]{:S(2)}) copy-start(bf16[256,512]{1,0:T(8,128)(2,1)} %cot.9) | copy-start | bytes 786436
  7.2 99.3 %all-gather.3.cloned.1.call-start = ((), (), s32[]{:S(2)}) async-start(), calls=%async_computation.6 | async-start | bytes 3538944 | tf_op jit(solution)/shard_map/all_gather | solution.py:186
  7.2 25.1 %collective-permute-start.1 = (bf16[256,512]{1,0:T(8,128)(2,1)}, bf16[256,512]{1,0:T(8,128)(2,1)S(1)}, u32[]{:S(2)}, u32[]{:S(2)}) collective-permute-start(bf16[256,512]{1,0:T(8,128)(2,1)} %inputs.7), channel_id=1, source_target_pairs={{0,2},{1,3},{2,0},{3,1},{4,6},{5,7},{6,4},{7,5},{8,10},{9,11},{10,... | collective-permute-start | bytes 786440 | tf_op jit(solution)/shard_map/ppermute | solution.py:43
  12.3 20.1 %collective-permute-start = (bf16[256,512]{1,0:T(8,128)(2,1)}, bf16[256,512]{1,0:T(8,128)(2,1)S(1)}, u32[]{:S(2)}, u32[]{:S(2)}) collective-permute-start(bf16[256,512]{1,0:T(8,128)(2,1)} %inputs.7), channel_id=1, source_target_pairs={{0,1},{1,0},{2,3},{3,2},{4,5},{5,4},{6,7},{7,6},{8,9},{9,8},{10,11... | collective-permute-start | bytes 786440 | tf_op jit(solution)/shard_map/ppermute | solution.py:43
  16.5 21.1 %collective-permute-start.2 = (bf16[7,32,512]{2,1,0:T(8,128)(2,1)S(1)}, bf16[7,32,512]{2,1,0:T(8,128)(2,1)S(1)}, u32[]{:S(2)}, u32[]{:S(2)}) collective-permute-start(bf16[7,32,512]{2,1,0:T(8,128)(2,1)S(1)} %pad_maximum_fusion.mine), channel_id=1, source_target_pairs={{0,64},{32,96},{64,0},{96,32},{128,192},{160,224},{192,128},{224,1... | collective-permute-start | bytes 688136 | tf_op jit(solution)/shard_map/ppermute | solution.py:39
  39.1 30.2 %all-to-all-start = ((bf16[8,2,32,512]{3,2,1,0:T(8,128)(2,1)}), bf16[8,2,32,512]{3,2,1,0:T(8,128)(2,1)S(1)}, u32[]{:S(2)}, u32[]{:S(2)}) async-start(bf16[8,2,32,512]{3,2,1,0:T(8,128)(2,1)} %get-tuple-element.31), calls=%async_computation | async-start | bytes 1048576 | tf_op jit(solution)/shard_map/all_to_all | solution.py:47
  44.0 24.6 %collective-permute-start.3 = (bf16[256,512]{1,0:T(8,128)(2,1)}, bf16[256,512]{1,0:T(8,128)(2,1)S(1)}, u32[]{:S(2)}, u32[]{:S(2)}) collective-permute-start(bf16[256,512]{1,0:T(8,128)(2,1)} %inputs.7), channel_id=1, source_target_pairs={{0,4},{1,5},{2,6},{3,7},{4,0},{5,1},{6,2},{7,3},{8,12},{9,13},{10,... | collective-permute-start | bytes 786440 | tf_op jit(solution)/shard_map/ppermute | solution.py:43
  61.7 16.4 %collective-permute-start.4 = (bf16[256,512]{1,0:T(8,128)(2,1)}, bf16[256,512]{1,0:T(8,128)(2,1)S(1)}, u32[]{:S(2)}, u32[]{:S(2)}) collective-permute-start(bf16[256,512]{1,0:T(8,128)(2,1)} %inputs.7), channel_id=1, source_target_pairs={{0,8},{1,9},{2,10},{3,11},{4,12},{5,13},{6,14},{7,15},{8,0},{9,1},... | collective-permute-start | bytes 786440 | tf_op jit(solution)/shard_map/ppermute | solution.py:43
  72.1 10.1 %all-to-all-start.1 = ((bf16[4,64,512]{2,1,0:T(8,128)(2,1)}), bf16[4,64,512]{2,1,0:T(8,128)(2,1)S(1)}, u32[]{:S(2)}, u32[]{:S(2)}) async-start(bf16[4,64,512]{2,1,0:T(8,128)(2,1)} %get-tuple-element.33), calls=%async_computation.1 | async-start | bytes 524288 | tf_op jit(solution)/shard_map/all_to_all | solution.py:47
  75.5 92.0 %reduce-scatter.2.cloned.1.call-start = ((), (), s32[]{:S(2)}) async-start(), calls=%async_computation.5 | async-start | bytes 1769472 | tf_op jit(solution)/shard_map/reduce_scatter | solution.py:206
  78.1 35.5 %copy-start.9 = (bf16[256,512]{1,0:T(8,128)(2,1)}, bf16[256,512]{1,0:T(8,128)(2,1)S(1)}, u32[]{:S(2)}) copy-start(bf16[256,512]{1,0:T(8,128)(2,1)S(1)} %collective-permute-done.4.n3) | copy-start | bytes 786436
  82.8 6.5 %collective-permute-start.6 = (bf16[64,512]{1,0:T(8,128)(2,1)S(1)}, bf16[64,512]{1,0:T(8,128)(2,1)S(1)}, u32[]{:S(2)}, u32[]{:S(2)}) collective-permute-start(bf16[64,512]{1,0:T(8,128)(2,1)S(1)} %x_sum.1), channel_id=1, source_target_pairs={{0,4},{1,5},{2,6},{3,7},{4,0},{5,1},{6,2},{7,3},{8,12},{9,13},{10,... | collective-permute-start | bytes 196616 | tf_op jit(solution)/shard_map/ppermute | solution.py:43
  89.3 7.1 %collective-permute-start.7 = (bf16[64,512]{1,0:T(8,128)(2,1)S(1)}, bf16[64,512]{1,0:T(8,128)(2,1)S(1)}, u32[]{:S(2)}, u32[]{:S(2)}) collective-permute-start(bf16[64,512]{1,0:T(8,128)(2,1)S(1)} %add_convert_fusion.2), channel_id=1, source_target_pairs={{0,8},{1,9},{2,10},{3,11},{4,12},{5,13},{6,14},{7,15},{8,0},{9,1},... | collective-permute-start | bytes 196616 | tf_op jit(solution)/shard_map/ppermute | solution.py:43
  96.4 10.1 %collective-permute-start.8 = (bf16[64,512]{1,0:T(8,128)(2,1)S(1)}, bf16[64,512]{1,0:T(8,128)(2,1)S(1)}, u32[]{:S(2)}, u32[]{:S(2)}) collective-permute-start(bf16[64,512]{1,0:T(8,128)(2,1)S(1)} %add_convert_fusion.1), channel_id=1, source_target_pairs={{0,16},{1,17},{2,18},{3,19},{4,20},{5,21},{6,22},{7,23},{8,24},{9,... | collective-permute-start | bytes 196616 | tf_op jit(solution)/shard_map/ppermute | solution.py:43
  106.6 27.1 %collective-permute-start.5 = (bf16[256,512]{1,0:T(8,128)(2,1)}, bf16[256,512]{1,0:T(8,128)(2,1)}, u32[]{:S(2)}, u32[]{:S(2)}) collective-permute-start(bf16[256,512]{1,0:T(8,128)(2,1)} %inputs.7), channel_id=1, source_target_pairs={{0,16},{1,17},{2,18},{3,19},{4,20},{5,21},{6,22},{7,23},{8,24},{9,... | collective-permute-start | bytes 786440 | tf_op jit(solution)/shard_map/ppermute | solution.py:43
  113.6 11.4 %all-to-all-start.2 = ((bf16[4,64,512]{2,1,0:T(8,128)(2,1)}), bf16[4,64,512]{2,1,0:T(8,128)(2,1)}, u32[]{:S(2)}, u32[]{:S(2)}) async-start(bf16[4,64,512]{2,1,0:T(8,128)(2,1)} %broadcast_in_dim.7), calls=%async_computation.2 | async-start | bytes 524288 | tf_op jit(solution)/shard_map/all_to_all | solution.py:47
  137.7 4.6 %collective-permute-start.9 = (bf16[4,2,4,32,512]{4,3,2,1,0:T(8,128)(2,1)S(1)}, bf16[4,2,4,32,512]{4,3,2,1,0:T(8,128)(2,1)S(1)}, u32[]{:S(2)}, u32[]{:S(2)}) collective-permute-start(bf16[4,2,4,32,512]{4,3,2,1,0:T(8,128)(2,1)S(1)} %get-tuple-element.39), channel_id=1, source_target_pairs={{0,32},{32,0},{64,96},{96,64},{128,160},{160,128},{192,224},{224,1... | collective-permute-start | bytes 3145736 | tf_op jit(solution)/shard_map/ppermute | solution.py:39
  144.0 23.5 %all-to-all-start.3 = ((bf16[4,2,4,32,512]{4,3,2,1,0:T(8,128)(2,1)}), bf16[4,2,4,32,512]{4,3,2,1,0:T(8,128)(2,1)}, u32[]{:S(2)}, u32[]{:S(2)}) async-start(bf16[4,2,4,32,512]{4,3,2,1,0:T(8,128)(2,1)} %copy-done.2), calls=%async_computation.4 | async-start | bytes 2097152 | tf_op jit(solution)/shard_map/all_to_all | solution.py:47
  149.3 20.5 %collective-permute-start.10 = (bf16[256,512]{1,0:T(8,128)(2,1)}, bf16[256,512]{1,0:T(8,128)(2,1)}, u32[]{:S(2)}, u32[]{:S(2)}) collective-permute-start(bf16[256,512]{1,0:T(8,128)(2,1)} %copy-done.21), channel_id=1, source_target_pairs={{0,1},{1,0},{2,3},{3,2},{4,5},{5,4},{6,7},{7,6},{8,9},{9,8},{10,11... | collective-permute-start | bytes 786440 | tf_op jit(solution)/shard_map/ppermute | solution.py:43
  152.0 35.3 %collective-permute-start.11 = (bf16[256,512]{1,0:T(8,128)(2,1)}, bf16[256,512]{1,0:T(8,128)(2,1)}, u32[]{:S(2)}, u32[]{:S(2)}) collective-permute-start(bf16[256,512]{1,0:T(8,128)(2,1)} %copy-done.20), channel_id=1, source_target_pairs={{0,2},{1,3},{2,0},{3,1},{4,6},{5,7},{6,4},{7,5},{8,10},{9,11},{10,... | collective-permute-start | bytes 786440 | tf_op jit(solution)/shard_map/ppermute | solution.py:43
  155.7 31.7 %collective-permute-start.12 = (bf16[256,512]{1,0:T(8,128)(2,1)}, bf16[256,512]{1,0:T(8,128)(2,1)}, u32[]{:S(2)}, u32[]{:S(2)}) collective-permute-start(bf16[256,512]{1,0:T(8,128)(2,1)} %copy-done.19), channel_id=1, source_target_pairs={{0,4},{1,5},{2,6},{3,7},{4,0},{5,1},{6,2},{7,3},{8,12},{9,13},{10,... | collective-permute-start | bytes 786440 | tf_op jit(solution)/shard_map/ppermute | solution.py:43
  157.6 38.8 %collective-permute-start.13 = (bf16[256,512]{1,0:T(8,128)(2,1)}, bf16[256,512]{1,0:T(8,128)(2,1)}, u32[]{:S(2)}, u32[]{:S(2)}) collective-permute-start(bf16[256,512]{1,0:T(8,128)(2,1)} %copy-done.18), channel_id=1, source_target_pairs={{0,8},{1,9},{2,10},{3,11},{4,12},{5,13},{6,14},{7,15},{8,0},{9,1},... | collective-permute-start | bytes 786440 | tf_op jit(solution)/shard_map/ppermute | solution.py:43
  159.6 50.2 %collective-permute-start.14 = (bf16[256,512]{1,0:T(8,128)(2,1)}, bf16[256,512]{1,0:T(8,128)(2,1)}, u32[]{:S(2)}, u32[]{:S(2)}) collective-permute-start(bf16[256,512]{1,0:T(8,128)(2,1)} %copy-done.17), channel_id=1, source_target_pairs={{0,16},{1,17},{2,18},{3,19},{4,20},{5,21},{6,22},{7,23},{8,24},{9,... | collective-permute-start | bytes 786440 | tf_op jit(solution)/shard_map/ppermute | solution.py:43
  169.8 42.5 %collective-permute-start.15 = (bf16[7,32,512]{2,1,0:T(8,128)(2,1)S(1)}, bf16[7,32,512]{2,1,0:T(8,128)(2,1)S(1)}, u32[]{:S(2)}, u32[]{:S(2)}) collective-permute-start(bf16[7,32,512]{2,1,0:T(8,128)(2,1)S(1)} %get-tuple-element.48), channel_id=1, source_target_pairs={{0,64},{32,96},{64,0},{96,32},{128,192},{160,224},{192,128},{224,1... | collective-permute-start | bytes 688136 | tf_op jit(solution)/shard_map/ppermute | solution.py:39
  (20 other events, 29.0 us)
Sparse Core Ops, SparseCore 0:
  39.2 48.4 all-gather.2
  106.7 37.1 reduce-scatter.1

commit v3 on v2

--- a/solution.py
+++ b/solution.py
@@ -23,9 +23,7 @@
     return pairs
 
 
-CORE = dp_pairs(lambda y, h, c: (y, h, 1 - c))
 Z_HI = dp_pairs(lambda y, h, c: (y, 1 - h, c))
-Y_GROUPS = [[(y * 2 + h) * 2 + c for y in range(4)] for h in range(2) for c in range(2)]
 YC_GROUPS = [[(y * 2 + h) * 2 + c for y in range(4) for c in range(2)] for h in range(2)]
 X_GROUPS = [[z * 4 + x for x in range(4)] for z in range(8)]
 PARTNER = [[(i, i ^ (1 << level)) for i in range(32)] for level in range(LEVELS)]
@@ -86,17 +84,21 @@
         low[k, 1] = got[LEVELS + 1]
 
 
-def project_kernel(place, gathered, inputs, cot, low, out, part):
+def order_low(place, gathered, low):
     for k in range(8):
         for g in range(2):
             low[pl.ds(rows_of(place, k // 2, g, k % 2), 32), :] = gathered[k, g]
+
+
+def project_kernel(place, gathered, inputs, cot, out, low, part):
+    order_low(place, gathered, low)
     part[:, :R] = dot_nn(inputs[...], low[:, :R])
     part[:, R:] = dot_nn(cot[...], low[:, R:])
     for x in range(4):
         out[x] = part[x * 64 : (x + 1) * 64, :].astype(BF16)
 
 
-def weights_kernel(place, gathered, cot, z0, z1, z2, z3, z4, w):
+def weights_kernel(place, gathered, cot, z4, z3, z2, z1, z0, w):
     for k in range(8):
         for g in range(2):
             w[:, pl.ds(rows_of(place, k // 2, g, k % 2), 32), :] = gathered[k, g]
@@ -111,8 +113,8 @@
     out[...] = total.astype(BF16)
 
 
-def near_grads_kernel(place, inputs, n0, n1, cot, out, grad):
-    for n, left in enumerate((inputs, n0, n1)):
+def near_grads_kernel(place, inputs, n0, n1, n2, cot, out, grad):
+    for n, left in enumerate((inputs, n0, n1, n2)):
         grad[...] = dot_tn(left[...], cot[...])
         for k in range(8):
             for g in range(2):
@@ -120,45 +122,41 @@
                 out[k, g, n] = grad[pl.ds(row, 32), :].astype(BF16)
 
 
-def far_grads_kernel(place, n2, n3, n4, st, inputs, cot, keep, send, grad):
-    for n, left in enumerate((n2, n3, n4, None)):
+def far_grads_kernel(place, n3, n4, st, inputs, cot, out, grad):
+    for n, left in enumerate((n3, n4, None)):
         if left is None:
             grad[:, :R] = dot_tn(inputs[...], st[:, R:])
             grad[:, R:] = dot_tn(cot[...], st[:, :R])
         else:
             grad[...] = dot_tn(left[...], cot[...])
-        for y in range(4):
+        for k in range(8):
             for g in range(2):
-                row = rows_of(place, y, g, place[2])
-                keep[y, g, n] = grad[pl.ds(row, 32), :].astype(BF16)
-                row = rows_of(place, y, g, 1 - place[2])
-                send[y, g, n] = grad[pl.ds(row, 32), :].astype(BF16)
-
-
-def core_sum_kernel(place, keep, got, out):
-    out[...] = (keep[...].astype(F32) + got[...].astype(F32)).astype(BF16)
+                row = rows_of(place, k // 2, g, k % 2)
+                out[k, g, n] = grad[pl.ds(row, 32), :].astype(BF16)
 
 
 def group_sum_kernel(place, near, far, mine, send):
     total = far[0].astype(F32)
-    for y in range(1, 4):
-        total = total + far[y].astype(F32)
-    mine[:3] = near[0].astype(F32)
-    mine[3:] = total[0]
-    send[:3] = near[1]
-    send[3:] = total[1].astype(BF16)
-
-
-def output_kernel(place, inputs, n0, n1, n2, n3, n4, w, st, low, out):
+    for k in range(1, 8):
+        total = total + far[k].astype(F32)
+    mine[:4] = near[0].astype(F32)
+    mine[4:] = total[0]
+    send[:4] = near[1]
+    send[4:] = total[1].astype(BF16)
+
+
+def output_kernel(place, inputs, n0, n1, n2, n3, n4, w, st, gathered, out, low):
+    order_low(place, gathered, low)
     total = dot_nt(st[:, :R], low[:, R:])
     for n, left in enumerate((inputs, n0, n1, n2, n3, n4)):
         total = total + dot_nn(left[...], w[n])
     out[...] = total.astype(BF16)
 
 
-def grad_inputs_kernel(place, cot, w, z0, z1, z2, z3, z4, st, low, out):
+def grad_inputs_kernel(place, cot, w, z4, z3, z2, z1, z0, st, gathered, out, low):
+    order_low(place, gathered, low)
     total = dot_nt(cot[...], w[0]) + dot_nt(st[:, R:], low[:, :R])
-    for z in (z0, z1, z2, z3, z4):
+    for z in (z4, z3, z2, z1, z0):
         total = total + z[...].astype(F32)
     out[...] = total.astype(BF16)
 
@@ -173,9 +171,9 @@
         [butterfly, jnp.concatenate([low_in, low_out.T], axis=1)[None]], axis=0
     )
     got = over_dp(shard, Z_HI)
-    near = [over_feat(inputs, PARTNER[l]) for l in range(2)]
+    near = [over_feat(inputs, PARTNER[l]) for l in range(3)]
     (near_parts,) = call(
-        near_grads_kernel, [((8, 2, 3, 32, BS), BF16)], place, inputs, *near, cotangent,
+        near_grads_kernel, [((8, 2, 4, 32, BS), BF16)], place, inputs, *near, cotangent,
         scratch=[pltpu.VMEM((BS, BS), F32)], name="near_grads",
     )
     got = tie(got, near_parts)
@@ -186,51 +184,48 @@
     gathered = lax.all_gather(weights, "dp", axis_index_groups=YC_GROUPS)
     low_rows = exchange(low_pair, "dp", YC_GROUPS)
     z_inputs = tie(inputs, got)
-    near += [over_feat(z_inputs, PARTNER[l]) for l in range(2, LEVELS)]
-    low_rows = tie(low_rows, near[2])
-
-    low, parts = call(
-        project_kernel, [((BS, 2 * R), BF16), ((4, 64, 2 * R), BF16)],
-        place, low_rows, inputs, cotangent,
-        scratch=[pltpu.VMEM((256, 2 * R), F32)], name="project",
-    )
-    parts = tie(exchange(parts, "feat", X_GROUPS), near[3])
+    near += [over_feat(z_inputs, PARTNER[l]) for l in range(3, LEVELS)]
+    (parts,) = call(
+        project_kernel, [((4, 64, 2 * R), BF16)], place, low_rows, inputs, cotangent,
+        scratch=[pltpu.VMEM((BS, 2 * R), BF16), pltpu.VMEM((256, 2 * R), F32)], name="project",
+    )
+    parts = tie(exchange(parts, "feat", X_GROUPS), near[4])
     (total,) = call(x_sum_kernel, [((64, 2 * R), BF16)], place, parts, name="x_sum")
+    near_parts = tie(near_parts, total)
     for level in (2, 3, 4):
         total = (total.astype(F32) + over_feat(total, PARTNER[level]).astype(F32)).astype(BF16)
+    near_sum = lax.psum_scatter(near_parts, "dp", axis_index_groups=YC_GROUPS)
+
     st = exchange(jnp.broadcast_to(total, (4, 64, 2 * R)), "feat", X_GROUPS)
     st = st.reshape(256, 2 * R)
 
     gathered = tie(gathered, total)
-    near_parts = tie(near_parts, gathered)
-    near_sum = lax.psum_scatter(near_parts, "dp", axis_index_groups=YC_GROUPS)
     *z, w = call(
         weights_kernel, [(block, BF16)] * LEVELS + [((levels, BS, BS), BF16)],
-        place, gathered, cotangent, name="weights",
-    )
+        place, gathered, cotangent, name="weights", limit=60,
+    )
+    z = z[::-1]
+    z = [over_feat(z[l], PARTNER[l]) for l in reversed(range(LEVELS))][::-1]
     st = tie(st, w)
-    z = [over_feat(z[l], PARTNER[l]) for l in reversed(range(LEVELS))][::-1]
-
-    half = (4, 2, 4, 32, BS)
-    keep, send = call(
-        far_grads_kernel, [(half, BF16)] * 2, place, *near[2:], st, inputs, cotangent,
+
+    (parts,) = call(
+        far_grads_kernel, [((8, 2, 3, 32, BS), BF16)], place, *near[3:], st, inputs, cotangent,
         scratch=[pltpu.VMEM((BS, BS), F32)], name="far_grads",
     )
-    got = over_dp(send, CORE)
-    (parts,) = call(core_sum_kernel, [(half, BF16)], place, keep, got, name="far_grads_core")
     w = tie(w, parts)
     (output,) = call(
-        output_kernel, [(block, BF16)], place, inputs, *near, w, st, low, name="output"
-    )
-    parts = exchange(parts, "dp", Y_GROUPS)
+        output_kernel, [(block, BF16)], place, inputs, *near, w, st, low_rows,
+        scratch=[pltpu.VMEM((BS, 2 * R), BF16)], name="output",
+    )
+    parts = exchange(parts, "dp", YC_GROUPS)
     piece = (levels + 1, 32, BS)
     mine, send = call(
         group_sum_kernel, [(piece, F32), (piece, BF16)], place, near_sum, parts, name="grads_sum"
     )
     grads = (mine + over_dp(send, Z_HI).astype(F32)) * SCALE
     (grad_inputs,) = call(
-        grad_inputs_kernel, [(block, BF16)], place, cotangent, w, *z, tie(st, send), low,
-        name="grad_inputs",
+        grad_inputs_kernel, [(block, BF16)], place, cotangent, w, *z[::-1], tie(st, send), low_rows,
+        scratch=[pltpu.VMEM((BS, 2 * R), BF16)], name="grad_inputs",
     )
     return output, grad_inputs, grads[:levels], grads[levels, :, :R], grads[levels, :, R:].T
 

time: 222 us -> 206 us (0.928)
  the two profiles are of different devices: /device:TPU:8 before, /device:TPU:104 now
where the time goes in v3:
time: 206 us; the launch traced here: 205 us
  starting transfers between devices  96.1 us (47%)
  waiting for transfers between devices  57.9 us (28%)
  Pallas kernels  19.8 us (10%)
  local copies, waits for them, and re-layouts  14.5 us (7%)
  between operations  14.5 us (7%)
    ppermute x13, starting transfers between devices, over_feat(): return lax.ppermute(value, 'feat', pairs)  52.5 us
    ppermute x13, waiting for transfers between devices, over_feat(): return lax.ppermute(value, 'feat', pairs)  29.2 us
    ppermute x2, starting transfers between devices, over_dp(): return lax.ppermute(value, 'dp', pairs)  26.7 us
    ppermute x2, waiting for transfers between devices, over_dp(): return lax.ppermute(value, 'dp', pairs)  23.1 us
    pallas_call x9, Pallas kernels, call(): pl.pallas_call(kernel, out_shape=shapes, in_specs=[pl.BlockSpec(memory_sp...  19.8 us
    all_to_all x4, starting transfers between devices, exchange(): lax.all_to_all(value, axis, 0, 0, tiled=True, axis_index_groups=groups)  16.8 us
    unnamed x52, local copies, waits for them, and re-layouts  12.3 us
    all_to_all x4, waiting for transfers between devices, exchange(): lax.all_to_all(value, axis, 0, 0, tiled=True, axis_index_groups=groups)  5.49 us
  transfers between devices with their start and end apart: 21, of which 10 were waited for; matrix products, arithmetic and copies ran while one was open for 1% of the time, Pallas kernels for 9%

profile of v3, /device:TPU:104, one launch (start us, length us, event | category | flops | bytes accessed | tf_op | source)
XLA Modules:
  0.0 204.6 jit_solution(10098032229922520014)
XLA Ops:
  9.2 4.9 %collective-permute-start.1 = (bf16[256,512]{1,0:T(8,128)(2,1)}, bf16[256,512]{1,0:T(8,128)(2,1)S(1)}, u32[]{:S(2)}, u32[]{:S(2)}) collective-permute-start(bf16[256,512]{1,0:T(8,128)(2,1)} %inputs.7), channel_id=1, source_target_pairs={{0,2},{1,3},{2,0},{3,1},{4,6},{5,7},{6,4},{7,5},{8,10},{9,11},{10,... | collective-permute-start | bytes 786440 | tf_op jit(solution)/shard_map/ppermute | solution.py:41
  14.2 2.5 %collective-permute-start = (bf16[256,512]{1,0:T(8,128)(2,1)}, bf16[256,512]{1,0:T(8,128)(2,1)S(1)}, u32[]{:S(2)}, u32[]{:S(2)}) collective-permute-start(bf16[256,512]{1,0:T(8,128)(2,1)} %inputs.7), channel_id=1, source_target_pairs={{0,1},{1,0},{2,3},{3,2},{4,5},{5,4},{6,7},{7,6},{8,9},{9,8},{10,11... | collective-permute-start | bytes 786440 | tf_op jit(solution)/shard_map/ppermute | solution.py:41
  18.4 13.9 %collective-permute-start.3 = (bf16[7,32,512]{2,1,0:T(8,128)(2,1)S(1)}, bf16[7,32,512]{2,1,0:T(8,128)(2,1)S(1)}, u32[]{:S(2)}, u32[]{:S(2)}) collective-permute-start(bf16[7,32,512]{2,1,0:T(8,128)(2,1)S(1)} %pad_maximum_fusion.mine), channel_id=1, source_target_pairs={{0,64},{32,96},{64,0},{96,32},{128,192},{160,224},{192,128},{224,1... | collective-permute-start | bytes 688136 | tf_op jit(solution)/shard_map/ppermute | solution.py:37
  34.6 3.2 %near_grads.1 = bf16[8,2,4,32,512]{4,3,2,1,0:T(8,128)(2,1)} custom-call(s32[4]{0:T(128)S(1)} %pad_add_fusion.place, bf16[256,512]{1,0:T(8,128)(2,1)S(1)} %copy-done.7, bf16[256,512]{1,0:T(8,128)(2,1)S(1)} %collective-permute-done.n0, bf16[256,512]{1,0:T(8,128)(2,1)S(1)} %collective-permute-done.1.n1, bf16[256,512]{1,0:T(8,128)(2,1)S(1)} %collective-permute-done.2.n2, ...), custom_call_target="tpu_custom_call" | custom-call | tf_op jit(solution)/shard_map/near_grads/pallas_call | solution.py:62
  37.8 7.4 %collective-permute-done.3.got = bf16[7,32,512]{2,1,0:T(8,128)(2,1)S(1)} collective-permute-done((bf16[7,32,512]{2,1,0:T(8,128)(2,1)S(1)}, bf16[7,32,512]{2,1,0:T(8,128)(2,1)S(1)}, u32[]{:S(2)}, u32[]{:S(2)}) %collective-permute-start.3) | collective-permute-done | bytes 229408 | tf_op jit(solution)/shard_map/ppermute | solution.py:37
  46.7 4.9 %all-to-all-start = ((bf16[8,2,32,512]{3,2,1,0:T(8,128)(2,1)}), bf16[8,2,32,512]{3,2,1,0:T(8,128)(2,1)S(1)}, u32[]{:S(2)}, u32[]{:S(2)}) async-start(bf16[8,2,32,512]{3,2,1,0:T(8,128)(2,1)} %get-tuple-element.26), calls=%async_computation | async-start | bytes 1048576 | tf_op jit(solution)/shard_map/all_to_all | solution.py:45
  51.7 6.2 %collective-permute-start.5 = (bf16[256,512]{1,0:T(8,128)(2,1)S(1)}, bf16[256,512]{1,0:T(8,128)(2,1)S(1)}, u32[]{:S(2)}, u32[]{:S(2)}) collective-permute-start(bf16[256,512]{1,0:T(8,128)(2,1)S(1)} %copy-done.8), channel_id=1, source_target_pairs={{0,16},{1,17},{2,18},{3,19},{4,20},{5,21},{6,22},{7,23},{8,24},{9,... | collective-permute-start | bytes 786440 | tf_op jit(solution)/shard_map/ppermute | solution.py:41
  57.9 2.6 %all-to-all-done.gathered = bf16[8,2,32,512]{3,2,1,0:T(8,128)(2,1)S(1)} async-done(((bf16[8,2,32,512]{3,2,1,0:T(8,128)(2,1)}), bf16[8,2,32,512]{3,2,1,0:T(8,128)(2,1)S(1)}, u32[]{:S(2)}, u32[]{:S(2)}) %all-to-all-start) | async-done | bytes 524320 | tf_op jit(solution)/shard_map/all_to_all | solution.py:45
  62.1 3.4 %all-to-all-start.1 = ((bf16[4,64,512]{2,1,0:T(8,128)(2,1)}), bf16[4,64,512]{2,1,0:T(8,128)(2,1)S(1)}, u32[]{:S(2)}, u32[]{:S(2)}) async-start(bf16[4,64,512]{2,1,0:T(8,128)(2,1)} %project.1), calls=%async_computation.1 | async-start | bytes 524288 | tf_op jit(solution)/shard_map/all_to_all | solution.py:45
  65.6 15.0 %collective-permute-done.5.n4 = bf16[256,512]{1,0:T(8,128)(2,1)S(1)} collective-permute-done((bf16[256,512]{1,0:T(8,128)(2,1)S(1)}, bf16[256,512]{1,0:T(8,128)(2,1)S(1)}, u32[]{:S(2)}, u32[]{:S(2)}) %collective-permute-start.5) | collective-permute-done | bytes 262176 | tf_op jit(solution)/shard_map/ppermute | solution.py:41
  83.2 4.2 %collective-permute-done.6 = bf16[64,512]{1,0:T(8,128)(2,1)S(1)} collective-permute-done((bf16[64,512]{1,0:T(8,128)(2,1)S(1)}, bf16[64,512]{1,0:T(8,128)(2,1)S(1)}, u32[]{:S(2)}, u32[]{:S(2)}) %collective-permute-start.6) | collective-permute-done | bytes 65568 | tf_op jit(solution)/shard_map/ppermute | solution.py:41
  87.4 5.9 %collective-permute-start.7 = (bf16[64,512]{1,0:T(8,128)(2,1)S(1)}, bf16[64,512]{1,0:T(8,128)(2,1)S(1)}, u32[]{:S(2)}, u32[]{:S(2)}) collective-permute-start(bf16[64,512]{1,0:T(8,128)(2,1)S(1)} %add_convert_fusion.2), channel_id=1, source_target_pairs={{0,8},{1,9},{2,10},{3,11},{4,12},{5,13},{6,14},{7,15},{8,0},{9,1},... | collective-permute-start | bytes 196616 | tf_op jit(solution)/shard_map/ppermute | solution.py:41
  93.3 2.5 %collective-permute-done.7 = bf16[64,512]{1,0:T(8,128)(2,1)S(1)} collective-permute-done((bf16[64,512]{1,0:T(8,128)(2,1)S(1)}, bf16[64,512]{1,0:T(8,128)(2,1)S(1)}, u32[]{:S(2)}, u32[]{:S(2)}) %collective-permute-start.7) | collective-permute-done | bytes 65568 | tf_op jit(solution)/shard_map/ppermute | solution.py:41
  95.8 7.1 %collective-permute-start.8 = (bf16[64,512]{1,0:T(8,128)(2,1)S(1)}, bf16[64,512]{1,0:T(8,128)(2,1)S(1)}, u32[]{:S(2)}, u32[]{:S(2)}) collective-permute-start(bf16[64,512]{1,0:T(8,128)(2,1)S(1)} %add_convert_fusion.1), channel_id=1, source_target_pairs={{0,16},{1,17},{2,18},{3,19},{4,20},{5,21},{6,22},{7,23},{8,24},{9,... | collective-permute-start | bytes 196616 | tf_op jit(solution)/shard_map/ppermute | solution.py:41
  106.8 3.4 %all-to-all-start.2 = ((bf16[4,64,512]{2,1,0:T(8,128)(2,1)}), bf16[4,64,512]{2,1,0:T(8,128)(2,1)S(1)}, u32[]{:S(2)}, u32[]{:S(2)}) async-start(bf16[4,64,512]{2,1,0:T(8,128)(2,1)} %broadcast_in_dim.7), calls=%async_computation.2 | async-start | bytes 524288 | tf_op jit(solution)/shard_map/all_to_all | solution.py:45
  110.2 4.9 %weights.1 = (bf16[256,512]{1,0:T(8,128)(2,1)}, bf16[256,512]{1,0:T(8,128)(2,1)}, bf16[256,512]{1,0:T(8,128)(2,1)}, bf16[256,512]{1,0:T(8,128)(2,1)}, bf16[256,5...) custom-call(s32[4]{0:T(128)} %copy-done.24, bf16[8,2,6,32,512]{4,3,2,1,0:T(8,128)(2,1)} %bitcast.20, bf16[256,512]{1,0:T(8,128)(2,1)} %cot.9), custom_call_target="tpu_custom_call" | custom-call | tf_op jit(solution)/shard_map/weights/pallas_call | solution.py:62
  121.0 5.1 %all-to-all-start.3 = ((bf16[8,2,3,32,512]{4,3,2,1,0:T(8,128)(2,1)}), bf16[8,2,3,32,512]{4,3,2,1,0:T(8,128)(2,1)}, u32[]{:S(2)}, u32[]{:S(2)}) async-start(bf16[8,2,3,32,512]{4,3,2,1,0:T(8,128)(2,1)} %copy-done.6), calls=%async_computation.4 | async-start | bytes 3145728 | tf_op jit(solution)/shard_map/all_to_all | solution.py:45
  126.1 8.0 %collective-permute-start.9 = (bf16[256,512]{1,0:T(8,128)(2,1)}, bf16[256,512]{1,0:T(8,128)(2,1)}, u32[]{:S(2)}, u32[]{:S(2)}) collective-permute-start(bf16[256,512]{1,0:T(8,128)(2,1)} %get-tuple-element.32), channel_id=1, source_target_pairs={{0,16},{1,17},{2,18},{3,19},{4,20},{5,21},{6,22},{7,23},{8,24},{9,... | collective-permute-start | bytes 786440 | tf_op jit(solution)/shard_map/ppermute | solution.py:41
  134.1 3.9 %collective-permute-start.10 = (bf16[256,512]{1,0:T(8,128)(2,1)}, bf16[256,512]{1,0:T(8,128)(2,1)}, u32[]{:S(2)}, u32[]{:S(2)}) collective-permute-start(bf16[256,512]{1,0:T(8,128)(2,1)} %get-tuple-element.33), channel_id=1, source_target_pairs={{0,8},{1,9},{2,10},{3,11},{4,12},{5,13},{6,14},{7,15},{8,0},{9,1},... | collective-permute-start | bytes 786440 | tf_op jit(solution)/shard_map/ppermute | solution.py:41
  139.9 3.8 %collective-permute-start.12 = (bf16[256,512]{1,0:T(8,128)(2,1)}, bf16[256,512]{1,0:T(8,128)(2,1)}, u32[]{:S(2)}, u32[]{:S(2)}) collective-permute-start(bf16[256,512]{1,0:T(8,128)(2,1)} %get-tuple-element.35), channel_id=1, source_target_pairs={{0,2},{1,3},{2,0},{3,1},{4,6},{5,7},{6,4},{7,5},{8,10},{9,11},{10,... | collective-permute-start | bytes 786440 | tf_op jit(solution)/shard_map/ppermute | solution.py:41
  150.0 6.3 %collective-permute-done.9.z4 = bf16[256,512]{1,0:T(8,128)(2,1)} collective-permute-done((bf16[256,512]{1,0:T(8,128)(2,1)}, bf16[256,512]{1,0:T(8,128)(2,1)}, u32[]{:S(2)}, u32[]{:S(2)}) %collective-permute-start.9) | collective-permute-done | bytes 262176 | tf_op jit(solution)/shard_map/ppermute | solution.py:41
  156.2 12.8 %collective-permute-start.14 = (bf16[7,32,512]{2,1,0:T(8,128)(2,1)S(1)}, bf16[7,32,512]{2,1,0:T(8,128)(2,1)S(1)}, u32[]{:S(2)}, u32[]{:S(2)}) collective-permute-start(bf16[7,32,512]{2,1,0:T(8,128)(2,1)S(1)} %get-tuple-element.38), channel_id=1, source_target_pairs={{0,64},{32,96},{64,0},{96,32},{128,192},{160,224},{192,128},{224,1... | collective-permute-start | bytes 688136 | tf_op jit(solution)/shard_map/ppermute | solution.py:37
  178.0 2.5 %grad_inputs.1 = bf16[256,512]{1,0:T(8,128)(2,1)} custom-call(s32[4]{0:T(128)S(1)} %copy-done.25, bf16[256,512]{1,0:T(8,128)(2,1)S(1)} %copy-done.5, bf16[6,512,512]{2,1,0:T(8,128)(2,1)S(1)} %copy-done, bf16[256,512]{1,0:T(8,128)(2,1)} %collective-permute-done.9.z4, bf16[256,512]{1,0:T(8,128)(2,1)} %collective-permute-done.10.z3, ...), custom_call_target="tpu_custom_call" | custom-call | tf_op jit(solution)/shard_map/grad_inputs/pallas_call | solution.py:62
  180.6 15.8 %collective-permute-done.14 = bf16[7,32,512]{2,1,0:T(8,128)(2,1)S(1)} collective-permute-done((bf16[7,32,512]{2,1,0:T(8,128)(2,1)S(1)}, bf16[7,32,512]{2,1,0:T(8,128)(2,1)S(1)}, u32[]{:S(2)}, u32[]{:S(2)}) %collective-permute-start.14) | collective-permute-done | bytes 229408 | tf_op jit(solution)/shard_map/ppermute | solution.py:37
  (91 shorter events, 39.9 us)
Async XLA Ops:
  7.2 103.1 %all-gather.3.cloned.1.call-start = ((), (), s32[]{:S(2)}) async-start(), calls=%async_computation.6 | async-start | bytes 3538944 | tf_op jit(solution)/shard_map/all_gather | solution.py:184
  7.2 25.2 %collective-permute-start.2 = (bf16[256,512]{1,0:T(8,128)(2,1)}, bf16[256,512]{1,0:T(8,128)(2,1)S(1)}, u32[]{:S(2)}, u32[]{:S(2)}) collective-permute-start(bf16[256,512]{1,0:T(8,128)(2,1)} %inputs.7), channel_id=1, source_target_pairs={{0,4},{1,5},{2,6},{3,7},{4,0},{5,1},{6,2},{7,3},{8,12},{9,13},{10,... | collective-permute-start | bytes 786440 | tf_op jit(solution)/shard_map/ppermute | solution.py:41
  9.2 23.2 %collective-permute-start.1 = (bf16[256,512]{1,0:T(8,128)(2,1)}, bf16[256,512]{1,0:T(8,128)(2,1)S(1)}, u32[]{:S(2)}, u32[]{:S(2)}) collective-permute-start(bf16[256,512]{1,0:T(8,128)(2,1)} %inputs.7), channel_id=1, source_target_pairs={{0,2},{1,3},{2,0},{3,1},{4,6},{5,7},{6,4},{7,5},{8,10},{9,11},{10,... | collective-permute-start | bytes 786440 | tf_op jit(solution)/shard_map/ppermute | solution.py:41
  14.2 18.3 %collective-permute-start = (bf16[256,512]{1,0:T(8,128)(2,1)}, bf16[256,512]{1,0:T(8,128)(2,1)S(1)}, u32[]{:S(2)}, u32[]{:S(2)}) collective-permute-start(bf16[256,512]{1,0:T(8,128)(2,1)} %inputs.7), channel_id=1, source_target_pairs={{0,1},{1,0},{2,3},{3,2},{4,5},{5,4},{6,7},{7,6},{8,9},{9,8},{10,11... | collective-permute-start | bytes 786440 | tf_op jit(solution)/shard_map/ppermute | solution.py:41
  18.4 26.8 %collective-permute-start.3 = (bf16[7,32,512]{2,1,0:T(8,128)(2,1)S(1)}, bf16[7,32,512]{2,1,0:T(8,128)(2,1)S(1)}, u32[]{:S(2)}, u32[]{:S(2)}) collective-permute-start(bf16[7,32,512]{2,1,0:T(8,128)(2,1)S(1)} %pad_maximum_fusion.mine), channel_id=1, source_target_pairs={{0,64},{32,96},{64,0},{96,32},{128,192},{160,224},{192,128},{224,1... | collective-permute-start | bytes 688136 | tf_op jit(solution)/shard_map/ppermute | solution.py:37
  32.4 48.2 %copy-start.24 = (s32[4]{0:T(128)}, s32[4]{0:T(128)S(1)}, u32[]{:S(2)}) copy-start(s32[4]{0:T(128)S(1)} %pad_add_fusion.place) | copy-start | bytes 52
  46.7 13.8 %all-to-all-start = ((bf16[8,2,32,512]{3,2,1,0:T(8,128)(2,1)}), bf16[8,2,32,512]{3,2,1,0:T(8,128)(2,1)S(1)}, u32[]{:S(2)}, u32[]{:S(2)}) async-start(bf16[8,2,32,512]{3,2,1,0:T(8,128)(2,1)} %get-tuple-element.26), calls=%async_computation | async-start | bytes 1048576 | tf_op jit(solution)/shard_map/all_to_all | solution.py:45
  51.7 29.0 %collective-permute-start.5 = (bf16[256,512]{1,0:T(8,128)(2,1)S(1)}, bf16[256,512]{1,0:T(8,128)(2,1)S(1)}, u32[]{:S(2)}, u32[]{:S(2)}) collective-permute-start(bf16[256,512]{1,0:T(8,128)(2,1)S(1)} %copy-done.8), channel_id=1, source_target_pairs={{0,16},{1,17},{2,18},{3,19},{4,20},{5,21},{6,22},{7,23},{8,24},{9,... | collective-permute-start | bytes 786440 | tf_op jit(solution)/shard_map/ppermute | solution.py:41
  62.1 18.5 %all-to-all-start.1 = ((bf16[4,64,512]{2,1,0:T(8,128)(2,1)}), bf16[4,64,512]{2,1,0:T(8,128)(2,1)S(1)}, u32[]{:S(2)}, u32[]{:S(2)}) async-start(bf16[4,64,512]{2,1,0:T(8,128)(2,1)} %project.1), calls=%async_computation.1 | async-start | bytes 524288 | tf_op jit(solution)/shard_map/all_to_all | solution.py:45
  65.6 80.6 %reduce-scatter.2.cloned.1.call-start = ((), (), s32[]{:S(2)}) async-start(), calls=%async_computation.5 | async-start | bytes 2359296 | tf_op jit(solution)/shard_map/reduce_scatter | solution.py:197
  80.6 36.2 %copy-start.19 = (bf16[256,512]{1,0:T(8,128)(2,1)}, bf16[256,512]{1,0:T(8,128)(2,1)S(1)}, u32[]{:S(2)}) copy-start(bf16[256,512]{1,0:T(8,128)(2,1)S(1)} %collective-permute-done.5.n4) | copy-start | bytes 786436
  81.2 6.2 %collective-permute-start.6 = (bf16[64,512]{1,0:T(8,128)(2,1)S(1)}, bf16[64,512]{1,0:T(8,128)(2,1)S(1)}, u32[]{:S(2)}, u32[]{:S(2)}) collective-permute-start(bf16[64,512]{1,0:T(8,128)(2,1)S(1)} %x_sum.1), channel_id=1, source_target_pairs={{0,4},{1,5},{2,6},{3,7},{4,0},{5,1},{6,2},{7,3},{8,12},{9,13},{10,... | collective-permute-start | bytes 196616 | tf_op jit(solution)/shard_map/ppermute | solution.py:41
  87.4 8.4 %collective-permute-start.7 = (bf16[64,512]{1,0:T(8,128)(2,1)S(1)}, bf16[64,512]{1,0:T(8,128)(2,1)S(1)}, u32[]{:S(2)}, u32[]{:S(2)}) collective-permute-start(bf16[64,512]{1,0:T(8,128)(2,1)S(1)} %add_convert_fusion.2), channel_id=1, source_target_pairs={{0,8},{1,9},{2,10},{3,11},{4,12},{5,13},{6,14},{7,15},{8,0},{9,1},... | collective-permute-start | bytes 196616 | tf_op jit(solution)/shard_map/ppermute | solution.py:41
  95.8 10.2 %collective-permute-start.8 = (bf16[64,512]{1,0:T(8,128)(2,1)S(1)}, bf16[64,512]{1,0:T(8,128)(2,1)S(1)}, u32[]{:S(2)}, u32[]{:S(2)}) collective-permute-start(bf16[64,512]{1,0:T(8,128)(2,1)S(1)} %add_convert_fusion.1), channel_id=1, source_target_pairs={{0,16},{1,17},{2,18},{3,19},{4,20},{5,21},{6,22},{7,23},{8,24},{9,... | collective-permute-start | bytes 196616 | tf_op jit(solution)/shard_map/ppermute | solution.py:41
  103.0 13.9 %collective-permute-start.4 = (bf16[256,512]{1,0:T(8,128)(2,1)S(1)}, bf16[256,512]{1,0:T(8,128)(2,1)S(1)}, u32[]{:S(2)}, u32[]{:S(2)}) collective-permute-start(bf16[256,512]{1,0:T(8,128)(2,1)S(1)} %copy-done.8), channel_id=1, source_target_pairs={{0,8},{1,9},{2,10},{3,11},{4,12},{5,13},{6,14},{7,15},{8,0},{9,1},... | collective-permute-start | bytes 786440 | tf_op jit(solution)/shard_map/ppermute | solution.py:41
  106.8 10.1 %all-to-all-start.2 = ((bf16[4,64,512]{2,1,0:T(8,128)(2,1)}), bf16[4,64,512]{2,1,0:T(8,128)(2,1)S(1)}, u32[]{:S(2)}, u32[]{:S(2)}) async-start(bf16[4,64,512]{2,1,0:T(8,128)(2,1)} %broadcast_in_dim.7), calls=%async_computation.2 | async-start | bytes 524288 | tf_op jit(solution)/shard_map/all_to_all | solution.py:45
  121.0 48.0 %copy-start = (bf16[6,512,512]{2,1,0:T(8,128)(2,1)S(1)}, bf16[6,512,512]{2,1,0:T(8,128)(2,1)}, u32[]{:S(2)}) copy-start(bf16[6,512,512]{2,1,0:T(8,128)(2,1)} %get-tuple-element.31.w) | copy-start | bytes 9437188
  121.0 26.3 %all-to-all-start.3 = ((bf16[8,2,3,32,512]{4,3,2,1,0:T(8,128)(2,1)}), bf16[8,2,3,32,512]{4,3,2,1,0:T(8,128)(2,1)}, u32[]{:S(2)}, u32[]{:S(2)}) async-start(bf16[8,2,3,32,512]{4,3,2,1,0:T(8,128)(2,1)} %copy-done.6), calls=%async_computation.4 | async-start | bytes 3145728 | tf_op jit(solution)/shard_map/all_to_all | solution.py:45
  126.1 30.2 %collective-permute-start.9 = (bf16[256,512]{1,0:T(8,128)(2,1)}, bf16[256,512]{1,0:T(8,128)(2,1)}, u32[]{:S(2)}, u32[]{:S(2)}) collective-permute-start(bf16[256,512]{1,0:T(8,128)(2,1)} %get-tuple-element.32), channel_id=1, source_target_pairs={{0,16},{1,17},{2,18},{3,19},{4,20},{5,21},{6,22},{7,23},{8,24},{9,... | collective-permute-start | bytes 786440 | tf_op jit(solution)/shard_map/ppermute | solution.py:41
  134.1 43.9 %collective-permute-start.10 = (bf16[256,512]{1,0:T(8,128)(2,1)}, bf16[256,512]{1,0:T(8,128)(2,1)}, u32[]{:S(2)}, u32[]{:S(2)}) collective-permute-start(bf16[256,512]{1,0:T(8,128)(2,1)} %get-tuple-element.33), channel_id=1, source_target_pairs={{0,8},{1,9},{2,10},{3,11},{4,12},{5,13},{6,14},{7,15},{8,0},{9,1},... | collective-permute-start | bytes 786440 | tf_op jit(solution)/shard_map/ppermute | solution.py:41
  138.0 40.0 %collective-permute-start.11 = (bf16[256,512]{1,0:T(8,128)(2,1)}, bf16[256,512]{1,0:T(8,128)(2,1)}, u32[]{:S(2)}, u32[]{:S(2)}) collective-permute-start(bf16[256,512]{1,0:T(8,128)(2,1)} %get-tuple-element.34), channel_id=1, source_target_pairs={{0,4},{1,5},{2,6},{3,7},{4,0},{5,1},{6,2},{7,3},{8,12},{9,13},{10,... | collective-permute-start | bytes 786440 | tf_op jit(solution)/shard_map/ppermute | solution.py:41
  139.9 38.1 %collective-permute-start.12 = (bf16[256,512]{1,0:T(8,128)(2,1)}, bf16[256,512]{1,0:T(8,128)(2,1)}, u32[]{:S(2)}, u32[]{:S(2)}) collective-permute-start(bf16[256,512]{1,0:T(8,128)(2,1)} %get-tuple-element.35), channel_id=1, source_target_pairs={{0,2},{1,3},{2,0},{3,1},{4,6},{5,7},{6,4},{7,5},{8,10},{9,11},{10,... | collective-permute-start | bytes 786440 | tf_op jit(solution)/shard_map/ppermute | solution.py:41
  143.7 34.3 %collective-permute-start.13 = (bf16[256,512]{1,0:T(8,128)(2,1)}, bf16[256,512]{1,0:T(8,128)(2,1)}, u32[]{:S(2)}, u32[]{:S(2)}) collective-permute-start(bf16[256,512]{1,0:T(8,128)(2,1)} %get-tuple-element.36), channel_id=1, source_target_pairs={{0,1},{1,0},{2,3},{3,2},{4,5},{5,4},{6,7},{7,6},{8,9},{9,8},{10,11... | collective-permute-start | bytes 786440 | tf_op jit(solution)/shard_map/ppermute | solution.py:41
  156.2 40.1 %collective-permute-start.14 = (bf16[7,32,512]{2,1,0:T(8,128)(2,1)S(1)}, bf16[7,32,512]{2,1,0:T(8,128)(2,1)S(1)}, u32[]{:S(2)}, u32[]{:S(2)}) collective-permute-start(bf16[7,32,512]{2,1,0:T(8,128)(2,1)S(1)} %get-tuple-element.38), channel_id=1, source_target_pairs={{0,64},{32,96},{64,0},{96,32},{128,192},{160,224},{192,128},{224,1... | collective-permute-start | bytes 688136 | tf_op jit(solution)/shard_map/ppermute | solution.py:37
  (23 other events, 162.4 us)
Sparse Core Ops, SparseCore 0:
  46.8 42.1 all-gather.2
  91.9 42.0 reduce-scatter.1

commit v4 on v3

--- a/solution.py
+++ b/solution.py
@@ -26,6 +26,7 @@
 Z_HI = dp_pairs(lambda y, h, c: (y, 1 - h, c))
 YC_GROUPS = [[(y * 2 + h) * 2 + c for y in range(4) for c in range(2)] for h in range(2)]
 X_GROUPS = [[z * 4 + x for x in range(4)] for z in range(8)]
+Z_GROUPS = [[(z + i) * 4 + x for i in range(4)] for z in (0, 4) for x in range(4)]
 PARTNER = [[(i, i ^ (1 << level)) for i in range(32)] for level in range(LEVELS)]
 
 
@@ -98,19 +99,36 @@
         out[x] = part[x * 64 : (x + 1) * 64, :].astype(BF16)
 
 
-def weights_kernel(place, gathered, cot, z4, z3, z2, z1, z0, w):
+def far_weights_kernel(place, gathered, cot, z4, z3, z2, w):
     for k in range(8):
         for g in range(2):
-            w[:, pl.ds(rows_of(place, k // 2, g, k % 2), 32), :] = gathered[k, g]
-    for level, z in enumerate((z0, z1, z2, z3, z4)):
+            rows = pl.ds(rows_of(place, k // 2, g, k % 2), 32)
+            w[:, rows, :] = gathered[k, g, 3:]
+    for level, z in enumerate((z2, z3, z4)):
+        z[...] = dot_nt(cot[...], w[level]).astype(BF16)
+
+
+def near_weights_kernel(place, gathered, cot, z1, z0, w):
+    for k in range(8):
+        for g in range(2):
+            rows = pl.ds(rows_of(place, k // 2, g, k % 2), 32)
+            w[:, rows, :] = gathered[k, g, :3]
+    for level, z in enumerate((z0, z1)):
         z[...] = dot_nt(cot[...], w[level + 1]).astype(BF16)
 
 
-def x_sum_kernel(place, parts, out):
+def sum_kernel(place, parts, out):
     total = parts[0].astype(F32)
-    for x in range(1, 4):
-        total = total + parts[x].astype(F32)
-    out[...] = total.astype(BF16)
+    for k in range(1, parts.shape[0]):
+        total = total + parts[k].astype(F32)
+    for k in range(out.shape[0]):
+        out[k] = total.astype(BF16)
+
+
+def pair_sum_kernel(place, mine, got, out):
+    total = mine[0].astype(F32) + got[0].astype(F32)
+    for k in range(out.shape[0]):
+        out[k] = total.astype(BF16)
 
 
 def near_grads_kernel(place, inputs, n0, n1, n2, cot, out, grad):
@@ -145,11 +163,13 @@
     send[4:] = total[1].astype(BF16)
 
 
-def output_kernel(place, inputs, n0, n1, n2, n3, n4, w, st, gathered, out, low):
+def output_kernel(
+    place, inputs, n0, n1, n2, n3, n4, near_w, far_w, st, gathered, out, low
+):
     order_low(place, gathered, low)
     total = dot_nt(st[:, :R], low[:, R:])
     for n, left in enumerate((inputs, n0, n1, n2, n3, n4)):
-        total = total + dot_nn(left[...], w[n])
+        total = total + dot_nn(left[...], near_w[n] if n < 3 else far_w[n - 3])
     out[...] = total.astype(BF16)
 
 
@@ -190,31 +210,38 @@
         scratch=[pltpu.VMEM((BS, 2 * R), BF16), pltpu.VMEM((256, 2 * R), F32)], name="project",
     )
     parts = tie(exchange(parts, "feat", X_GROUPS), near[4])
-    (total,) = call(x_sum_kernel, [((64, 2 * R), BF16)], place, parts, name="x_sum")
-    near_parts = tie(near_parts, total)
-    for level in (2, 3, 4):
-        total = (total.astype(F32) + over_feat(total, PARTNER[level]).astype(F32)).astype(BF16)
+    (parts,) = call(sum_kernel, [((4, 64, 2 * R), BF16)], place, parts, name="x_sum")
+    near_parts = tie(near_parts, parts)
+    parts = exchange(parts, "feat", Z_GROUPS)
+    (total,) = call(sum_kernel, [((1, 64, 2 * R), BF16)], place, parts, name="z_sum")
+    (parts,) = call(
+        pair_sum_kernel, [((4, 64, 2 * R), BF16)], place, total, over_feat(total, PARTNER[4]),
+        name="last_sum",
+    )
     near_sum = lax.psum_scatter(near_parts, "dp", axis_index_groups=YC_GROUPS)
 
-    st = exchange(jnp.broadcast_to(total, (4, 64, 2 * R)), "feat", X_GROUPS)
+    st = exchange(parts, "feat", X_GROUPS)
     st = st.reshape(256, 2 * R)
 
-    gathered = tie(gathered, total)
-    *z, w = call(
-        weights_kernel, [(block, BF16)] * LEVELS + [((levels, BS, BS), BF16)],
-        place, gathered, cotangent, name="weights", limit=60,
-    )
-    z = z[::-1]
-    z = [over_feat(z[l], PARTNER[l]) for l in reversed(range(LEVELS))][::-1]
-    st = tie(st, w)
+    gathered = tie(gathered, parts)
+    *far_z, far_w = call(
+        far_weights_kernel, [(block, BF16)] * 3 + [((3, BS, BS), BF16)],
+        place, gathered, cotangent, name="far_weights", limit=60,
+    )
+    far_z = [over_feat(far_z[4 - l], PARTNER[l]) for l in (4, 3, 2)][::-1]
+    st = tie(st, far_w)
 
     (parts,) = call(
         far_grads_kernel, [((8, 2, 3, 32, BS), BF16)], place, *near[3:], st, inputs, cotangent,
         scratch=[pltpu.VMEM((BS, BS), F32)], name="far_grads",
     )
-    w = tie(w, parts)
+    *near_z, near_w = call(
+        near_weights_kernel, [(block, BF16)] * 2 + [((3, BS, BS), BF16)],
+        place, tie(gathered, parts), cotangent, name="near_weights", limit=60,
+    )
+    z = [over_feat(near_z[1 - l], PARTNER[l]) for l in (1, 0)][::-1] + far_z
     (output,) = call(
-        output_kernel, [(block, BF16)], place, inputs, *near, w, st, low_rows,
+        output_kernel, [(block, BF16)], place, inputs, *near, near_w, far_w, st, low_rows,
         scratch=[pltpu.VMEM((BS, 2 * R), BF16)], name="output",
     )
     parts = exchange(parts, "dp", YC_GROUPS)
@@ -224,7 +251,7 @@
     )
     grads = (mine + over_dp(send, Z_HI).astype(F32)) * SCALE
     (grad_inputs,) = call(
-        grad_inputs_kernel, [(block, BF16)], place, cotangent, w, *z[::-1], tie(st, send), low_rows,
+        grad_inputs_kernel, [(block, BF16)], place, cotangent, near_w, *z[::-1], tie(st, send), low_rows,
         scratch=[pltpu.VMEM((BS, 2 * R), BF16)], name="grad_inputs",
     )
     return output, grad_inputs, grads[:levels], grads[levels, :, :R], grads[levels, :, R:].T

time: 206 us -> 203 us (0.985)
  blocking collectives: 0 us -> 14.7 us
  starting transfers between devices: 96.1 us -> 85.7 us
  local copies, waits for them, and re-layouts: 14.5 us -> 8.02 us
  waiting for transfers between devices: 57.9 us -> 53.9 us
  Pallas kernels: 19.8 us -> 23.5 us
    all_to_all x0 -> x1, blocking collectives: none -> 14.7 us  [exchange(): lax.all_to_all(value, axis, 0, 0, tiled=True, axis_index_groups=groups)]
    ppermute x13 -> x11, starting transfers between devices: 52.5 us -> 40.7 us  [over_feat(): return lax.ppermute(value, 'feat', pairs)]
    ppermute x13 -> x11, waiting for transfers between devices: 29.2 us -> 21.6 us  [over_feat(): return lax.ppermute(value, 'feat', pairs)]
    unnamed x52 -> x34, local copies, waits for them, and re-layouts: 12.3 us -> 6.6 us
    ppermute x2, waiting for transfers between devices: 23.1 us -> 26.9 us  [over_dp(): return lax.ppermute(value, 'dp', pairs)]
    pallas_call x9 -> x12, Pallas kernels: 19.8 us -> 23.5 us  [call(): pl.pallas_call(kernel, out_shape=shapes, in_specs=[pl.BlockSpec(memory_sp...]
  transfers between devices with their start and end apart: 21 -> 19, of which waited for: 10 -> 8; matrix products, arithmetic and copies ran while one was open for 1% -> 1% of each run, Pallas kernels for 9% -> 11%
where the time goes in v4:
time: 203 us; the launch traced here: 202 us
  starting transfers between devices  85.7 us (42%)
  waiting for transfers between devices  53.9 us (27%)
  Pallas kernels  23.5 us (12%)
  blocking collectives  14.7 us (7%)
  between operations  14.4 us (7%)
  local copies, waits for them, and re-layouts  8.02 us (4%)
    ppermute x11, starting transfers between devices, over_feat(): return lax.ppermute(value, 'feat', pairs)  40.7 us
    ppermute x2, starting transfers between devices, over_dp(): return lax.ppermute(value, 'dp', pairs)  28.4 us
    ppermute x2, waiting for transfers between devices, over_dp(): return lax.ppermute(value, 'dp', pairs)  26.9 us
    pallas_call x12, Pallas kernels, call(): pl.pallas_call(kernel, out_shape=shapes, in_specs=[pl.BlockSpec(memory_sp...  23.5 us
    ppermute x11, waiting for transfers between devices, over_feat(): return lax.ppermute(value, 'feat', pairs)  21.6 us
    all_to_all x4, starting transfers between devices, exchange(): lax.all_to_all(value, axis, 0, 0, tiled=True, axis_index_groups=groups)  16.5 us
    all_to_all x1, blocking collectives, exchange(): lax.all_to_all(value, axis, 0, 0, tiled=True, axis_index_groups=groups)  14.7 us
    unnamed x34, local copies, waits for them, and re-layouts  6.6 us
  transfers between devices with their start and end apart: 19, of which 8 were waited for; matrix products, arithmetic and copies ran while one was open for 1% of the time, Pallas kernels for 11%

profile of v4, /device:TPU:104, one launch (start us, length us, event | category | flops | bytes accessed | tf_op | source)
XLA Modules:
  0.0 202.1 jit_solution(13462625930986350392)
XLA Ops:
  9.2 4.9 %collective-permute-start.1 = (bf16[256,512]{1,0:T(8,128)(2,1)}, bf16[256,512]{1,0:T(8,128)(2,1)S(1)}, u32[]{:S(2)}, u32[]{:S(2)}) collective-permute-start(bf16[256,512]{1,0:T(8,128)(2,1)} %inputs.7), channel_id=1, source_target_pairs={{0,2},{1,3},{2,0},{3,1},{4,6},{5,7},{6,4},{7,5},{8,10},{9,11},{10,... | collective-permute-start | bytes 786440 | tf_op jit(solution)/shard_map/ppermute | solution.py:42
  18.4 13.9 %collective-permute-start.3 = (bf16[7,32,512]{2,1,0:T(8,128)(2,1)S(1)}, bf16[7,32,512]{2,1,0:T(8,128)(2,1)S(1)}, u32[]{:S(2)}, u32[]{:S(2)}) collective-permute-start(bf16[7,32,512]{2,1,0:T(8,128)(2,1)S(1)} %pad_maximum_fusion.mine), channel_id=1, source_target_pairs={{0,64},{32,96},{64,0},{96,32},{128,192},{160,224},{192,128},{224,1... | collective-permute-start | bytes 688136 | tf_op jit(solution)/shard_map/ppermute | solution.py:38
  34.4 3.2 %near_grads.1 = bf16[8,2,4,32,512]{4,3,2,1,0:T(8,128)(2,1)} custom-call(s32[4]{0:T(128)S(1)} %pad_add_fusion.place, bf16[256,512]{1,0:T(8,128)(2,1)S(1)} %copy-done.6, bf16[256,512]{1,0:T(8,128)(2,1)S(1)} %collective-permute-done.n0, bf16[256,512]{1,0:T(8,128)(2,1)S(1)} %collective-permute-done.1.n1, bf16[256,512]{1,0:T(8,128)(2,1)S(1)} %collective-permute-done.2.n2, ...), custom_call_target="tpu_custom_call" | custom-call | tf_op jit(solution)/shard_map/near_grads/pallas_call | solution.py:63
  37.6 7.6 %collective-permute-done.3.got = bf16[7,32,512]{2,1,0:T(8,128)(2,1)S(1)} collective-permute-done((bf16[7,32,512]{2,1,0:T(8,128)(2,1)S(1)}, bf16[7,32,512]{2,1,0:T(8,128)(2,1)S(1)}, u32[]{:S(2)}, u32[]{:S(2)}) %collective-permute-start.3) | collective-permute-done | bytes 229408 | tf_op jit(solution)/shard_map/ppermute | solution.py:38
  46.7 4.9 %all-to-all-start = ((bf16[8,2,32,512]{3,2,1,0:T(8,128)(2,1)}), bf16[8,2,32,512]{3,2,1,0:T(8,128)(2,1)S(1)}, u32[]{:S(2)}, u32[]{:S(2)}) async-start(bf16[8,2,32,512]{3,2,1,0:T(8,128)(2,1)} %get-tuple-element.27), calls=%async_computation | async-start | bytes 1048576 | tf_op jit(solution)/shard_map/all_to_all | solution.py:46
  51.6 6.2 %collective-permute-start.5 = (bf16[256,512]{1,0:T(8,128)(2,1)S(1)}, bf16[256,512]{1,0:T(8,128)(2,1)S(1)}, u32[]{:S(2)}, u32[]{:S(2)}) collective-permute-start(bf16[256,512]{1,0:T(8,128)(2,1)S(1)} %copy-done.7), channel_id=1, source_target_pairs={{0,16},{1,17},{2,18},{3,19},{4,20},{5,21},{6,22},{7,23},{8,24},{9,... | collective-permute-start | bytes 786440 | tf_op jit(solution)/shard_map/ppermute | solution.py:42
  57.9 2.6 %all-to-all-done.gathered = bf16[8,2,32,512]{3,2,1,0:T(8,128)(2,1)S(1)} async-done(((bf16[8,2,32,512]{3,2,1,0:T(8,128)(2,1)}), bf16[8,2,32,512]{3,2,1,0:T(8,128)(2,1)S(1)}, u32[]{:S(2)}, u32[]{:S(2)}) %all-to-all-start) | async-done | bytes 524320 | tf_op jit(solution)/shard_map/all_to_all | solution.py:46
  62.1 3.4 %all-to-all-start.1 = ((bf16[4,64,512]{2,1,0:T(8,128)(2,1)}), bf16[4,64,512]{2,1,0:T(8,128)(2,1)S(1)}, u32[]{:S(2)}, u32[]{:S(2)}) async-start(bf16[4,64,512]{2,1,0:T(8,128)(2,1)} %project.1), calls=%async_computation.1 | async-start | bytes 524288 | tf_op jit(solution)/shard_map/all_to_all | solution.py:46
  65.6 15.0 %collective-permute-done.5.n4 = bf16[256,512]{1,0:T(8,128)(2,1)S(1)} collective-permute-done((bf16[256,512]{1,0:T(8,128)(2,1)S(1)}, bf16[256,512]{1,0:T(8,128)(2,1)S(1)}, u32[]{:S(2)}, u32[]{:S(2)}) %collective-permute-start.5) | collective-permute-done | bytes 262176 | tf_op jit(solution)/shard_map/ppermute | solution.py:42
  81.2 14.7 %all_to_all.25.parts = bf16[4,64,512]{2,1,0:T(8,128)(2,1)S(1)} all-to-all(bf16[4,64,512]{2,1,0:T(8,128)(2,1)S(1)} %x_sum.1), channel_id=1, replica_groups={{0,4,8,12},{1,5,9,13},{2,6,10,14},{3,7,11,15},{16,20,24,28},{17,21,25,2..., dimensions={0} | all-to-all | bytes 524288 | tf_op jit(solution)/shard_map/all_to_all | solution.py:46
  96.5 4.5 %collective-permute-start.6 = (bf16[1,64,512]{2,1,0:T(8,128)(2,1)S(1)}, bf16[1,64,512]{2,1,0:T(8,128)(2,1)S(1)}, u32[]{:S(2)}, u32[]{:S(2)}) collective-permute-start(bf16[1,64,512]{2,1,0:T(8,128)(2,1)S(1)} %z_sum.1.mine), channel_id=1, source_target_pairs={{0,16},{1,17},{2,18},{3,19},{4,20},{5,21},{6,22},{7,23},{8,24},{9,... | collective-permute-start | bytes 196616 | tf_op jit(solution)/shard_map/ppermute | solution.py:42
  101.0 3.0 %collective-permute-start.4 = (bf16[256,512]{1,0:T(8,128)(2,1)S(1)}, bf16[256,512]{1,0:T(8,128)(2,1)S(1)}, u32[]{:S(2)}, u32[]{:S(2)}) collective-permute-start(bf16[256,512]{1,0:T(8,128)(2,1)S(1)} %copy-done.7), channel_id=1, source_target_pairs={{0,8},{1,9},{2,10},{3,11},{4,12},{5,13},{6,14},{7,15},{8,0},{9,1},... | collective-permute-start | bytes 786440 | tf_op jit(solution)/shard_map/ppermute | solution.py:42
  104.0 2.9 %collective-permute-done.6.got = bf16[1,64,512]{2,1,0:T(8,128)(2,1)S(1)} collective-permute-done((bf16[1,64,512]{2,1,0:T(8,128)(2,1)S(1)}, bf16[1,64,512]{2,1,0:T(8,128)(2,1)S(1)}, u32[]{:S(2)}, u32[]{:S(2)}) %collective-permute-start.6) | collective-permute-done | bytes 65568 | tf_op jit(solution)/shard_map/ppermute | solution.py:42
  108.1 3.4 %all-to-all-start.3 = ((bf16[4,64,512]{2,1,0:T(8,128)(2,1)}), bf16[4,64,512]{2,1,0:T(8,128)(2,1)S(1)}, u32[]{:S(2)}, u32[]{:S(2)}) async-start(bf16[4,64,512]{2,1,0:T(8,128)(2,1)} %last_sum.1), calls=%async_computation.3 | async-start | bytes 524288 | tf_op jit(solution)/shard_map/all_to_all | solution.py:46
  111.6 4.0 %far_weights.1 = (bf16[256,512]{1,0:T(8,128)(2,1)}, bf16[256,512]{1,0:T(8,128)(2,1)}, bf16[256,512]{1,0:T(8,128)(2,1)}, bf16[3,512,512]{2,1,0:T(8,128)(2,1)}) custom-call(s32[4]{0:T(128)} %copy-done.14, bf16[8,2,6,32,512]{4,3,2,1,0:T(8,128)(2,1)} %bitcast.20, bf16[256,512]{1,0:T(8,128)(2,1)} %cot.11), custom_call_target="tpu_custom_call" | custom-call | tf_op jit(solution)/shard_map/far_weights/pallas_call | solution.py:63
  121.0 4.8 %all-to-all-start.4 = ((bf16[8,2,3,32,512]{4,3,2,1,0:T(8,128)(2,1)}), bf16[8,2,3,32,512]{4,3,2,1,0:T(8,128)(2,1)S(1)}, u32[]{:S(2)}, u32[]{:S(2)}) async-start(bf16[8,2,3,32,512]{4,3,2,1,0:T(8,128)(2,1)} %copy-done.4), calls=%async_computation.5 | async-start | bytes 3145728 | tf_op jit(solution)/shard_map/all_to_all | solution.py:46
  125.8 6.5 %collective-permute-start.7 = (bf16[256,512]{1,0:T(8,128)(2,1)}, bf16[256,512]{1,0:T(8,128)(2,1)}, u32[]{:S(2)}, u32[]{:S(2)}) collective-permute-start(bf16[256,512]{1,0:T(8,128)(2,1)} %get-tuple-element.34), channel_id=1, source_target_pairs={{0,16},{1,17},{2,18},{3,19},{4,20},{5,21},{6,22},{7,23},{8,24},{9,... | collective-permute-start | bytes 786440 | tf_op jit(solution)/shard_map/ppermute | solution.py:42
  134.3 3.3 %collective-permute-start.9 = (bf16[256,512]{1,0:T(8,128)(2,1)}, bf16[256,512]{1,0:T(8,128)(2,1)}, u32[]{:S(2)}, u32[]{:S(2)}) collective-permute-start(bf16[256,512]{1,0:T(8,128)(2,1)} %get-tuple-element.36), channel_id=1, source_target_pairs={{0,4},{1,5},{2,6},{3,7},{4,0},{5,1},{6,2},{7,3},{8,12},{9,13},{10,... | collective-permute-start | bytes 786440 | tf_op jit(solution)/shard_map/ppermute | solution.py:42
  137.6 3.7 %near_weights.1 = (bf16[256,512]{1,0:T(8,128)(2,1)}, bf16[256,512]{1,0:T(8,128)(2,1)}, bf16[3,512,512]{2,1,0:T(8,128)(2,1)}) custom-call(s32[4]{0:T(128)} %copy-done.14, bf16[8,2,6,32,512]{4,3,2,1,0:T(8,128)(2,1)} %bitcast.21, bf16[256,512]{1,0:T(8,128)(2,1)} %cot.11), custom_call_target="tpu_custom_call" | custom-call | tf_op jit(solution)/shard_map/near_weights/pallas_call | solution.py:63
  141.3 2.7 %collective-permute-start.10 = (bf16[256,512]{1,0:T(8,128)(2,1)}, bf16[256,512]{1,0:T(8,128)(2,1)}, u32[]{:S(2)}, u32[]{:S(2)}) collective-permute-start(bf16[256,512]{1,0:T(8,128)(2,1)} %get-tuple-element.37), channel_id=1, source_target_pairs={{0,2},{1,3},{2,0},{3,1},{4,6},{5,7},{6,4},{7,5},{8,10},{9,11},{10,... | collective-permute-start | bytes 786440 | tf_op jit(solution)/shard_map/ppermute | solution.py:42
  144.0 3.1 %collective-permute-start.11 = (bf16[256,512]{1,0:T(8,128)(2,1)}, bf16[256,512]{1,0:T(8,128)(2,1)}, u32[]{:S(2)}, u32[]{:S(2)}) collective-permute-start(bf16[256,512]{1,0:T(8,128)(2,1)} %get-tuple-element.38), channel_id=1, source_target_pairs={{0,1},{1,0},{2,3},{3,2},{4,5},{5,4},{6,7},{7,6},{8,9},{9,8},{10,11... | collective-permute-start | bytes 786440 | tf_op jit(solution)/shard_map/ppermute | solution.py:42
  149.1 3.7 %collective-permute-done.7.z4 = bf16[256,512]{1,0:T(8,128)(2,1)} collective-permute-done((bf16[256,512]{1,0:T(8,128)(2,1)}, bf16[256,512]{1,0:T(8,128)(2,1)}, u32[]{:S(2)}, u32[]{:S(2)}) %collective-permute-start.7) | collective-permute-done | bytes 262176 | tf_op jit(solution)/shard_map/ppermute | solution.py:42
  152.8 14.4 %collective-permute-start.12 = (bf16[7,32,512]{2,1,0:T(8,128)(2,1)S(1)}, bf16[7,32,512]{2,1,0:T(8,128)(2,1)S(1)}, u32[]{:S(2)}, u32[]{:S(2)}) collective-permute-start(bf16[7,32,512]{2,1,0:T(8,128)(2,1)S(1)} %get-tuple-element.40), channel_id=1, source_target_pairs={{0,64},{32,96},{64,0},{96,32},{128,192},{160,224},{192,128},{224,1... | collective-permute-start | bytes 688136 | tf_op jit(solution)/shard_map/ppermute | solution.py:38
  174.5 19.3 %collective-permute-done.12 = bf16[7,32,512]{2,1,0:T(8,128)(2,1)S(1)} collective-permute-done((bf16[7,32,512]{2,1,0:T(8,128)(2,1)S(1)}, bf16[7,32,512]{2,1,0:T(8,128)(2,1)S(1)}, u32[]{:S(2)}, u32[]{:S(2)}) %collective-permute-start.12) | collective-permute-done | bytes 229408 | tf_op jit(solution)/shard_map/ppermute | solution.py:38
  (69 shorter events, 31.8 us)
Async XLA Ops:
  7.2 104.4 %all-gather.3.cloned.1.call-start = ((), (), s32[]{:S(2)}) async-start(), calls=%async_computation.7 | async-start | bytes 3538944 | tf_op jit(solution)/shard_map/all_gather | solution.py:204
  7.2 25.2 %collective-permute-start.2 = (bf16[256,512]{1,0:T(8,128)(2,1)}, bf16[256,512]{1,0:T(8,128)(2,1)S(1)}, u32[]{:S(2)}, u32[]{:S(2)}) collective-permute-start(bf16[256,512]{1,0:T(8,128)(2,1)} %inputs.7), channel_id=1, source_target_pairs={{0,4},{1,5},{2,6},{3,7},{4,0},{5,1},{6,2},{7,3},{8,12},{9,13},{10,... | collective-permute-start | bytes 786440 | tf_op jit(solution)/shard_map/ppermute | solution.py:42
  9.2 23.2 %collective-permute-start.1 = (bf16[256,512]{1,0:T(8,128)(2,1)}, bf16[256,512]{1,0:T(8,128)(2,1)S(1)}, u32[]{:S(2)}, u32[]{:S(2)}) collective-permute-start(bf16[256,512]{1,0:T(8,128)(2,1)} %inputs.7), channel_id=1, source_target_pairs={{0,2},{1,3},{2,0},{3,1},{4,6},{5,7},{6,4},{7,5},{8,10},{9,11},{10,... | collective-permute-start | bytes 786440 | tf_op jit(solution)/shard_map/ppermute | solution.py:42
  14.2 18.3 %collective-permute-start = (bf16[256,512]{1,0:T(8,128)(2,1)}, bf16[256,512]{1,0:T(8,128)(2,1)S(1)}, u32[]{:S(2)}, u32[]{:S(2)}) collective-permute-start(bf16[256,512]{1,0:T(8,128)(2,1)} %inputs.7), channel_id=1, source_target_pairs={{0,1},{1,0},{2,3},{3,2},{4,5},{5,4},{6,7},{7,6},{8,9},{9,8},{10,11... | collective-permute-start | bytes 786440 | tf_op jit(solution)/shard_map/ppermute | solution.py:42
  18.4 26.8 %collective-permute-start.3 = (bf16[7,32,512]{2,1,0:T(8,128)(2,1)S(1)}, bf16[7,32,512]{2,1,0:T(8,128)(2,1)S(1)}, u32[]{:S(2)}, u32[]{:S(2)}) collective-permute-start(bf16[7,32,512]{2,1,0:T(8,128)(2,1)S(1)} %pad_maximum_fusion.mine), channel_id=1, source_target_pairs={{0,64},{32,96},{64,0},{96,32},{128,192},{160,224},{192,128},{224,1... | collective-permute-start | bytes 688136 | tf_op jit(solution)/shard_map/ppermute | solution.py:38
  32.4 74.4 %copy-start.14 = (s32[4]{0:T(128)}, s32[4]{0:T(128)S(1)}, u32[]{:S(2)}) copy-start(s32[4]{0:T(128)S(1)} %pad_add_fusion.place) | copy-start | bytes 52
  37.6 23.0 %copy-start.1 = (bf16[256,512]{1,0:T(8,128)(2,1)S(1)}, bf16[256,512]{1,0:T(8,128)(2,1)}, u32[]{:S(2)}) copy-start(bf16[256,512]{1,0:T(8,128)(2,1)} %cot.11) | copy-start | bytes 786436
  46.7 13.8 %all-to-all-start = ((bf16[8,2,32,512]{3,2,1,0:T(8,128)(2,1)}), bf16[8,2,32,512]{3,2,1,0:T(8,128)(2,1)S(1)}, u32[]{:S(2)}, u32[]{:S(2)}) async-start(bf16[8,2,32,512]{3,2,1,0:T(8,128)(2,1)} %get-tuple-element.27), calls=%async_computation | async-start | bytes 1048576 | tf_op jit(solution)/shard_map/all_to_all | solution.py:46
  51.6 29.0 %collective-permute-start.5 = (bf16[256,512]{1,0:T(8,128)(2,1)S(1)}, bf16[256,512]{1,0:T(8,128)(2,1)S(1)}, u32[]{:S(2)}, u32[]{:S(2)}) collective-permute-start(bf16[256,512]{1,0:T(8,128)(2,1)S(1)} %copy-done.7), channel_id=1, source_target_pairs={{0,16},{1,17},{2,18},{3,19},{4,20},{5,21},{6,22},{7,23},{8,24},{9,... | collective-permute-start | bytes 786440 | tf_op jit(solution)/shard_map/ppermute | solution.py:42
  62.1 18.5 %all-to-all-start.1 = ((bf16[4,64,512]{2,1,0:T(8,128)(2,1)}), bf16[4,64,512]{2,1,0:T(8,128)(2,1)S(1)}, u32[]{:S(2)}, u32[]{:S(2)}) async-start(bf16[4,64,512]{2,1,0:T(8,128)(2,1)} %project.1), calls=%async_computation.1 | async-start | bytes 524288 | tf_op jit(solution)/shard_map/all_to_all | solution.py:46
  65.5 81.6 %reduce-scatter.2.cloned.1.call-start = ((), (), s32[]{:S(2)}) async-start(), calls=%async_computation.6 | async-start | bytes 2359296 | tf_op jit(solution)/shard_map/reduce_scatter | solution.py:221
  80.6 37.6 %copy-start.9 = (bf16[256,512]{1,0:T(8,128)(2,1)}, bf16[256,512]{1,0:T(8,128)(2,1)S(1)}, u32[]{:S(2)}) copy-start(bf16[256,512]{1,0:T(8,128)(2,1)S(1)} %collective-permute-done.5.n4) | copy-start | bytes 786436
  96.5 10.4 %collective-permute-start.6 = (bf16[1,64,512]{2,1,0:T(8,128)(2,1)S(1)}, bf16[1,64,512]{2,1,0:T(8,128)(2,1)S(1)}, u32[]{:S(2)}, u32[]{:S(2)}) collective-permute-start(bf16[1,64,512]{2,1,0:T(8,128)(2,1)S(1)} %z_sum.1.mine), channel_id=1, source_target_pairs={{0,16},{1,17},{2,18},{3,19},{4,20},{5,21},{6,22},{7,23},{8,24},{9,... | collective-permute-start | bytes 196616 | tf_op jit(solution)/shard_map/ppermute | solution.py:42
  101.0 17.2 %collective-permute-start.4 = (bf16[256,512]{1,0:T(8,128)(2,1)S(1)}, bf16[256,512]{1,0:T(8,128)(2,1)S(1)}, u32[]{:S(2)}, u32[]{:S(2)}) collective-permute-start(bf16[256,512]{1,0:T(8,128)(2,1)S(1)} %copy-done.7), channel_id=1, source_target_pairs={{0,8},{1,9},{2,10},{3,11},{4,12},{5,13},{6,14},{7,15},{8,0},{9,1},... | collective-permute-start | bytes 786440 | tf_op jit(solution)/shard_map/ppermute | solution.py:42
  108.1 10.1 %all-to-all-start.3 = ((bf16[4,64,512]{2,1,0:T(8,128)(2,1)}), bf16[4,64,512]{2,1,0:T(8,128)(2,1)S(1)}, u32[]{:S(2)}, u32[]{:S(2)}) async-start(bf16[4,64,512]{2,1,0:T(8,128)(2,1)} %last_sum.1), calls=%async_computation.3 | async-start | bytes 524288 | tf_op jit(solution)/shard_map/all_to_all | solution.py:46
  121.0 26.2 %all-to-all-start.4 = ((bf16[8,2,3,32,512]{4,3,2,1,0:T(8,128)(2,1)}), bf16[8,2,3,32,512]{4,3,2,1,0:T(8,128)(2,1)S(1)}, u32[]{:S(2)}, u32[]{:S(2)}) async-start(bf16[8,2,3,32,512]{4,3,2,1,0:T(8,128)(2,1)} %copy-done.4), calls=%async_computation.5 | async-start | bytes 3145728 | tf_op jit(solution)/shard_map/all_to_all | solution.py:46
  125.8 27.0 %collective-permute-start.7 = (bf16[256,512]{1,0:T(8,128)(2,1)}, bf16[256,512]{1,0:T(8,128)(2,1)}, u32[]{:S(2)}, u32[]{:S(2)}) collective-permute-start(bf16[256,512]{1,0:T(8,128)(2,1)} %get-tuple-element.34), channel_id=1, source_target_pairs={{0,16},{1,17},{2,18},{3,19},{4,20},{5,21},{6,22},{7,23},{8,24},{9,... | collective-permute-start | bytes 786440 | tf_op jit(solution)/shard_map/ppermute | solution.py:42
  132.3 39.6 %collective-permute-start.8 = (bf16[256,512]{1,0:T(8,128)(2,1)}, bf16[256,512]{1,0:T(8,128)(2,1)}, u32[]{:S(2)}, u32[]{:S(2)}) collective-permute-start(bf16[256,512]{1,0:T(8,128)(2,1)} %get-tuple-element.35), channel_id=1, source_target_pairs={{0,8},{1,9},{2,10},{3,11},{4,12},{5,13},{6,14},{7,15},{8,0},{9,1},... | collective-permute-start | bytes 786440 | tf_op jit(solution)/shard_map/ppermute | solution.py:42
  134.3 37.7 %collective-permute-start.9 = (bf16[256,512]{1,0:T(8,128)(2,1)}, bf16[256,512]{1,0:T(8,128)(2,1)}, u32[]{:S(2)}, u32[]{:S(2)}) collective-permute-start(bf16[256,512]{1,0:T(8,128)(2,1)} %get-tuple-element.36), channel_id=1, source_target_pairs={{0,4},{1,5},{2,6},{3,7},{4,0},{5,1},{6,2},{7,3},{8,12},{9,13},{10,... | collective-permute-start | bytes 786440 | tf_op jit(solution)/shard_map/ppermute | solution.py:42
  141.3 30.7 %collective-permute-start.10 = (bf16[256,512]{1,0:T(8,128)(2,1)}, bf16[256,512]{1,0:T(8,128)(2,1)}, u32[]{:S(2)}, u32[]{:S(2)}) collective-permute-start(bf16[256,512]{1,0:T(8,128)(2,1)} %get-tuple-element.37), channel_id=1, source_target_pairs={{0,2},{1,3},{2,0},{3,1},{4,6},{5,7},{6,4},{7,5},{8,10},{9,11},{10,... | collective-permute-start | bytes 786440 | tf_op jit(solution)/shard_map/ppermute | solution.py:42
  144.0 27.9 %collective-permute-start.11 = (bf16[256,512]{1,0:T(8,128)(2,1)}, bf16[256,512]{1,0:T(8,128)(2,1)}, u32[]{:S(2)}, u32[]{:S(2)}) collective-permute-start(bf16[256,512]{1,0:T(8,128)(2,1)} %get-tuple-element.38), channel_id=1, source_target_pairs={{0,1},{1,0},{2,3},{3,2},{4,5},{5,4},{6,7},{7,6},{8,9},{9,8},{10,11... | collective-permute-start | bytes 786440 | tf_op jit(solution)/shard_map/ppermute | solution.py:42
  147.2 20.0 %copy-start.5 = (bf16[3,512,512]{2,1,0:T(8,128)(2,1)S(1)}, bf16[3,512,512]{2,1,0:T(8,128)(2,1)}, u32[]{:S(2)}) copy-start(bf16[3,512,512]{2,1,0:T(8,128)(2,1)} %get-tuple-element.33.near_w.w) | copy-start | bytes 4718596
  147.2 20.0 %copy-start.10 = (bf16[256,512]{1,0:T(8,128)(2,1)S(1)}, bf16[256,512]{1,0:T(8,128)(2,1)}, u32[]{:S(2)}) copy-start(bf16[256,512]{1,0:T(8,128)(2,1)} %copy-done.9) | copy-start | bytes 786436
  152.8 41.0 %collective-permute-start.12 = (bf16[7,32,512]{2,1,0:T(8,128)(2,1)S(1)}, bf16[7,32,512]{2,1,0:T(8,128)(2,1)S(1)}, u32[]{:S(2)}, u32[]{:S(2)}) collective-permute-start(bf16[7,32,512]{2,1,0:T(8,128)(2,1)S(1)} %get-tuple-element.40), channel_id=1, source_target_pairs={{0,64},{32,96},{64,0},{96,32},{128,192},{160,224},{192,128},{224,1... | collective-permute-start | bytes 688136 | tf_op jit(solution)/shard_map/ppermute | solution.py:38
  (12 other events, 52.0 us)
Sparse Core Ops, SparseCore 0:
  46.8 42.1 all-gather.2
  91.9 41.9 reduce-scatter.1

commit v5 on v4

--- a/solution.py
+++ b/solution.py
@@ -58,13 +58,17 @@
     return lax.dot_general(a, b, (((0,), (0,)), ((), ())), preferred_element_type=F32)
 
 
-def call(kernel, out, place, *args, scratch=(), name, limit=24):
+def call(kernel, out, place, *args, scratch=(), name, limit=24, part=None):
     shapes = [jax.ShapeDtypeStruct(s, d) for s, d in out]
+    specs = [pl.BlockSpec(memory_space=pltpu.VMEM)] * len(args)
+    if part is not None:
+        specs[0] = pl.BlockSpec((8, 2, 3, 32, BS), lambda _: (0, 0, part, 0, 0))
     return pl.pallas_call(
         kernel,
         out_shape=shapes,
         in_specs=[pl.BlockSpec(memory_space=pltpu.SMEM)]
-        + [pl.BlockSpec(memory_space=pltpu.VMEM)] * len(args),
+        + specs,
+        grid=() if part is None else (1,),
         out_specs=[pl.BlockSpec(memory_space=pltpu.VMEM)] * len(out),
         scratch_shapes=list(scratch),
         compiler_params=pltpu.CompilerParams(vmem_limit_bytes=limit << 20),
@@ -103,7 +107,7 @@
     for k in range(8):
         for g in range(2):
             rows = pl.ds(rows_of(place, k // 2, g, k % 2), 32)
-            w[:, rows, :] = gathered[k, g, 3:]
+            w[:, rows, :] = gathered[k, g]
     for level, z in enumerate((z2, z3, z4)):
         z[...] = dot_nt(cot[...], w[level]).astype(BF16)
 
@@ -112,7 +116,7 @@
     for k in range(8):
         for g in range(2):
             rows = pl.ds(rows_of(place, k // 2, g, k % 2), 32)
-            w[:, rows, :] = gathered[k, g, :3]
+            w[:, rows, :] = gathered[k, g]
     for level, z in enumerate((z0, z1)):
         z[...] = dot_nt(cot[...], w[level + 1]).astype(BF16)
 
@@ -226,7 +230,7 @@
     gathered = tie(gathered, parts)
     *far_z, far_w = call(
         far_weights_kernel, [(block, BF16)] * 3 + [((3, BS, BS), BF16)],
-        place, gathered, cotangent, name="far_weights", limit=60,
+        place, gathered, cotangent, name="far_weights", limit=60, part=1,
     )
     far_z = [over_feat(far_z[4 - l], PARTNER[l]) for l in (4, 3, 2)][::-1]
     st = tie(st, far_w)
@@ -237,7 +241,7 @@
     )
     *near_z, near_w = call(
         near_weights_kernel, [(block, BF16)] * 2 + [((3, BS, BS), BF16)],
-        place, tie(gathered, parts), cotangent, name="near_weights", limit=60,
+        place, tie(gathered, parts), cotangent, name="near_weights", limit=60, part=0,
     )
     z = [over_feat(near_z[1 - l], PARTNER[l]) for l in (1, 0)][::-1] + far_z
     (output,) = call(

time: 203 us -> 203 us (level)
  transfers between devices with their start and end apart: 19 -> 19, of which waited for: 8 -> 8; matrix products, arithmetic and copies ran while one was open for 1% -> 1% of each run, Pallas kernels for 11% -> 10%
where the time goes in v5:
time: 203 us; the launch traced here: 202 us
  starting transfers between devices  85.7 us (42%)
  waiting for transfers between devices  54.9 us (27%)
  Pallas kernels  22.6 us (11%)
  blocking collectives  14.7 us (7%)
  between operations  14.4 us (7%)
  local copies, waits for them, and re-layouts  8.02 us (4%)
    ppermute x11, starting transfers between devices, over_feat(): return lax.ppermute(value, 'feat', pairs)  40.7 us
    ppermute x2, starting transfers between devices, over_dp(): return lax.ppermute(value, 'dp', pairs)  28.4 us
    ppermute x2, waiting for transfers between devices, over_dp(): return lax.ppermute(value, 'dp', pairs)  26.9 us
    pallas_call x12, Pallas kernels, call(): pl.pallas_call(kernel, out_shape=shapes, in_specs=[pl.BlockSpec(memory_sp...  22.6 us
    ppermute x11, waiting for transfers between devices, over_feat(): return lax.ppermute(value, 'feat', pairs)  21.6 us
    all_to_all x4, starting transfers between devices, exchange(): lax.all_to_all(value, axis, 0, 0, tiled=True, axis_index_groups=groups)  16.5 us
    all_to_all x1, blocking collectives, exchange(): lax.all_to_all(value, axis, 0, 0, tiled=True, axis_index_groups=groups)  14.7 us
    unnamed x34, local copies, waits for them, and re-layouts  6.6 us
  transfers between devices with their start and end apart: 19, of which 8 were waited for; matrix products, arithmetic and copies ran while one was open for 1% of the time, Pallas kernels for 10%

profile of v5, /device:TPU:104, one launch (start us, length us, event | category | flops | bytes accessed | tf_op | source)
XLA Modules:
  0.0 202.1 jit_solution(13404225695115832997)
XLA Ops:
  9.2 4.9 %collective-permute-start.1 = (bf16[256,512]{1,0:T(8,128)(2,1)}, bf16[256,512]{1,0:T(8,128)(2,1)S(1)}, u32[]{:S(2)}, u32[]{:S(2)}) collective-permute-start(bf16[256,512]{1,0:T(8,128)(2,1)} %inputs.7), channel_id=1, source_target_pairs={{0,2},{1,3},{2,0},{3,1},{4,6},{5,7},{6,4},{7,5},{8,10},{9,11},{10,... | collective-permute-start | bytes 786440 | tf_op jit(solution)/shard_map/ppermute | solution.py:42
  18.4 13.9 %collective-permute-start.3 = (bf16[7,32,512]{2,1,0:T(8,128)(2,1)S(1)}, bf16[7,32,512]{2,1,0:T(8,128)(2,1)S(1)}, u32[]{:S(2)}, u32[]{:S(2)}) collective-permute-start(bf16[7,32,512]{2,1,0:T(8,128)(2,1)S(1)} %pad_maximum_fusion.mine), channel_id=1, source_target_pairs={{0,64},{32,96},{64,0},{96,32},{128,192},{160,224},{192,128},{224,1... | collective-permute-start | bytes 688136 | tf_op jit(solution)/shard_map/ppermute | solution.py:38
  34.4 3.2 %near_grads.1 = bf16[8,2,4,32,512]{4,3,2,1,0:T(8,128)(2,1)} custom-call(s32[4]{0:T(128)S(1)} %pad_add_fusion.place, bf16[256,512]{1,0:T(8,128)(2,1)S(1)} %copy-done.6, bf16[256,512]{1,0:T(8,128)(2,1)S(1)} %collective-permute-done.n0, bf16[256,512]{1,0:T(8,128)(2,1)S(1)} %collective-permute-done.1.n1, bf16[256,512]{1,0:T(8,128)(2,1)S(1)} %collective-permute-done.2.n2, ...), custom_call_target="tpu_custom_call" | custom-call | tf_op jit(solution)/shard_map/near_grads/pallas_call | solution.py:66
  37.6 7.6 %collective-permute-done.3.got = bf16[7,32,512]{2,1,0:T(8,128)(2,1)S(1)} collective-permute-done((bf16[7,32,512]{2,1,0:T(8,128)(2,1)S(1)}, bf16[7,32,512]{2,1,0:T(8,128)(2,1)S(1)}, u32[]{:S(2)}, u32[]{:S(2)}) %collective-permute-start.3) | collective-permute-done | bytes 229408 | tf_op jit(solution)/shard_map/ppermute | solution.py:38
  46.7 4.9 %all-to-all-start = ((bf16[8,2,32,512]{3,2,1,0:T(8,128)(2,1)}), bf16[8,2,32,512]{3,2,1,0:T(8,128)(2,1)S(1)}, u32[]{:S(2)}, u32[]{:S(2)}) async-start(bf16[8,2,32,512]{3,2,1,0:T(8,128)(2,1)} %get-tuple-element.27), calls=%async_computation | async-start | bytes 1048576 | tf_op jit(solution)/shard_map/all_to_all | solution.py:46
  51.6 6.2 %collective-permute-start.5 = (bf16[256,512]{1,0:T(8,128)(2,1)S(1)}, bf16[256,512]{1,0:T(8,128)(2,1)S(1)}, u32[]{:S(2)}, u32[]{:S(2)}) collective-permute-start(bf16[256,512]{1,0:T(8,128)(2,1)S(1)} %copy-done.7), channel_id=1, source_target_pairs={{0,16},{1,17},{2,18},{3,19},{4,20},{5,21},{6,22},{7,23},{8,24},{9,... | collective-permute-start | bytes 786440 | tf_op jit(solution)/shard_map/ppermute | solution.py:42
  57.9 2.6 %all-to-all-done.gathered = bf16[8,2,32,512]{3,2,1,0:T(8,128)(2,1)S(1)} async-done(((bf16[8,2,32,512]{3,2,1,0:T(8,128)(2,1)}), bf16[8,2,32,512]{3,2,1,0:T(8,128)(2,1)S(1)}, u32[]{:S(2)}, u32[]{:S(2)}) %all-to-all-start) | async-done | bytes 524320 | tf_op jit(solution)/shard_map/all_to_all | solution.py:46
  62.1 3.4 %all-to-all-start.1 = ((bf16[4,64,512]{2,1,0:T(8,128)(2,1)}), bf16[4,64,512]{2,1,0:T(8,128)(2,1)S(1)}, u32[]{:S(2)}, u32[]{:S(2)}) async-start(bf16[4,64,512]{2,1,0:T(8,128)(2,1)} %project.1), calls=%async_computation.1 | async-start | bytes 524288 | tf_op jit(solution)/shard_map/all_to_all | solution.py:46
  65.6 15.0 %collective-permute-done.5.n4 = bf16[256,512]{1,0:T(8,128)(2,1)S(1)} collective-permute-done((bf16[256,512]{1,0:T(8,128)(2,1)S(1)}, bf16[256,512]{1,0:T(8,128)(2,1)S(1)}, u32[]{:S(2)}, u32[]{:S(2)}) %collective-permute-start.5) | collective-permute-done | bytes 262176 | tf_op jit(solution)/shard_map/ppermute | solution.py:42
  81.2 14.7 %all_to_all.25.parts = bf16[4,64,512]{2,1,0:T(8,128)(2,1)S(1)} all-to-all(bf16[4,64,512]{2,1,0:T(8,128)(2,1)S(1)} %x_sum.1), channel_id=1, replica_groups={{0,4,8,12},{1,5,9,13},{2,6,10,14},{3,7,11,15},{16,20,24,28},{17,21,25,2..., dimensions={0} | all-to-all | bytes 524288 | tf_op jit(solution)/shard_map/all_to_all | solution.py:46
  96.5 4.5 %collective-permute-start.6 = (bf16[1,64,512]{2,1,0:T(8,128)(2,1)S(1)}, bf16[1,64,512]{2,1,0:T(8,128)(2,1)S(1)}, u32[]{:S(2)}, u32[]{:S(2)}) collective-permute-start(bf16[1,64,512]{2,1,0:T(8,128)(2,1)S(1)} %z_sum.1.mine), channel_id=1, source_target_pairs={{0,16},{1,17},{2,18},{3,19},{4,20},{5,21},{6,22},{7,23},{8,24},{9,... | collective-permute-start | bytes 196616 | tf_op jit(solution)/shard_map/ppermute | solution.py:42
  101.0 3.0 %collective-permute-start.4 = (bf16[256,512]{1,0:T(8,128)(2,1)S(1)}, bf16[256,512]{1,0:T(8,128)(2,1)S(1)}, u32[]{:S(2)}, u32[]{:S(2)}) collective-permute-start(bf16[256,512]{1,0:T(8,128)(2,1)S(1)} %copy-done.7), channel_id=1, source_target_pairs={{0,8},{1,9},{2,10},{3,11},{4,12},{5,13},{6,14},{7,15},{8,0},{9,1},... | collective-permute-start | bytes 786440 | tf_op jit(solution)/shard_map/ppermute | solution.py:42
  104.0 2.9 %collective-permute-done.6.got = bf16[1,64,512]{2,1,0:T(8,128)(2,1)S(1)} collective-permute-done((bf16[1,64,512]{2,1,0:T(8,128)(2,1)S(1)}, bf16[1,64,512]{2,1,0:T(8,128)(2,1)S(1)}, u32[]{:S(2)}, u32[]{:S(2)}) %collective-permute-start.6) | collective-permute-done | bytes 65568 | tf_op jit(solution)/shard_map/ppermute | solution.py:42
  108.1 3.4 %all-to-all-start.3 = ((bf16[4,64,512]{2,1,0:T(8,128)(2,1)}), bf16[4,64,512]{2,1,0:T(8,128)(2,1)S(1)}, u32[]{:S(2)}, u32[]{:S(2)}) async-start(bf16[4,64,512]{2,1,0:T(8,128)(2,1)} %last_sum.1), calls=%async_computation.3 | async-start | bytes 524288 | tf_op jit(solution)/shard_map/all_to_all | solution.py:46
  111.6 3.5 %far_weights.1 = (bf16[256,512]{1,0:T(8,128)(2,1)}, bf16[256,512]{1,0:T(8,128)(2,1)}, bf16[256,512]{1,0:T(8,128)(2,1)}, bf16[3,512,512]{2,1,0:T(8,128)(2,1)}) custom-call(s32[4]{0:T(128)} %copy-done.14, bf16[8,2,6,32,512]{4,3,2,1,0:T(8,128)(2,1)} %bitcast.20, bf16[256,512]{1,0:T(8,128)(2,1)} %cot.11), custom_call_target="tpu_custom_call" | custom-call | tf_op jit(solution)/shard_map/far_weights/pallas_call | solution.py:66
  115.1 3.1 %all-to-all-done.3 = bf16[4,64,512]{2,1,0:T(8,128)(2,1)S(1)} async-done(((bf16[4,64,512]{2,1,0:T(8,128)(2,1)}), bf16[4,64,512]{2,1,0:T(8,128)(2,1)S(1)}, u32[]{:S(2)}, u32[]{:S(2)}) %all-to-all-start.3) | async-done | bytes 262176 | tf_op jit(solution)/shard_map/all_to_all | solution.py:46
  121.0 4.8 %all-to-all-start.4 = ((bf16[8,2,3,32,512]{4,3,2,1,0:T(8,128)(2,1)}), bf16[8,2,3,32,512]{4,3,2,1,0:T(8,128)(2,1)S(1)}, u32[]{:S(2)}, u32[]{:S(2)}) async-start(bf16[8,2,3,32,512]{4,3,2,1,0:T(8,128)(2,1)} %copy-done.4), calls=%async_computation.5 | async-start | bytes 3145728 | tf_op jit(solution)/shard_map/all_to_all | solution.py:46
  125.8 6.5 %collective-permute-start.7 = (bf16[256,512]{1,0:T(8,128)(2,1)}, bf16[256,512]{1,0:T(8,128)(2,1)}, u32[]{:S(2)}, u32[]{:S(2)}) collective-permute-start(bf16[256,512]{1,0:T(8,128)(2,1)} %get-tuple-element.34), channel_id=1, source_target_pairs={{0,16},{1,17},{2,18},{3,19},{4,20},{5,21},{6,22},{7,23},{8,24},{9,... | collective-permute-start | bytes 786440 | tf_op jit(solution)/shard_map/ppermute | solution.py:42
  134.3 3.3 %collective-permute-start.9 = (bf16[256,512]{1,0:T(8,128)(2,1)}, bf16[256,512]{1,0:T(8,128)(2,1)}, u32[]{:S(2)}, u32[]{:S(2)}) collective-permute-start(bf16[256,512]{1,0:T(8,128)(2,1)} %get-tuple-element.36), channel_id=1, source_target_pairs={{0,4},{1,5},{2,6},{3,7},{4,0},{5,1},{6,2},{7,3},{8,12},{9,13},{10,... | collective-permute-start | bytes 786440 | tf_op jit(solution)/shard_map/ppermute | solution.py:42
  137.6 3.2 %near_weights.1 = (bf16[256,512]{1,0:T(8,128)(2,1)}, bf16[256,512]{1,0:T(8,128)(2,1)}, bf16[3,512,512]{2,1,0:T(8,128)(2,1)}) custom-call(s32[4]{0:T(128)} %copy-done.14, bf16[8,2,6,32,512]{4,3,2,1,0:T(8,128)(2,1)} %bitcast.21, bf16[256,512]{1,0:T(8,128)(2,1)} %cot.11), custom_call_target="tpu_custom_call" | custom-call | tf_op jit(solution)/shard_map/near_weights/pallas_call | solution.py:66
  143.3 3.4 %collective-permute-start.11 = (bf16[256,512]{1,0:T(8,128)(2,1)}, bf16[256,512]{1,0:T(8,128)(2,1)}, u32[]{:S(2)}, u32[]{:S(2)}) collective-permute-start(bf16[256,512]{1,0:T(8,128)(2,1)} %get-tuple-element.38), channel_id=1, source_target_pairs={{0,1},{1,0},{2,3},{3,2},{4,5},{5,4},{6,7},{7,6},{8,9},{9,8},{10,11... | collective-permute-start | bytes 786440 | tf_op jit(solution)/shard_map/ppermute | solution.py:42
  149.1 3.7 %collective-permute-done.7.z4 = bf16[256,512]{1,0:T(8,128)(2,1)} collective-permute-done((bf16[256,512]{1,0:T(8,128)(2,1)}, bf16[256,512]{1,0:T(8,128)(2,1)}, u32[]{:S(2)}, u32[]{:S(2)}) %collective-permute-start.7) | collective-permute-done | bytes 262176 | tf_op jit(solution)/shard_map/ppermute | solution.py:42
  152.8 14.4 %collective-permute-start.12 = (bf16[7,32,512]{2,1,0:T(8,128)(2,1)S(1)}, bf16[7,32,512]{2,1,0:T(8,128)(2,1)S(1)}, u32[]{:S(2)}, u32[]{:S(2)}) collective-permute-start(bf16[7,32,512]{2,1,0:T(8,128)(2,1)S(1)} %get-tuple-element.40), channel_id=1, source_target_pairs={{0,64},{32,96},{64,0},{96,32},{128,192},{160,224},{192,128},{224,1... | collective-permute-start | bytes 688136 | tf_op jit(solution)/shard_map/ppermute | solution.py:38
  174.5 19.3 %collective-permute-done.12 = bf16[7,32,512]{2,1,0:T(8,128)(2,1)S(1)} collective-permute-done((bf16[7,32,512]{2,1,0:T(8,128)(2,1)S(1)}, bf16[7,32,512]{2,1,0:T(8,128)(2,1)S(1)}, u32[]{:S(2)}, u32[]{:S(2)}) %collective-permute-start.12) | collective-permute-done | bytes 229408 | tf_op jit(solution)/shard_map/ppermute | solution.py:38
  (69 shorter events, 32.1 us)
Async XLA Ops:
  7.2 104.4 %all-gather.3.cloned.1.call-start = ((), (), s32[]{:S(2)}) async-start(), calls=%async_computation.7 | async-start | bytes 3538944 | tf_op jit(solution)/shard_map/all_gather | solution.py:208
  7.2 25.2 %collective-permute-start.2 = (bf16[256,512]{1,0:T(8,128)(2,1)}, bf16[256,512]{1,0:T(8,128)(2,1)S(1)}, u32[]{:S(2)}, u32[]{:S(2)}) collective-permute-start(bf16[256,512]{1,0:T(8,128)(2,1)} %inputs.7), channel_id=1, source_target_pairs={{0,4},{1,5},{2,6},{3,7},{4,0},{5,1},{6,2},{7,3},{8,12},{9,13},{10,... | collective-permute-start | bytes 786440 | tf_op jit(solution)/shard_map/ppermute | solution.py:42
  9.2 23.2 %collective-permute-start.1 = (bf16[256,512]{1,0:T(8,128)(2,1)}, bf16[256,512]{1,0:T(8,128)(2,1)S(1)}, u32[]{:S(2)}, u32[]{:S(2)}) collective-permute-start(bf16[256,512]{1,0:T(8,128)(2,1)} %inputs.7), channel_id=1, source_target_pairs={{0,2},{1,3},{2,0},{3,1},{4,6},{5,7},{6,4},{7,5},{8,10},{9,11},{10,... | collective-permute-start | bytes 786440 | tf_op jit(solution)/shard_map/ppermute | solution.py:42
  14.2 18.3 %collective-permute-start = (bf16[256,512]{1,0:T(8,128)(2,1)}, bf16[256,512]{1,0:T(8,128)(2,1)S(1)}, u32[]{:S(2)}, u32[]{:S(2)}) collective-permute-start(bf16[256,512]{1,0:T(8,128)(2,1)} %inputs.7), channel_id=1, source_target_pairs={{0,1},{1,0},{2,3},{3,2},{4,5},{5,4},{6,7},{7,6},{8,9},{9,8},{10,11... | collective-permute-start | bytes 786440 | tf_op jit(solution)/shard_map/ppermute | solution.py:42
  18.4 26.8 %collective-permute-start.3 = (bf16[7,32,512]{2,1,0:T(8,128)(2,1)S(1)}, bf16[7,32,512]{2,1,0:T(8,128)(2,1)S(1)}, u32[]{:S(2)}, u32[]{:S(2)}) collective-permute-start(bf16[7,32,512]{2,1,0:T(8,128)(2,1)S(1)} %pad_maximum_fusion.mine), channel_id=1, source_target_pairs={{0,64},{32,96},{64,0},{96,32},{128,192},{160,224},{192,128},{224,1... | collective-permute-start | bytes 688136 | tf_op jit(solution)/shard_map/ppermute | solution.py:38
  32.4 74.4 %copy-start.14 = (s32[4]{0:T(128)}, s32[4]{0:T(128)S(1)}, u32[]{:S(2)}) copy-start(s32[4]{0:T(128)S(1)} %pad_add_fusion.place) | copy-start | bytes 52
  37.6 23.0 %copy-start.1 = (bf16[256,512]{1,0:T(8,128)(2,1)S(1)}, bf16[256,512]{1,0:T(8,128)(2,1)}, u32[]{:S(2)}) copy-start(bf16[256,512]{1,0:T(8,128)(2,1)} %cot.11) | copy-start | bytes 786436
  46.7 13.8 %all-to-all-start = ((bf16[8,2,32,512]{3,2,1,0:T(8,128)(2,1)}), bf16[8,2,32,512]{3,2,1,0:T(8,128)(2,1)S(1)}, u32[]{:S(2)}, u32[]{:S(2)}) async-start(bf16[8,2,32,512]{3,2,1,0:T(8,128)(2,1)} %get-tuple-element.27), calls=%async_computation | async-start | bytes 1048576 | tf_op jit(solution)/shard_map/all_to_all | solution.py:46
  51.6 29.0 %collective-permute-start.5 = (bf16[256,512]{1,0:T(8,128)(2,1)S(1)}, bf16[256,512]{1,0:T(8,128)(2,1)S(1)}, u32[]{:S(2)}, u32[]{:S(2)}) collective-permute-start(bf16[256,512]{1,0:T(8,128)(2,1)S(1)} %copy-done.7), channel_id=1, source_target_pairs={{0,16},{1,17},{2,18},{3,19},{4,20},{5,21},{6,22},{7,23},{8,24},{9,... | collective-permute-start | bytes 786440 | tf_op jit(solution)/shard_map/ppermute | solution.py:42
  62.1 18.5 %all-to-all-start.1 = ((bf16[4,64,512]{2,1,0:T(8,128)(2,1)}), bf16[4,64,512]{2,1,0:T(8,128)(2,1)S(1)}, u32[]{:S(2)}, u32[]{:S(2)}) async-start(bf16[4,64,512]{2,1,0:T(8,128)(2,1)} %project.1), calls=%async_computation.1 | async-start | bytes 524288 | tf_op jit(solution)/shard_map/all_to_all | solution.py:46
  65.5 81.1 %reduce-scatter.2.cloned.1.call-start = ((), (), s32[]{:S(2)}) async-start(), calls=%async_computation.6 | async-start | bytes 2359296 | tf_op jit(solution)/shard_map/reduce_scatter | solution.py:225
  80.6 37.6 %copy-start.9 = (bf16[256,512]{1,0:T(8,128)(2,1)}, bf16[256,512]{1,0:T(8,128)(2,1)S(1)}, u32[]{:S(2)}) copy-start(bf16[256,512]{1,0:T(8,128)(2,1)S(1)} %collective-permute-done.5.n4) | copy-start | bytes 786436
  96.5 10.4 %collective-permute-start.6 = (bf16[1,64,512]{2,1,0:T(8,128)(2,1)S(1)}, bf16[1,64,512]{2,1,0:T(8,128)(2,1)S(1)}, u32[]{:S(2)}, u32[]{:S(2)}) collective-permute-start(bf16[1,64,512]{2,1,0:T(8,128)(2,1)S(1)} %z_sum.1.mine), channel_id=1, source_target_pairs={{0,16},{1,17},{2,18},{3,19},{4,20},{5,21},{6,22},{7,23},{8,24},{9,... | collective-permute-start | bytes 196616 | tf_op jit(solution)/shard_map/ppermute | solution.py:42
  101.0 17.2 %collective-permute-start.4 = (bf16[256,512]{1,0:T(8,128)(2,1)S(1)}, bf16[256,512]{1,0:T(8,128)(2,1)S(1)}, u32[]{:S(2)}, u32[]{:S(2)}) collective-permute-start(bf16[256,512]{1,0:T(8,128)(2,1)S(1)} %copy-done.7), channel_id=1, source_target_pairs={{0,8},{1,9},{2,10},{3,11},{4,12},{5,13},{6,14},{7,15},{8,0},{9,1},... | collective-permute-start | bytes 786440 | tf_op jit(solution)/shard_map/ppermute | solution.py:42
  108.1 10.1 %all-to-all-start.3 = ((bf16[4,64,512]{2,1,0:T(8,128)(2,1)}), bf16[4,64,512]{2,1,0:T(8,128)(2,1)S(1)}, u32[]{:S(2)}, u32[]{:S(2)}) async-start(bf16[4,64,512]{2,1,0:T(8,128)(2,1)} %last_sum.1), calls=%async_computation.3 | async-start | bytes 524288 | tf_op jit(solution)/shard_map/all_to_all | solution.py:46
  121.0 26.2 %all-to-all-start.4 = ((bf16[8,2,3,32,512]{4,3,2,1,0:T(8,128)(2,1)}), bf16[8,2,3,32,512]{4,3,2,1,0:T(8,128)(2,1)S(1)}, u32[]{:S(2)}, u32[]{:S(2)}) async-start(bf16[8,2,3,32,512]{4,3,2,1,0:T(8,128)(2,1)} %copy-done.4), calls=%async_computation.5 | async-start | bytes 3145728 | tf_op jit(solution)/shard_map/all_to_all | solution.py:46
  125.8 27.0 %collective-permute-start.7 = (bf16[256,512]{1,0:T(8,128)(2,1)}, bf16[256,512]{1,0:T(8,128)(2,1)}, u32[]{:S(2)}, u32[]{:S(2)}) collective-permute-start(bf16[256,512]{1,0:T(8,128)(2,1)} %get-tuple-element.34), channel_id=1, source_target_pairs={{0,16},{1,17},{2,18},{3,19},{4,20},{5,21},{6,22},{7,23},{8,24},{9,... | collective-permute-start | bytes 786440 | tf_op jit(solution)/shard_map/ppermute | solution.py:42
  132.3 39.6 %collective-permute-start.8 = (bf16[256,512]{1,0:T(8,128)(2,1)}, bf16[256,512]{1,0:T(8,128)(2,1)}, u32[]{:S(2)}, u32[]{:S(2)}) collective-permute-start(bf16[256,512]{1,0:T(8,128)(2,1)} %get-tuple-element.35), channel_id=1, source_target_pairs={{0,8},{1,9},{2,10},{3,11},{4,12},{5,13},{6,14},{7,15},{8,0},{9,1},... | collective-permute-start | bytes 786440 | tf_op jit(solution)/shard_map/ppermute | solution.py:42
  134.3 37.7 %collective-permute-start.9 = (bf16[256,512]{1,0:T(8,128)(2,1)}, bf16[256,512]{1,0:T(8,128)(2,1)}, u32[]{:S(2)}, u32[]{:S(2)}) collective-permute-start(bf16[256,512]{1,0:T(8,128)(2,1)} %get-tuple-element.36), channel_id=1, source_target_pairs={{0,4},{1,5},{2,6},{3,7},{4,0},{5,1},{6,2},{7,3},{8,12},{9,13},{10,... | collective-permute-start | bytes 786440 | tf_op jit(solution)/shard_map/ppermute | solution.py:42
  140.8 31.1 %collective-permute-start.10 = (bf16[256,512]{1,0:T(8,128)(2,1)}, bf16[256,512]{1,0:T(8,128)(2,1)}, u32[]{:S(2)}, u32[]{:S(2)}) collective-permute-start(bf16[256,512]{1,0:T(8,128)(2,1)} %get-tuple-element.37), channel_id=1, source_target_pairs={{0,2},{1,3},{2,0},{3,1},{4,6},{5,7},{6,4},{7,5},{8,10},{9,11},{10,... | collective-permute-start | bytes 786440 | tf_op jit(solution)/shard_map/ppermute | solution.py:42
  143.3 28.7 %collective-permute-start.11 = (bf16[256,512]{1,0:T(8,128)(2,1)}, bf16[256,512]{1,0:T(8,128)(2,1)}, u32[]{:S(2)}, u32[]{:S(2)}) collective-permute-start(bf16[256,512]{1,0:T(8,128)(2,1)} %get-tuple-element.38), channel_id=1, source_target_pairs={{0,1},{1,0},{2,3},{3,2},{4,5},{5,4},{6,7},{7,6},{8,9},{9,8},{10,11... | collective-permute-start | bytes 786440 | tf_op jit(solution)/shard_map/ppermute | solution.py:42
  147.2 20.0 %copy-start.5 = (bf16[3,512,512]{2,1,0:T(8,128)(2,1)S(1)}, bf16[3,512,512]{2,1,0:T(8,128)(2,1)}, u32[]{:S(2)}) copy-start(bf16[3,512,512]{2,1,0:T(8,128)(2,1)} %get-tuple-element.33.near_w.w) | copy-start | bytes 4718596
  147.2 20.0 %copy-start.10 = (bf16[256,512]{1,0:T(8,128)(2,1)S(1)}, bf16[256,512]{1,0:T(8,128)(2,1)}, u32[]{:S(2)}) copy-start(bf16[256,512]{1,0:T(8,128)(2,1)} %copy-done.9) | copy-start | bytes 786436
  152.8 41.0 %collective-permute-start.12 = (bf16[7,32,512]{2,1,0:T(8,128)(2,1)S(1)}, bf16[7,32,512]{2,1,0:T(8,128)(2,1)S(1)}, u32[]{:S(2)}, u32[]{:S(2)}) collective-permute-start(bf16[7,32,512]{2,1,0:T(8,128)(2,1)S(1)} %get-tuple-element.40), channel_id=1, source_target_pairs={{0,64},{32,96},{64,0},{96,32},{128,192},{160,224},{192,128},{224,1... | collective-permute-start | bytes 688136 | tf_op jit(solution)/shard_map/ppermute | solution.py:38
  (12 other events, 52.0 us)
Sparse Core Ops, SparseCore 0:
  46.8 42.1 all-gather.2
  91.9 41.9 reduce-scatter.1
